TPU v7x, 256 devices: a whole 4x4x8 slice. The times are simulated.
256 devices in a mesh: grp: 8 (over y, core), dev: 32 (over x, z).
Axes of the slice: x: 4, y: 4, z: 8, core: 2. Of those that a mesh axis runs over, the one named last changes fastest.
Arguments:
- residual_edges: float32 [16, 1376256], P(None, ('grp', 'dev')), may hold values from -6 to 6
- pi_block: float32 [144, 192], replicated, may hold values from -0.4375 to 0.4375
- stiff_block: float32 [64, 64], replicated, may hold values from -0.05 to 5.15, as said below
- mass_block: float32 [64, 64], replicated, may hold values from -0.03 to 3.89, as said below
- permittivity: float32 [6, 16384], P(None, ('grp', 'dev')), may hold values from -1.6 to 4, as said below
- curl_coef: float32 [16384], P(('grp', 'dev')), may hold values from 0.02 to 2
- edge_map: int32 [144, 16384], P(None, ('grp', 'dev')), may hold values from 0 to 6719, as said below
- local_map: int32 [64, 16384], P(None, ('grp', 'dev')), may hold values from 0 to 2047
- node_owner: int32 [524288], P(('grp', 'dev')), may hold values from 0 to 31, as said below
- node_slot: int32 [524288], P(('grp', 'dev')), may hold values from 0 to 1727
Outputs:
- correction: float32 [16, 1376256], P(None, ('grp', 'dev'))
Inputs may be any that keep to these rules, and one draw needn't show every extreme that they name: `edge_map`: entries of one device's elements (aligned blocks of 64 columns) below 672 or at 6048 or above occur only where the neighbouring block along grp+dev order exists; both ends of the range are reached wherever that neighbour exists. `node_owner`: among the 2048 touched nodes of one device at most 128 have the same owner; in every group one owner has exactly 128 from every device of that group. `stiff_block`: Symmetric; diagonal entries between 4.15 and 5.15, the others within 0.05 of zero. `mass_block`: Symmetric; diagonal entries between 2.89 and 3.89, the others within 0.03 of zero. `permittivity`: rows 0 to 2 lie between 0.05 and 4; rows 3 to 5 within 1.6 of zero.
All inputs are finite; a program needn't handle non-finite values.
Results may differ from a plain program's by a relative error of at most 0.0003.
Values sent between devices are 32-bit elements; how exact they have to be, the bound alone decides.
No kernel may reach another device: no remote copies, remote signals or barrier semaphores. Data moves between devices by JAX's collectives and lax.ppermute only.
A program may use at most 128 MiB of HBM per device.

v0:
```python
import jax
import jax.numpy as jnp
from jax import lax
from jax.sharding import PartitionSpec as P

N_LOC = 1728


HIGH = lax.Precision.HIGHEST
CHEB_LOW = 0.3
CHEB_HIGH = 2.0


def extended_2(array, sides, width):
    for axis, dim in sides:
        size, length = (lax.axis_size(axis), array.shape[dim])
        up = [(i, (i + 1) % size) for i in range(size - 1)]
        down = [(j, i) for i, j in up]
        last = lax.slice_in_dim(array, length - width, length, axis=dim)
        leading = lax.slice_in_dim(array, 0, width, axis=dim)
        before = lax.ppermute(last, axis, up)
        after = lax.ppermute(leading, axis, down)
        array = jnp.concatenate([before, array, after], axis=dim)
    return array


def cheb_factors():
    center = 0.5 * (CHEB_HIGH + CHEB_LOW)
    half_width = 0.5 * (CHEB_HIGH - CHEB_LOW)
    sigma_ratio = center / half_width
    rho_first = 1.0 / sigma_ratio
    rho_second = 1.0 / (2.0 * sigma_ratio - rho_first)
    return (1.0 / center, 1.0 + rho_second * rho_first, 2.0 * rho_second / half_width)


def mixed_terms(stiff_part, mass_part, curl_scale, tensor):
    row_x = (
        curl_scale * stiff_part[:, 0]
        + tensor[0] * mass_part[:, 0]
        + tensor[3] * mass_part[:, 1]
        + tensor[4] * mass_part[:, 2]
    )
    row_y = (
        curl_scale * stiff_part[:, 1]
        + tensor[3] * mass_part[:, 0]
        + tensor[1] * mass_part[:, 1]
        + tensor[5] * mass_part[:, 2]
    )
    row_z = (
        curl_scale * stiff_part[:, 2]
        + tensor[4] * mass_part[:, 0]
        + tensor[5] * mass_part[:, 1]
        + tensor[2] * mass_part[:, 2]
    )
    return jnp.stack([row_x, row_y, row_z], axis=1)


def element_apply(values, stiff_block, mass_block, curl_scale, tensor):
    stiff_part = jnp.einsum("kj,rcje->rcke", stiff_block, values, precision=HIGH)
    mass_part = jnp.einsum("kj,rcje->rcke", mass_block, values, precision=HIGH)
    return mixed_terms(stiff_part, mass_part, curl_scale, tensor)


def diag_terms(stiff_block, mass_block, curl_scale, tensor):
    stiff_diag = jnp.diagonal(stiff_block)[:, None]
    mass_diag = jnp.diagonal(mass_block)[:, None]
    base = curl_scale[None, :] * stiff_diag
    return jnp.stack(
        [
            base + mass_diag * tensor[0][None, :],
            base + mass_diag * tensor[1][None, :],
            base + mass_diag * tensor[2][None, :],
        ],
        axis=0,
    )


def per_device(
    residual_edges,
    pi_block,
    stiff_block,
    mass_block,
    permittivity,
    curl_coef,
    edge_map,
    local_map,
    node_owner,
    node_slot,
):
    rhs_count, edge_count = residual_edges.shape
    elem_count = curl_coef.shape[0]
    node_count = local_map.shape[0]
    touched = node_owner.shape[0]
    peer_count = lax.axis_size("dev")
    capacity = 2 * touched // peer_count
    owned = N_LOC
    rim_depth = edge_count // 8
    value_rows = rhs_count * 3
    first, keep, step = cheb_factors()
    extended = extended_2(residual_edges, ((("grp", "dev"), 1),), edge_count)
    local_edges = edge_map - rim_depth + edge_count
    edge_values = extended[:, local_edges]
    node_terms = jnp.einsum("dp,rde->rpe", pi_block, edge_values, precision=HIGH)
    flat_ids = local_map.reshape(-1)
    diag_rows = diag_terms(stiff_block, mass_block, curl_coef, permittivity).reshape(3, -1)
    term_rows = jnp.concatenate([node_terms.reshape(value_rows, -1), diag_rows], axis=0)
    touched_sums = (
        jnp.zeros((term_rows.shape[0], touched), jnp.float32).at[:, flat_ids].add(term_rows)
    )
    sort_order = jnp.argsort(node_owner, stable=True)
    sorted_owner = node_owner[sort_order]
    counts = jnp.sum(
        (node_owner[:, None] == jnp.arange(peer_count, dtype=jnp.int32)[None, :]).astype(jnp.int32),
        axis=0,
    )
    starts = jnp.cumsum(counts) - counts
    bucket_rank = jnp.arange(touched, dtype=jnp.int32) - starts[sorted_owner]
    buffer_pos = (
        jnp.zeros((touched,), jnp.int32).at[sort_order].set(sorted_owner * capacity + bucket_rank)
    )
    sent_slots = (
        jnp.full((peer_count * capacity,), -1, jnp.int32)
        .at[buffer_pos]
        .set(node_slot)
        .reshape(1, peer_count, capacity)
    )
    got_slots = lax.all_to_all(sent_slots, "dev", split_axis=1, concat_axis=1, tiled=True).reshape(
        -1
    )
    valid = got_slots >= 0
    safe_slots = jnp.where(valid, got_slots, 0)

    def send_home(values):
        rows = values.shape[0]
        packed = jnp.zeros((rows, peer_count * capacity), jnp.float32).at[:, buffer_pos].set(values)
        arrived = lax.all_to_all(
            packed.reshape(rows, peer_count, capacity),
            "dev",
            split_axis=1,
            concat_axis=1,
            tiled=True,
        ).reshape(rows, -1)
        return (
            jnp.zeros((rows, owned), jnp.float32)
            .at[:, safe_slots]
            .add(jnp.where(valid[None, :], arrived, 0.0))
        )

    def fetch_home(values):
        rows = values.shape[0]
        wanted = jnp.where(valid[None, :], values[:, safe_slots], 0.0).reshape(
            rows, peer_count, capacity
        )
        returned = lax.all_to_all(wanted, "dev", split_axis=1, concat_axis=1, tiled=True).reshape(
            rows, -1
        )
        return returned[:, buffer_pos]

    nodal = send_home(touched_sums)
    rhs_nodes = nodal[:value_rows].reshape(rhs_count, 3, owned)
    floored = jnp.maximum(nodal[value_rows:], 1.0)
    first_iter = first * rhs_nodes / floored[None]

    def element_values(node_values):
        touched_values = fetch_home(node_values.reshape(value_rows, owned))
        return touched_values[:, local_map].reshape(rhs_count, 3, node_count, elem_count)

    applied_elems = element_apply(
        element_values(first_iter), stiff_block, mass_block, curl_coef, permittivity
    )
    applied_touched = (
        jnp.zeros((value_rows, touched), jnp.float32)
        .at[:, flat_ids]
        .add(applied_elems.reshape(value_rows, -1))
    )
    applied = send_home(applied_touched).reshape(rhs_count, 3, owned)
    second_iter = keep * first_iter + step * (rhs_nodes - applied) / floored[None]
    final_values = element_values(second_iter).reshape(rhs_count, 3 * node_count, elem_count)
    edge_terms = jnp.einsum("dp,rpe->rde", pi_block, final_values, precision=HIGH)
    collected = (
        jnp.zeros((rhs_count, edge_count + 2 * edge_count), jnp.float32)
        .at[:, local_edges]
        .add(edge_terms)
    )
    outgoing = jnp.concatenate(
        [collected[:, :edge_count], collected[:, edge_count + edge_count :]], axis=1
    )
    incoming = extended_2(outgoing, ((("grp", "dev"), 1),), edge_count)
    correction = collected[:, edge_count : edge_count + edge_count]
    correction = correction.at[:, :edge_count].add(incoming[:, :edge_count])
    correction = correction.at[:, edge_count - edge_count :].add(incoming[:, 3 * edge_count :])
    return correction


def solution(mesh):
    in_specs = (
        P(None, ("grp", "dev")),
        P(),
        P(),
        P(),
        P(None, ("grp", "dev")),
        P(("grp", "dev")),
        P(None, ("grp", "dev")),
        P(None, ("grp", "dev")),
        P(("grp", "dev")),
        P(("grp", "dev")),
    )
    out_specs = P(None, ("grp", "dev"))
    return jax.shard_map(
        per_device, mesh=mesh, in_specs=in_specs, out_specs=out_specs, check_vma=False
    )
```

profile of v0, /device:TPU:16, one launch (start us, length us, event | category | flops | bytes accessed | tf_op | source)
XLA Modules:
  0.0 535.9 jit_solution(13967832094352113781)
XLA Ops:
  0.0 3.9 collective-permute-start
  4.0 7.4 %collective-permute-start.1 = (f32[16,5376]{1,0:T(8,128)}, f32[16,5376]{1,0:T(8,128)S(1)}, u32[]{:S(2)}, u32[]{:S(2)}) collective-permute-start(f32[16,5376]{1,0:T(8,128)} %param.18), channel_id=1, source_target_pairs={{1,0},{2,1},{3,2},{4,3},{5,4},{6,5},{7,6},{8,7},{9,8},{10,9},{11,1... | collective-permute-start | bytes 1032200 | tf_op jit(solution)/shard_map/ppermute | solution.py:22
  11.4 0.8 convert_reduce_fusion
  12.5 0.7 fusion.40
  13.2 0.7 fusion.39
  13.9 5.7 %sort.17 = (s32[2048]{0:T(1024)}, s32[2048]{0:T(1024)S(1)}) sort(s32[2048]{0:T(1024)} %param.26, s32[2048]{0:T(1024)S(1)} %iota.22), dimensions={0}, to_apply=%region_0.1 | sort | flops 22528 | bytes 32768 | tf_op jit(solution)/shard_map/jit(argsort)/sort | solution.py:110
  19.7 11.8 %gather_fusion = s32[2048]{0:T(1024)S(1)} fusion(s32[2048]{0:T(1024)S(1)} %copy-done.1, s32[2048]{0:T(1024)S(1)} %get-tuple-element.85), kind=kCustom, calls=%fused_computation | custom fusion | bytes 24576 | tf_op jit(solution)/shard_map/gather | solution.py:111
  31.5 4.4 compare_select_fusion.6
  36.6 15.7 %fusion.33 = s32[2048]{0:T(1024)S(1)} fusion(pred[2048]{0:T(1024)(128)(4,1)S(1)} %get-tuple-element.71, pred[2048]{0:T(1024)(128)(4,1)S(1)} %get-tuple-element.70, pred[2048]{0:T(1024)(128)(4,1)S(1)} %get-tuple-element.69, pred[2048]{0:T(1024)(128)(4,1)S(1)} %get-tuple-element.68, pred[2048]{0:T(1024)(128)(4,1)S(1)} %get-tuple-element.67, ...), kind=kLoop, calls=%fused_computation.118 | loop fusion | flops 57344 | bytes 75876 | tf_op jit(solution)/shard_map/add | solution.py:119
  52.3 8.0 %scatter_custom_fusion = s32[2048]{0:T(1024)S(1)} fusion(s32[2048]{0:T(1024)S(1)} %get-tuple-element.86, s32[2048]{0:T(1024)S(1)} %fusion.33, s32[]{:T(128)} %constant.114.clone.1), kind=kCustom, calls=%fused_computation.124 | custom fusion | bytes 8196 | tf_op jit(solution)/shard_map/scatter | solution.py:119
  60.3 8.8 %scatter_custom_fusion.1 = s32[4096]{0:T(1024)} fusion(s32[2048]{0:T(1024)S(1)} %get-tuple-element.84, s32[2048]{0:T(1024)} %param.27, s32[]{:T(128)} %constant.116.clone.1), kind=kCustom, calls=%fused_computation.120 | custom fusion | bytes 16896 | tf_op jit(solution)/shard_map/scatter | solution.py:124
  69.1 7.7 %all-to-all-start = ((s32[1,32,128]{2,0,1:T(1,128)}), s32[1,32,128]{2,0,1:T(1,128)S(1)}, u32[]{:S(2)}, u32[]{:S(2)}) async-start(s32[1,32,128]{2,0,1:T(1,128)} %bitcast.35), calls=%async_computation | async-start | bytes 32768 | tf_op jit(solution)/shard_map/all_to_all | solution.py:127
  76.9 0.8 gather_fusion.3
  77.7 0.8 gather_fusion.2
  79.1 0.6 compare_select_fusion.1
  80.9 4.7 copy.126
  85.6 34.3 %gather_fusion.1 = f32[9216,16]{1,0:T(8,128)} fusion(f32[16,16128]{0,1:T(8,128)} %copy.126, s32[9216]{0:T(1024)S(1)} %broadcast_clamp_fusion), kind=kCustom, calls=%fused_computation.1 | custom fusion | bytes 1216512 | tf_op jit(solution)/shard_map/gather | solution.py:102
  119.9 5.6 %copy.127 = f32[144,64,16]{0,1,2:T(8,128)S(1)} copy(f32[144,64,16]{2,1,0:T(8,128)} %bitcast.148) | data formatting | bytes 1179648 | tf_op jit(solution)/shard_map/gather | solution.py:102
  125.5 1.0 convolution_bitcast_fusion.3
  127.6 2.0 copy.129
  129.6 22.9 %scatter_custom_fusion.2 = f32[51,2048]{0,1:T(8,128)S(1)} fusion(s32[4096]{0:T(1024)} %bitcast.163, f32[4096,51]{1,0:T(8,128)} %copy.129, f32[]{:T(128)} %constant.112.clone.1), kind=kCustom, calls=%fused_computation.56 | custom fusion | flops 208896 | bytes 418304 | tf_op jit(solution)/shard_map/scatter-add | solution.py:108
  152.5 6.3 %scatter_custom_fusion.3 = f32[51,4096]{0,1:T(8,128)S(1)} fusion(s32[2048]{0:T(1024)} %copy-done.11, f32[51,2048]{0,1:T(8,128)S(1)} %scatter_custom_fusion.2, f32[]{:T(128)} %constant.112.clone.1), kind=kCustom, calls=%fused_computation.34 | custom fusion | bytes 1253888 | tf_op jit(solution)/shard_map/scatter | solution.py:135
  158.8 1.6 copy.130
  160.4 10.1 %all-to-all-start.1 = ((f32[51,32,128]{2,0,1:T(8,128)}), f32[51,32,128]{2,0,1:T(8,128)S(1)}, u32[]{:S(2)}, u32[]{:S(2)}) async-start(f32[51,32,128]{2,0,1:T(8,128)} %copy.130), calls=%async_computation.1 | async-start | bytes 1835008 | tf_op jit(solution)/shard_map/all_to_all | solution.py:136
  170.5 24.5 %all-to-all-done.1 = f32[51,32,128]{2,0,1:T(8,128)S(1)} async-done(((f32[51,32,128]{2,0,1:T(8,128)}), f32[51,32,128]{2,0,1:T(8,128)S(1)}, u32[]{:S(2)}, u32[]{:S(2)}) %all-to-all-start.1) | async-done | bytes 835616 | tf_op jit(solution)/shard_map/all_to_all | solution.py:136
  195.1 2.0 copy.131
  197.1 3.6 bitcast_select_fusion.1
  200.7 25.4 %scatter_custom_fusion.4 = f32[51,1728]{0,1:T(8,128)S(1)} fusion(s32[4096]{0:T(1024)S(1)} %bitcast.160, f32[51,4096]{0,1:T(8,128)S(1)} %bitcast_select_fusion.1, f32[]{:T(128)} %constant.112.clone.1), kind=kCustom, calls=%fused_computation.24 | custom fusion | flops 208896 | bytes 2449668 | tf_op jit(solution)/shard_map/scatter-add | solution.py:146
  227.3 0.7 copy-done.6
  228.4 10.8 %gather_fusion.4 = f32[4096,48]{1,0:T(8,128)S(1)} fusion(f32[48,1728]{0,1:T(8,128)S(1)} %copy.134, s32[4096]{0:T(1024)S(1)} %broadcast_clamp_fusion.2), kind=kCustom, calls=%fused_computation.4 | custom fusion | bytes 1589248 | tf_op jit(solution)/shard_map/gather | solution.py:151
  239.7 1.0 broadcast_select_fusion.1
  240.7 4.9 all-to-all-start.2
  245.6 21.3 %all-to-all-done.2 = f32[48,32,128]{2,0,1:T(8,128)S(1)} async-done(((f32[48,32,128]{2,0,1:T(8,128)}), f32[48,32,128]{2,0,1:T(8,128)S(1)}, u32[]{:S(2)}, u32[]{:S(2)}) %all-to-all-start.2) | async-done | bytes 786464 | tf_op jit(solution)/shard_map/all_to_all | solution.py:154
  267.5 5.5 %gather_fusion.5 = f32[2048,48]{1,0:T(8,128)S(1)} fusion(f32[48,4096]{0,1:T(8,128)S(1)} %bitcast.143, s32[2048]{0:T(1024)S(1)} %get-tuple-element.83), kind=kCustom, calls=%fused_computation.5 | custom fusion | bytes 794624 | tf_op jit(solution)/shard_map/gather | solution.py:157
  273.0 14.1 %gather_fusion.6 = f32[4096,48]{1,0:T(8,128)} fusion(f32[48,2048]{0,1:T(8,128)S(1)} %bitcast.140, s32[4096]{0:T(1024)S(1)} %broadcast_clamp_fusion.1), kind=kCustom, calls=%fused_computation.6 | custom fusion | bytes 1589248 | tf_op jit(solution)/shard_map/gather | solution.py:166
  287.1 3.0 copy.137
  290.1 1.4 convolution_bitcast_fusion
  291.5 1.4 convolution_bitcast_fusion.1
  294.8 2.0 copy.139
  296.7 22.9 %scatter_custom_fusion.5 = f32[48,2048]{0,1:T(8,128)S(1)} fusion(s32[4096]{0:T(1024)} %bitcast.164, f32[4096,48]{1,0:T(8,128)} %copy.139, f32[]{:T(128)} %constant.112.clone.1), kind=kCustom, calls=%fused_computation.54 | custom fusion | flops 196608 | bytes 393728 | tf_op jit(solution)/shard_map/scatter-add | solution.py:174
  319.6 6.3 %scatter_custom_fusion.6 = f32[48,4096]{0,1:T(8,128)S(1)} fusion(s32[2048]{0:T(1024)} %copy-done.11, f32[48,2048]{0,1:T(8,128)S(1)} %scatter_custom_fusion.5, f32[]{:T(128)} %constant.112.clone.1), kind=kCustom, calls=%fused_computation.32 | custom fusion | bytes 1180160 | tf_op jit(solution)/shard_map/scatter | solution.py:135
  326.5 25.4 %all_to_all.25 = f32[48,32,128]{2,0,1:T(8,128)S(1)} all-to-all(f32[48,32,128]{2,0,1:T(8,128)S(1)} %copy.140), channel_id=1, replica_groups=mesh['grp'=8,'dev'=32] {'dev'}, dimensions={1} | all-to-all | bytes 1572864 | tf_op jit(solution)/shard_map/all_to_all | solution.py:136
  351.9 2.0 copy.141
  353.8 3.6 bitcast_select_fusion
  357.5 25.7 %scatter_custom_fusion.7 = f32[48,1728]{0,1:T(8,128)S(1)} fusion(s32[4096]{0:T(1024)} %bitcast.161, f32[48,4096]{0,1:T(8,128)S(1)} %bitcast_select_fusion, f32[]{:T(128)} %constant.112.clone.1), kind=kCustom, calls=%fused_computation.21 | custom fusion | flops 196608 | bytes 1118720 | tf_op jit(solution)/shard_map/scatter-add | solution.py:146
  383.4 1.1 divide_add_fusion
  384.8 10.8 %gather_fusion.7 = f32[4096,48]{1,0:T(8,128)S(1)} fusion(f32[48,1728]{0,1:T(8,128)S(1)} %copy.143, s32[4096]{0:T(1024)S(1)} %broadcast_clamp_fusion.2), kind=kCustom, calls=%fused_computation.7 | custom fusion | bytes 1589248 | tf_op jit(solution)/shard_map/gather | solution.py:151
  396.3 25.0 %all_to_all.26 = f32[48,32,128]{2,0,1:T(8,128)S(1)} all-to-all(f32[48,32,128]{2,0,1:T(8,128)S(1)} %broadcast_select_fusion), channel_id=1, replica_groups=mesh['grp'=8,'dev'=32] {'dev'}, dimensions={1} | all-to-all | bytes 1572864 | tf_op jit(solution)/shard_map/all_to_all | solution.py:154
  421.9 5.5 %gather_fusion.8 = f32[2048,48]{1,0:T(8,128)S(1)} fusion(f32[48,4096]{0,1:T(8,128)S(1)} %bitcast.144, s32[2048]{0:T(1024)S(1)} %get-tuple-element.83), kind=kCustom, calls=%fused_computation.8 | custom fusion | bytes 794624 | tf_op jit(solution)/shard_map/gather | solution.py:157
  427.4 10.8 %gather_fusion.9 = f32[4096,48]{1,0:T(8,128)S(1)} fusion(f32[48,2048]{0,1:T(8,128)S(1)} %bitcast.139, s32[4096]{0:T(1024)S(1)} %broadcast_clamp_fusion.1), kind=kCustom, calls=%fused_computation.9 | custom fusion | bytes 1589248 | tf_op jit(solution)/shard_map/gather | solution.py:166
  438.2 2.2 copy.146
  440.3 1.9 reshape_reshape.3
  442.3 1.5 convolution_bitcast_fusion.2
  443.8 5.0 copy.155
  448.8 53.6 %scatter_custom_fusion.8 = f32[16,16128]{0,1:T(8,128)} fusion(s32[9216]{0:T(1024)S(1)} %reshape.576, f32[9216,16]{1,0:T(8,128)} %bitcast.152, f32[]{:T(128)} %constant.112.clone.1), kind=kCustom, calls=%fused_computation.19 | custom fusion | flops 147456 | bytes 1032704 | tf_op jit(solution)/shard_map/scatter-add | solution.py:183
  502.4 6.4 %fusion.38 = (f32[16,5376]{0,1:T(8,128)}, f32[16,5376]{0,1:T(8,128)}, f32[16,5376]{0,1:T(8,128)S(1)}) fusion(f32[16,16128]{0,1:T(8,128)} %scatter_custom_fusion.8), kind=kLoop, calls=%fused_computation.133 | loop fusion | bytes 2064384 | tf_op jit(solution)/shard_map/slice | solution.py:186
  508.8 3.2 copy.151
  512.1 3.3 copy.152
  515.3 1.9 collective-permute-start.3
  517.2 4.1 collective-permute-start.2
  521.4 0.7 copy.159
  522.1 2.9 collective-permute-done.3
  525.0 8.8 %collective-permute-done.2 = f32[16,5376]{1,0:T(8,128)} collective-permute-done((f32[16,5376]{1,0:T(8,128)}, f32[16,5376]{1,0:T(8,128)}, u32[]{:S(2)}, u32[]{:S(2)}) %collective-permute-start.2) | collective-permute-done | bytes 344096 | tf_op jit(solution)/shard_map/ppermute | solution.py:21
  533.7 1.9 add_add_fusion
  (109 shorter events, 10.6 us)
Async XLA Ops:
  0.0 125.5 %copy-start = (f32[144,192]{1,0:T(8,128)S(1)}, f32[144,192]{1,0:T(8,128)}, u32[]{:S(2)}) copy-start(f32[144,192]{1,0:T(8,128)} %param.19) | copy-start | bytes 331780
  0.0 19.7 %copy-start.1 = (s32[2048]{0:T(1024)S(1)}, s32[2048]{0:T(1024)}, u32[]{:S(2)}) copy-start(s32[2048]{0:T(1024)} %param.26) | copy-start | bytes 24580
  0.0 80.8 %collective-permute-start = (f32[16,5376]{1,0:T(8,128)}, f32[16,5376]{1,0:T(8,128)S(1)}, u32[]{:S(2)}, u32[]{:S(2)}) collective-permute-start(f32[16,5376]{1,0:T(8,128)} %param.18), channel_id=1, source_target_pairs={{0,1},{1,2},{2,3},{3,4},{4,5},{5,6},{6,7},{7,8},{8,9},{9,10},{10,1... | collective-permute-start | bytes 1032200 | tf_op jit(solution)/shard_map/ppermute | solution.py:21
  4.0 76.8 %collective-permute-start.1 = (f32[16,5376]{1,0:T(8,128)}, f32[16,5376]{1,0:T(8,128)S(1)}, u32[]{:S(2)}, u32[]{:S(2)}) collective-permute-start(f32[16,5376]{1,0:T(8,128)} %param.18), channel_id=1, source_target_pairs={{1,0},{2,1},{3,2},{4,3},{5,4},{6,5},{7,6},{8,7},{9,8},{10,9},{11,1... | collective-permute-start | bytes 1032200 | tf_op jit(solution)/shard_map/ppermute | solution.py:22
  19.7 57.2 %copy-start.2 = (f32[64,64]{1,0:T(8,128)S(1)}, f32[64,64]{1,0:T(8,128)}, u32[]{:S(2)}) copy-start(f32[64,64]{1,0:T(8,128)} %param.21) | copy-start | bytes 49156
  19.7 58.0 %copy-start.3 = (f32[64,64]{1,0:T(8,128)S(1)}, f32[64,64]{1,0:T(8,128)}, u32[]{:S(2)}) copy-start(f32[64,64]{1,0:T(8,128)} %param.20) | copy-start | bytes 49156
  19.7 58.8 %copy-start.18 = (f32[6,64]{1,0:T(8,128)S(1)}, f32[6,64]{1,0:T(8,128)}, u32[]{:S(2)}) copy-start(f32[6,64]{1,0:T(8,128)} %param.22) | copy-start | bytes 4612
  19.7 59.3 %copy-start.8 = (s32[64,64]{1,0:T(8,128)S(1)}, s32[64,64]{1,0:T(8,128)}, u32[]{:S(2)}) copy-start(s32[64,64]{1,0:T(8,128)} %param.25) | copy-start | bytes 49156
  19.7 60.7 %copy-start.19 = (f32[64]{0:T(128)S(1)}, f32[64]{0:T(128)}, u32[]{:S(2)}) copy-start(f32[64]{0:T(128)} %param.23) | copy-start | bytes 772
  31.5 49.0 %copy-start.9 = (s32[144,64]{0,1:T(8,128)S(1)}, s32[144,64]{0,1:T(8,128)}, u32[]{:S(2)}) copy-start(s32[144,64]{0,1:T(8,128)} %param.24) | copy-start | bytes 110596
  31.5 49.3 %copy-start.7 = (f32[16,5376]{1,0:T(8,128)S(1)}, f32[16,5376]{1,0:T(8,128)}, u32[]{:S(2)}) copy-start(f32[16,5376]{1,0:T(8,128)} %param.18) | copy-start | bytes 1032196
  60.3 8.8 %copy-start.11 = (s32[2048]{0:T(1024)}, s32[2048]{0:T(1024)S(1)}, u32[]{:S(2)}) copy-start(s32[2048]{0:T(1024)S(1)} %get-tuple-element.84) | copy-start | bytes 24580
  69.1 91.2 %all-to-all-start = ((s32[1,32,128]{2,0,1:T(1,128)}), s32[1,32,128]{2,0,1:T(1,128)S(1)}, u32[]{:S(2)}, u32[]{:S(2)}) async-start(s32[1,32,128]{2,0,1:T(1,128)} %bitcast.35), calls=%async_computation | async-start | bytes 32768 | tf_op jit(solution)/shard_map/all_to_all | solution.py:127
  79.0 1.6 copy-start.12
  79.0 1.6 copy-start.14
  79.0 1.6 copy-start.16
  160.4 34.7 %all-to-all-start.1 = ((f32[51,32,128]{2,0,1:T(8,128)}), f32[51,32,128]{2,0,1:T(8,128)S(1)}, u32[]{:S(2)}, u32[]{:S(2)}) async-start(f32[51,32,128]{2,0,1:T(8,128)} %copy.130), calls=%async_computation.1 | async-start | bytes 1835008 | tf_op jit(solution)/shard_map/all_to_all | solution.py:136
  170.5 30.2 %copy-start.10 = (s32[4096,1]{0,1:T(1,128)}, s32[4096,1]{0,1:T(1,128)S(1)}, u32[]{:S(2)}) copy-start(s32[4096,1]{0,1:T(1,128)S(1)} %compare_select_fusion.2) | copy-start | bytes 49156
  226.7 1.4 copy-start.4
  227.3 0.7 copy-start.6
  240.7 26.3 %all-to-all-start.2 = ((f32[48,32,128]{2,0,1:T(8,128)}), f32[48,32,128]{2,0,1:T(8,128)S(1)}, u32[]{:S(2)}, u32[]{:S(2)}) async-start(f32[48,32,128]{2,0,1:T(8,128)} %broadcast_select_fusion.1), calls=%async_computation.2 | async-start | bytes 1572864 | tf_op jit(solution)/shard_map/all_to_all | solution.py:154
  291.5 1.5 copy-start.13
  291.5 1.5 copy-start.15
  291.5 1.5 copy-start.17
  291.5 1.5 copy-start.20
  291.5 1.5 copy-start.21
  291.5 1.5 copy-start.22
  291.5 1.5 copy-start.23
  357.5 26.0 %copy-start.5 = (f32[48,1728]{1,0:T(8,128)S(1)}, f32[48,1728]{1,0:T(8,128)}, u32[]{:S(2)}) copy-start(f32[48,1728]{1,0:T(8,128)} %copy-done.4) | copy-start | bytes 995332
  515.3 9.7 %collective-permute-start.3 = (f32[16,5376]{1,0:T(8,128)}, f32[16,5376]{1,0:T(8,128)}, u32[]{:S(2)}, u32[]{:S(2)}) collective-permute-start(f32[16,5376]{1,0:T(8,128)} %copy.152), channel_id=1, source_target_pairs={{1,0},{2,1},{3,2},{4,3},{5,4},{6,5},{7,6},{8,7},{9,8},{10,9},{11,1... | collective-permute-start | bytes 1032200 | tf_op jit(solution)/shard_map/ppermute | solution.py:22
  517.2 16.5 %collective-permute-start.2 = (f32[16,5376]{1,0:T(8,128)}, f32[16,5376]{1,0:T(8,128)}, u32[]{:S(2)}, u32[]{:S(2)}) collective-permute-start(f32[16,5376]{1,0:T(8,128)} %copy.151), channel_id=1, source_target_pairs={{0,1},{1,2},{2,3},{3,4},{4,5},{5,6},{6,7},{7,8},{8,9},{9,10},{10,1... | collective-permute-start | bytes 1032200 | tf_op jit(solution)/shard_map/ppermute | solution.py:21
where the time goes:
time: 542 us; the launch traced here: 536 us
  local copies, waits for them, and re-layouts  191 us (35%)
  other arithmetic  191 us (35%)
  waiting for transfers between devices  57.4 us (11%)
  blocking collectives  50.5 us (9%)
  starting transfers between devices  40 us (7%)
    scatter-add x1, other arithmetic, per_device(): collected = jnp.zeros((rhs_count, edge_count + 2 * edge_count), jnp.float...  53.6 us
    scatter-add x2, other arithmetic, send_home(): return jnp.zeros((rows, owned), jnp.float32).at[:, safe_slots].add(jnp.wh...  51.1 us
    gather x2, local copies, waits for them, and re-layouts, per_device(): edge_values = extended[:, local_edges]  39.9 us
    gather x4, local copies, waits for them, and re-layouts, element_values(): touched_values[:, local_map].reshape(rhs_count, 3, node_count, elem_count)  30 us
    all_to_all x1, blocking collectives, send_home(): lax.all_to_all(packed.reshape(rows, peer_count, capacity), 'dev', split_a...  25.4 us
    all_to_all x1, blocking collectives, fetch_home(): lax.all_to_all(wanted, 'dev', split_axis=1, concat_axis=1, tiled=True)  25 us
    all_to_all x1, waiting for transfers between devices, send_home(): lax.all_to_all(packed.reshape(rows, peer_count, capacity), 'dev', split_a...  24.5 us
    scatter-add x1, other arithmetic, per_device(): jnp.zeros((term_rows.shape[0], touched), jnp.float32).at[:, flat_ids]  22.9 us
  transfers between devices with their start and end apart: 7, of which 4 were waited for; matrix products, arithmetic and copies ran while one was open for 26% of the time, Pallas kernels for 0%

commit v1 on v0

v1 whole, which is shorter than its diff:
```python
import jax
import jax.numpy as jnp
from jax import lax
from jax.experimental import pallas as pl
from jax.experimental.pallas import tpu as pltpu
from jax.sharding import PartitionSpec as P

RHS = 16
ED = 144
NN = 64
EL = 64
E_LOC = 5376
RIM = 672
U_LOC = 2048
PEERS = 32
CAP = 128
ROWS = 3 * RHS
SENT = ROWS + 4
SLOTS = PEERS * CAP
ELN = NN * EL
LANE = 128
WIDE = 256
RIM_W = 768
H_OWN = E_LOC // WIDE
H_RIM = RIM_W // WIDE
H_EDGE = H_OWN + 2 * H_RIM
H_POS = SLOTS // WIDE
H_NODE = 7
E_TILES = 72
N_TILES = ELN // LANE
BF = jnp.bfloat16
F32 = jnp.float32
I32 = jnp.int32

CHEB_LOW = 0.3
CHEB_HIGH = 2.0


def cheb_factors():
    center = 0.5 * (CHEB_HIGH + CHEB_LOW)
    half_width = 0.5 * (CHEB_HIGH - CHEB_LOW)
    sigma_ratio = center / half_width
    rho_first = 1.0 / sigma_ratio
    rho_second = 1.0 / (2.0 * sigma_ratio - rho_first)
    return (1.0 / center, 1.0 + rho_second * rho_first, 2.0 * rho_second / half_width)


def split(x):
    high = x.astype(BF)
    return high, (x - high.astype(F32)).astype(BF)


def iota(shape, dim):
    return lax.broadcasted_iota(I32, shape, dim)


def spread(index_rows, height):
    return jnp.concatenate(
        [jnp.broadcast_to(index_rows[i : i + 1], (height, LANE)) for i in range(index_rows.shape[0])],
        axis=1,
    )


def one_hot_low(index_rows):
    low = spread(index_rows & (WIDE - 1), WIDE)
    return jnp.where(low == iota(low.shape, 0), 1.0, 0.0).astype(BF)


def gather_tile(table, index_rows, rows, count):
    hot = one_hot_low(index_rows)
    found = jnp.dot(table, jnp.concatenate([hot, hot], axis=0), preferred_element_type=F32)
    high = spread(index_rows >> 8, rows)
    out = found[:rows]
    for h in range(1, count):
        out = jnp.where(high == h, found[h * rows : (h + 1) * rows], out)
    return out


def fill_table(table, source, rows, count):
    for h in range(count):
        high, low = split(source(h))
        table[h * rows : (h + 1) * rows, :WIDE] = high
        table[h * rows : (h + 1) * rows, WIDE:] = low


def mask_rows(left, base, x, high_part, count):
    rows, width = x[0].shape
    high_b = jnp.broadcast_to(high_part, (rows, width))
    for h in range(count):
        here = high_b == float(h)
        for k in (0, 1):
            left[base + h * rows : base + (h + 1) * rows, k * width : (k + 1) * width] = jnp.where(
                here, x[k], jnp.zeros_like(x[k])
            )


def high_bf(index_rows):
    return spread((index_rows >> 8), 1).astype(F32).astype(BF)


def mask_diag(left, base, diag, index_rows):
    width = diag[0].shape[1]
    here = spread(index_rows >> 8, 16) == iota((16, width), 0)
    for c in range(3):
        high, low = split(jnp.where(here, jnp.broadcast_to(diag[c], (16, width)), 0.0))
        left[base + c * 16 : base + (c + 1) * 16, :width] = high
        left[base + c * 16 : base + (c + 1) * 16, width:] = low


def accumulate(acc, step, left, index_rows):
    hot = one_hot_low(index_rows)
    part = lax.dot_general(
        left[...],
        jnp.concatenate([hot, hot], axis=1),
        (((1,), (1,)), ((), ())),
        preferred_element_type=F32,
    )

    @pl.when(step == 0)
    def _():
        acc[...] = part

    @pl.when(step > 0)
    def _():
        acc[...] += part


def rows8(step):
    return pl.ds(pl.multiple_of(step * 8, 8), 8)


def lanes(step, width):
    return pl.ds(pl.multiple_of(step * width, width), width)


def prep_kernel(res, em, lm, owner, slot, epos_out, pos_out, slot_out, ev_out, table, hots, rank_s, pos_s):
    m = em[...]
    epos_out[...] = jnp.where(
        m < RIM,
        m + (E_LOC + RIM_W - RIM),
        jnp.where(m < RIM + E_LOC, m - RIM, m - (RIM + E_LOC) + E_LOC + RIM_W),
    )
    chunks = U_LOC // LANE
    for t in range(chunks):
        o = jnp.broadcast_to(owner[t : t + 1, :], (PEERS, LANE))
        hots[t * PEERS : (t + 1) * PEERS, :] = jnp.where(o == iota((PEERS, LANE), 0), 1.0, 0.0).astype(BF)
    before = jnp.where(iota((LANE, LANE), 0) < iota((LANE, LANE), 1), 1.0, 0.0)
    tri = jnp.concatenate([before, jnp.ones((LANE, LANE), F32)], axis=1).astype(BF)
    ranks = jnp.dot(hots[...], tri, preferred_element_type=F32)
    base = jnp.zeros((PEERS, LANE), F32)
    for t in range(chunks):
        hot = hots[t * PEERS : (t + 1) * PEERS, :].astype(F32)
        here = ranks[t * PEERS : (t + 1) * PEERS]
        rank = jnp.sum(hot * (here[:, :LANE] + base), axis=0, keepdims=True).astype(I32)
        base = base + here[:, LANE:]
        rank_s[t : t + 1, :] = rank
        pos_s[t : t + 1, :] = owner[t : t + 1, :] * CAP + rank
    left = []
    right = []
    for t in range(chunks):
        hot = hots[t * PEERS : (t + 1) * PEERS, :].astype(F32)
        s = slot[t : t + 1, :] + 1
        left.append(
            jnp.concatenate([hot * (s >> 6).astype(F32), hot * (s & 63).astype(F32)], axis=0).astype(BF)
        )
        r = jnp.broadcast_to(rank_s[t : t + 1, :], (LANE, LANE))
        right.append(jnp.where(r == iota((LANE, LANE), 0), 1.0, 0.0).astype(BF))
    packed = lax.dot_general(
        jnp.concatenate(left, axis=1),
        jnp.concatenate(right, axis=1),
        (((1,), (1,)), ((), ())),
        preferred_element_type=F32,
    )
    slot_out[...] = packed[:PEERS] * 64.0 + packed[PEERS:] - 1.0
    idx = lm[...]
    high, low = idx >> 7, idx & (LANE - 1)
    pos = jnp.zeros((N_TILES, LANE), I32)
    for t in range(chunks):
        row = jnp.broadcast_to(pos_s[t : t + 1, :], (N_TILES, LANE))
        pos = jnp.where(high == t, jnp.take_along_axis(row, low, axis=1), pos)
    pos_out[...] = pos
    fill_table(table, lambda h: res[:, h * WIDE : (h + 1) * WIDE], RHS, H_OWN)

    def body(step, carry):
        ev_out[:, lanes(step, 1024)] = gather_tile(table[...], epos_out[rows8(step), :], RHS, H_OWN)
        return carry

    lax.fori_loop(0, E_TILES // 8, body, 0)


def fill_pi(w, pi):
    zero = jnp.zeros((384, 384), BF)
    for v in range(4):
        for k in (0, 1):
            w[v, k] = zero
    for c in range(3):
        part = split(pi[:, c * NN : (c + 1) * NN])
        for k in (0, 1):
            for e2 in (0, 1):
                cols = slice(c * LANE + e2 * NN, c * LANE + (e2 + 1) * NN)
                for v in range(4):
                    w[v, k, e2 * LANE : (e2 + 1) * LANE, cols] = part[k][:LANE]
                    at = 2 * LANE + (2 * v + e2) * 16
                    w[v, k, at : at + 16, cols] = part[k][LANE:]


def fill_coefs(coef, wide, perm, curl):
    coef[...] = jnp.zeros((8, LANE), F32)
    coef[0:6, 0:EL] = perm[...]
    coef[6:7, 0:EL] = curl[...]
    c = coef[...]
    second = jnp.where(iota((8, LANE), 1) >= NN, 1, 0)
    for t in range(N_TILES):
        wide[:, t * LANE : (t + 1) * LANE] = jnp.take_along_axis(c, second + 2 * t, axis=1)


def restrict_kernel(
    ev_own, before, after, epos, pos, slots, pi, stiff, mass, perm, curl,
    out, table, ev, w, coef, wide, xs, diag, left, acc,
):
    def rim(h):
        ref = before if h < H_RIM else after
        at = h % H_RIM * WIDE
        return ref[:, at : at + WIDE]

    fill_table(table, rim, RHS, 2 * H_RIM)

    def rim_body(step, carry):
        idx = epos[rows8(step), :] - E_LOC
        found = gather_tile(table[...], idx, RHS, 2 * H_RIM)
        at = lanes(step, 1024)
        ev[:, at] = jnp.where(spread(idx, RHS) >= 0, found, ev_own[:, at])
        return carry

    lax.fori_loop(0, E_TILES // 8, rim_body, 0)
    fill_pi(w, pi)
    for v in range(4):
        blocks = []
        for g in range(8):
            t = 4 * g + v
            blocks.append(
                jnp.concatenate(
                    [ev[:, 2 * t * LANE : (2 * t + 2) * LANE], ev[:, (EL + g) * LANE : (EL + g + 1) * LANE]],
                    axis=1,
                )
            )
        high, low = split(jnp.concatenate(blocks, axis=0))
        y = (
            jnp.dot(high, w[v, 0], preferred_element_type=F32)
            + jnp.dot(high, w[v, 1], preferred_element_type=F32)
            + jnp.dot(low, w[v, 0], preferred_element_type=F32)
        )
        for g in range(8):
            t = 4 * g + v
            for c in range(3):
                part = split(y[g * RHS : (g + 1) * RHS, c * LANE : (c + 1) * LANE])
                for k in (0, 1):
                    xs[k, c * RHS : (c + 1) * RHS, t * LANE : (t + 1) * LANE] = part[k]
    fill_coefs(coef, wide, perm, curl)
    eye = iota((NN, NN), 0) == iota((NN, NN), 1)

    def diagonal(ref):
        d = jnp.sum(jnp.where(eye, ref[...], 0.0), axis=0, keepdims=True)
        return jnp.concatenate([d, d], axis=1)

    sd, md = diagonal(stiff), diagonal(mass)
    for t in range(N_TILES):
        at = slice(t * LANE, (t + 1) * LANE)
        diag[:, at] = wide[6:7, at] * sd + md * wide[0:3, at]

    def body(step, carry):
        at = lanes(step, 1024)
        idx = pos[rows8(step), :]
        mask_rows(left, 0, (xs[0, :, at], xs[1, :, at]), high_bf(idx), H_POS)
        mask_diag(left, H_POS * ROWS, [diag[c : c + 1, at] for c in range(3)], idx)
        accumulate(acc, step, left, idx)
        return carry

    lax.fori_loop(0, ELN // 1024, body, 0)
    unpack(out, acc)
    for p in range(PEERS):
        h, at = p // 2, slice(p % 2 * LANE, (p % 2 + 1) * LANE)
        for c in range(3):
            row = H_POS * ROWS + c * 16 + h
            out[p, ROWS + c : ROWS + c + 1, :] = acc[row : row + 1, at]
        out[p, SENT - 1 : SENT, :] = slots[p : p + 1, :]


def unpack(out, acc):
    for p in range(PEERS):
        h, at = p // 2, slice(p % 2 * LANE, (p % 2 + 1) * LANE)
        out[p, 0:ROWS, :] = acc[h * ROWS : (h + 1) * ROWS, at]


def collect(arrived, slots, left, acc, with_diag):
    def body(step, carry):
        idx = slots[rows8(step), :]
        block = arrived[rows8(step)]
        x = jnp.concatenate([block[i, 0:ROWS] for i in range(8)], axis=1)
        mask_rows(left, 0, split(x), high_bf(idx), H_NODE)
        if with_diag:
            diag = [
                jnp.concatenate([block[i, ROWS + c : ROWS + c + 1] for i in range(8)], axis=1)
                for c in range(3)
            ]
            mask_diag(left, H_NODE * ROWS, diag, idx)
        accumulate(acc, step, left, idx)
        return carry

    lax.fori_loop(0, PEERS // 8, body, 0)


def serve(out, table, slots):
    def body(step, carry):
        found = gather_tile(table[...], slots[rows8(step), :], ROWS, H_NODE)
        for i in range(8):
            out[step * 8 + i] = found[:, i * LANE : (i + 1) * LANE]
        return carry

    lax.fori_loop(0, PEERS // 8, body, 0)


def first_kernel(arrived, out, rhs_out, floor_out, slot_out, table, left, acc):
    first = cheb_factors()[0]
    for p in range(PEERS):
        slot_out[p : p + 1, :] = arrived[p, SENT - 1 : SENT, :].astype(I32)
    collect(arrived, slot_out, left, acc, True)
    for h in range(H_NODE):
        rhs_out[h] = acc[h * ROWS : (h + 1) * ROWS, :]
        for c in range(3):
            row = H_NODE * ROWS + c * 16 + h
            floor_out[h, c : c + 1, :] = jnp.maximum(acc[row : row + 1, :], 1.0)

    def value(h):
        parts = []
        for c in range(3):
            part = rhs_out[h, c * RHS : (c + 1) * RHS, :]
            parts.append(first * part / floor_out[h, c : c + 1, :])
        return jnp.concatenate(parts, axis=0)

    fill_table(table, value, ROWS, H_NODE)
    serve(out, table, slot_out)


def second_kernel(arrived, rhs, floor, slots, out, table, left, acc):
    first, keep, step = cheb_factors()
    collect(arrived, slots, left, acc, False)

    def value(h):
        parts = []
        for c in range(3):
            at = slice(c * RHS, (c + 1) * RHS)
            part = rhs[h, at, :]
            applied = acc[h * ROWS + c * RHS : h * ROWS + (c + 1) * RHS, :]
            low = floor[h, c : c + 1, :]
            parts.append(keep * (first * part / low) + step * (part - applied) / low)
        return jnp.concatenate(parts, axis=0)

    fill_table(table, value, ROWS, H_NODE)
    serve(out, table, slots)


def pair(arrived):
    return lambda h: jnp.concatenate([arrived[2 * h], arrived[2 * h + 1]], axis=1)


def apply_kernel(arrived, pos, stiff, mass, perm, curl, out, table, op, coef, wide, left, acc):
    fill_table(table, pair(arrived), ROWS, H_POS)
    fill_coefs(coef, wide, perm, curl)
    op[...] = jnp.zeros((2, LANE, 2 * LANE), BF)
    for m, ref in enumerate((stiff, mass)):
        part = split(ref[...].T)
        for k in (0, 1):
            for e2 in (0, 1):
                at = slice(m * LANE + e2 * NN, m * LANE + (e2 + 1) * NN)
                op[k, e2 * NN : (e2 + 1) * NN, at] = part[k]

    def body(step, carry):
        idx = pos[rows8(step), :]
        values = gather_tile(table[...], idx, ROWS, H_POS)
        high, low = split(
            jnp.concatenate([values[:, i * LANE : (i + 1) * LANE] for i in range(8)], axis=0)
        )
        y = (
            jnp.dot(high, op[0], preferred_element_type=F32)
            + jnp.dot(high, op[1], preferred_element_type=F32)
            + jnp.dot(low, op[0], preferred_element_type=F32)
        )
        cols = wide[:, lanes(step, 1024)]
        tiles = []
        for i in range(8):
            k = cols[:, i * LANE : (i + 1) * LANE]
            s = [y[i * ROWS + c * RHS : i * ROWS + (c + 1) * RHS, :LANE] for c in range(3)]
            m = [y[i * ROWS + c * RHS : i * ROWS + (c + 1) * RHS, LANE:] for c in range(3)]
            tensor = ((0, 3, 4), (3, 1, 5), (4, 5, 2))
            tiles.append(
                jnp.concatenate(
                    [
                        k[6:7] * s[c]
                        + k[tensor[c][0]][None] * m[0]
                        + k[tensor[c][1]][None] * m[1]
                        + k[tensor[c][2]][None] * m[2]
                        for c in range(3)
                    ],
                    axis=0,
                )
            )
        mask_rows(left, 0, split(jnp.concatenate(tiles, axis=1)), high_bf(idx), H_POS)
        accumulate(acc, step, left, idx)
        return carry

    lax.fori_loop(0, ELN // 1024, body, 0)
    unpack(out, acc)


def prolong_kernel(arrived, pos, epos, pi, own, low_out, high_out, table, w, values, terms, left, acc):
    fill_table(table, pair(arrived), ROWS, H_POS)
    fill_pi(w, pi)

    def gather_body(step, carry):
        values[:, lanes(step, 1024)] = gather_tile(table[...], pos[rows8(step), :], ROWS, H_POS)
        return carry

    lax.fori_loop(0, ELN // 1024, gather_body, 0)
    dims = (((1,), (1,)), ((), ()))
    rest = None
    for v in range(4):
        blocks = []
        for g in range(8):
            at = slice((4 * g + v) * LANE, (4 * g + v + 1) * LANE)
            blocks.append(
                jnp.concatenate([values[c * RHS : (c + 1) * RHS, at] for c in range(3)], axis=1)
            )
        high, low = split(jnp.concatenate(blocks, axis=0))
        y = (
            lax.dot_general(high, w[v, 0], dims, preferred_element_type=F32)
            + lax.dot_general(high, w[v, 1], dims, preferred_element_type=F32)
            + lax.dot_general(low, w[v, 0], dims, preferred_element_type=F32)
        )
        for g in range(8):
            t = 4 * g + v
            part = split(y[g * RHS : (g + 1) * RHS, : 2 * LANE])
            for k in (0, 1):
                terms[k, :, 2 * t * LANE : (2 * t + 2) * LANE] = part[k]
        rest = y[:, 2 * LANE :] if rest is None else rest + y[:, 2 * LANE :]
    for g in range(8):
        part = split(rest[g * RHS : (g + 1) * RHS])
        for k in (0, 1):
            terms[k, :, (EL + g) * LANE : (EL + g + 1) * LANE] = part[k]

    def body(step, carry):
        at = lanes(step, 1024)
        idx = epos[rows8(step), :]
        mask_rows(left, 0, (terms[0, :, at], terms[1, :, at]), high_bf(idx), H_EDGE)
        accumulate(acc, step, left, idx)
        return carry

    lax.fori_loop(0, E_TILES // 8, body, 0)
    for h in range(H_EDGE):
        if h < H_OWN:
            ref, at = own, h
        elif h < H_OWN + H_RIM:
            ref, at = low_out, h - H_OWN
        else:
            ref, at = high_out, h - H_OWN - H_RIM
        ref[:, at * WIDE : (at + 1) * WIDE] = acc[h * RHS : (h + 1) * RHS, :]


VM = pl.BlockSpec(memory_space=pltpu.VMEM)


def call(kernel, name, outs, scratch, *args):
    return pl.pallas_call(
        kernel,
        out_shape=[jax.ShapeDtypeStruct(s, t) for s, t in outs],
        in_specs=[VM] * len(args),
        out_specs=[VM] * len(outs),
        scratch_shapes=[pltpu.VMEM(s, t) for s, t in scratch],
        compiler_params=pltpu.CompilerParams(vmem_limit_bytes=40 << 20),
        name=name,
    )(*args)


def exchange(x):
    return lax.all_to_all(x, "dev", split_axis=0, concat_axis=0, tiled=True)


def per_device(
    residual_edges,
    pi_block,
    stiff_block,
    mass_block,
    permittivity,
    curl_coef,
    edge_map,
    local_map,
    node_owner,
    node_slot,
):
    axes = ("grp", "dev")
    size = lax.axis_size(axes)
    up = [(i, i + 1) for i in range(size - 1)]
    down = [(i + 1, i) for i in range(size - 1)]
    before = lax.ppermute(residual_edges[:, E_LOC - RIM_W :], axes, up)
    after = lax.ppermute(residual_edges[:, :RIM_W], axes, down)
    em = edge_map.T
    em = jnp.concatenate([em[:, :LANE], em[:, LANE:].reshape(8, LANE)], axis=0)
    lm = local_map.T.reshape(N_TILES, LANE)
    curl = curl_coef.reshape(1, EL)
    epos, pos, slot_rows, ev_own = call(
        prep_kernel,
        "index_prep",
        [((E_TILES, LANE), I32), ((N_TILES, LANE), I32), ((PEERS, CAP), F32), ((RHS, E_TILES * LANE), F32)],
        [
            ((H_OWN * RHS, 2 * WIDE), BF),
            ((U_LOC // LANE * PEERS, LANE), BF),
            ((U_LOC // LANE, LANE), I32),
            ((U_LOC // LANE, LANE), I32),
        ],
        residual_edges,
        em,
        lm,
        node_owner.reshape(U_LOC // LANE, LANE),
        node_slot.reshape(U_LOC // LANE, LANE),
    )
    (packed,) = call(
        restrict_kernel,
        "restrict",
        [((PEERS, SENT, CAP), F32)],
        [
            ((2 * H_RIM * RHS, 2 * WIDE), BF),
            ((RHS, E_TILES * LANE), F32),
            ((4, 2, 384, 384), BF),
            ((8, LANE), F32),
            ((8, ELN), F32),
            ((2, ROWS, ELN), BF),
            ((3, ELN), F32),
            ((H_POS * ROWS + 48, 2048), BF),
            ((H_POS * ROWS + 48, WIDE), F32),
        ],
        ev_own, before, after, epos, pos, slot_rows, pi_block, stiff_block, mass_block, permittivity, curl,
    )
    wanted, rhs, floor, slots = call(
        first_kernel,
        "first_iter",
        [
            ((PEERS, ROWS, CAP), F32),
            ((H_NODE, ROWS, WIDE), F32),
            ((H_NODE, 3, WIDE), F32),
            ((PEERS, CAP), I32),
        ],
        [
            ((H_NODE * ROWS, 2 * WIDE), BF),
            ((H_NODE * ROWS + 48, 2048), BF),
            ((H_NODE * ROWS + 48, WIDE), F32),
        ],
        exchange(packed),
    )
    (applied,) = call(
        apply_kernel,
        "operator",
        [((PEERS, ROWS, CAP), F32)],
        [
            ((H_POS * ROWS, 2 * WIDE), BF),
            ((2, LANE, 2 * LANE), BF),
            ((8, LANE), F32),
            ((8, ELN), F32),
            ((H_POS * ROWS, 2048), BF),
            ((H_POS * ROWS, WIDE), F32),
        ],
        exchange(wanted), pos, stiff_block, mass_block, permittivity, curl,
    )
    (wanted,) = call(
        second_kernel,
        "second_iter",
        [((PEERS, ROWS, CAP), F32)],
        [
            ((H_NODE * ROWS, 2 * WIDE), BF),
            ((H_NODE * ROWS, 2048), BF),
            ((H_NODE * ROWS, WIDE), F32),
        ],
        exchange(applied), rhs, floor, slots,
    )
    own, low_out, high_out = call(
        prolong_kernel,
        "prolong",
        [((RHS, E_LOC), F32), ((RHS, RIM_W), F32), ((RHS, RIM_W), F32)],
        [
            ((H_POS * ROWS, 2 * WIDE), BF),
            ((4, 2, 384, 384), BF),
            ((ROWS, ELN), F32),
            ((2, RHS, E_TILES * LANE), BF),
            ((H_EDGE * RHS, 2048), BF),
            ((H_EDGE * RHS, WIDE), F32),
        ],
        exchange(wanted), pos, epos, pi_block,
    )
    from_before = lax.ppermute(high_out, axes, up)
    from_after = lax.ppermute(low_out, axes, down)
    own = own.at[:, :RIM_W].add(from_before)
    return own.at[:, E_LOC - RIM_W :].add(from_after)


def solution(mesh):
    in_specs = (
        P(None, ("grp", "dev")),
        P(),
        P(),
        P(),
        P(None, ("grp", "dev")),
        P(("grp", "dev")),
        P(None, ("grp", "dev")),
        P(None, ("grp", "dev")),
        P(("grp", "dev")),
        P(("grp", "dev")),
    )
    out_specs = P(None, ("grp", "dev"))
    return jax.shard_map(
        per_device, mesh=mesh, in_specs=in_specs, out_specs=out_specs, check_vma=False
    )
```

time: 542 us -> 198 us (0.37)
  other arithmetic: 191 us -> 4.16 us
  local copies, waits for them, and re-layouts: 191 us -> 4.67 us
  blocking collectives: 50.5 us -> 114 us
  waiting for transfers between devices: 57.4 us -> 0.01 us
  Pallas kernels: 0 us -> 53.3 us
  starting transfers between devices: 40 us -> 21 us
    scatter-add x5 -> x2, other arithmetic: 150 us -> 3.48 us  [the longest x1 2.06 us: per_device(): own = own.at[:, :RIM_W].add(from_before)]
    gather x17 -> x0, local copies, waits for them, and re-layouts: 118 us -> none  [the longest x2 39.9 us: per_device(): edge_values = extended[:, local_edges]]
    all_to_all x2 -> x4, blocking collectives: 50.5 us -> 114 us  [exchange(): return lax.all_to_all(x, 'dev', split_axis=0, concat_axis=0, tiled=True)]
    pallas_call x0 -> x6, Pallas kernels: none -> 53.3 us  [call(): pl.pallas_call(kernel, out_shape=[jax.ShapeDtypeStruct(s, t) for s, t in...]
    all_to_all x3 -> x0, waiting for transfers between devices: 45.8 us -> none  [the longest x1 24.5 us: send_home(): lax.all_to_all(packed.reshape(rows, peer_count, capacity), 'dev', split_a...]
    scatter x4 -> x0, local copies, waits for them, and re-layouts: 29.4 us -> none  [the longest x2 12.5 us: send_home(): jnp.zeros((rows, peer_count * capacity), jnp.float32).at[:, buffer_pos]]
    all_to_all x3 -> x0, starting transfers between devices: 22.6 us -> none  [the longest x1 10.1 us: send_home(): lax.all_to_all(packed.reshape(rows, peer_count, capacity), 'dev', split_a...]
    add x5 -> x0, other arithmetic: 19.3 us -> none  [the longest x1 15.7 us: per_device(): sorted_owner * capacity + bucket_rank]
  transfers between devices with their start and end apart: 7 -> 4, of which waited for: 4 -> 0; matrix products, arithmetic and copies ran while one was open for 26% -> 2% of each run, Pallas kernels for 0% -> 3%
where the time goes in v1:
time: 198 us; the launch traced here: 197 us
  blocking collectives  114 us (58%)
  Pallas kernels  53.3 us (27%)
  starting transfers between devices  21 us (11%)
  local copies, waits for them, and re-layouts  4.67 us (2%)
  other arithmetic  4.16 us (2%)
    all_to_all x4, blocking collectives, exchange(): return lax.all_to_all(x, 'dev', split_axis=0, concat_axis=0, tiled=True)  114 us
    pallas_call x6, Pallas kernels, call(): pl.pallas_call(kernel, out_shape=[jax.ShapeDtypeStruct(s, t) for s, t in...  53.3 us
    ppermute x1, starting transfers between devices, per_device(): after = lax.ppermute(residual_edges[:, :RIM_W], axes, down)  7.38 us
    ppermute x1, starting transfers between devices, per_device(): from_after = lax.ppermute(low_out, axes, down)  6.14 us
  transfers between devices with their start and end apart: 4, of which 0 were waited for; matrix products, arithmetic and copies ran while one was open for 2% of the time, Pallas kernels for 3%

profile of v1, /device:TPU:16, one launch (start us, length us, event | category | flops | bytes accessed | tf_op | source)
XLA Modules:
  0.0 197.1 jit_solution(5382813313666533689)
XLA Ops:
  0.0 0.0 copy-start.1
  0.0 0.9 fusion.2
  0.9 3.8 %collective-permute-start = (f32[16,768]{1,0:T(8,128)S(1)}, f32[16,768]{1,0:T(8,128)S(1)}, u32[]{:S(2)}, u32[]{:S(2)}) collective-permute-start(f32[16,768]{1,0:T(8,128)S(1)} %get-tuple-element.52), channel_id=1, source_target_pairs={{0,1},{1,2},{2,3},{3,4},{4,5},{5,6},{6,7},{7,8},{8,9},{9,10},{10,1... | collective-permute-start | bytes 147464 | tf_op jit(solution)/shard_map/ppermute | solution.py:504
  4.7 7.4 %collective-permute-start.1 = (f32[16,768]{1,0:T(8,128)S(1)}, f32[16,768]{1,0:T(8,128)S(1)}, u32[]{:S(2)}, u32[]{:S(2)}) collective-permute-start(f32[16,768]{1,0:T(8,128)S(1)} %get-tuple-element.51), channel_id=1, source_target_pairs={{1,0},{2,1},{3,2},{4,3},{5,4},{6,5},{7,6},{8,7},{9,8},{10,9},{11,1... | collective-permute-start | bytes 147464 | tf_op jit(solution)/shard_map/ppermute | solution.py:505
  12.1 0.8 slice.57
  12.9 0.8 slice.56
  13.6 0.1 reshape.64
  13.7 0.0 copy-start.8
  13.7 0.7 copy-done.8
  14.5 0.1 copy.12
  14.5 0.0 copy-start.5
  14.5 0.0 copy-start.6
  14.6 0.1 reshape.65.lm
  14.6 0.0 copy-done.1
  14.6 0.6 copy-done.5
  15.2 0.0 copy-done.6
  15.3 0.0 copy-start
  15.3 0.0 copy-start.2
  15.3 0.0 copy-start.3
  15.3 5.8 %index_prep.1 = (s32[72,128]{1,0:T(8,128)S(1)}, s32[32,128]{1,0:T(8,128)S(1)}, f32[32,128]{1,0:T(8,128)S(1)}, f32[16,9216]{1,0:T(8,128)S(1)}) custom-call(f32[16,5376]{1,0:T(8,128)S(1)} %copy-done.1, s32[72,128]{1,0:T(8,128)S(1)} %pad_add_fusion.em, s32[32,128]{1,0:T(8,128)S(1)} %reshape.65.lm, s32[16,128]{1,0:T(8,128)S(1)} %bitcast.5, s32[16,128]{1,0:T(8,128)S(1)} %bitcast.6), custom_call_target="tpu_custom_call" | custom-call | tf_op jit(solution)/shard_map/index_prep/pallas_call | solution.py:473
  21.1 0.0 collective-permute-done.before
  21.1 0.0 collective-permute-done.1.after
  21.1 0.0 copy-start.4
  21.1 0.0 copy-start.7
  21.2 0.0 copy-done
  21.2 0.0 copy-done.2
  21.2 0.0 copy-done.3
  21.2 0.6 copy-done.4
  21.8 0.0 copy-done.7
  21.8 9.6 %restrict.1 = f32[32,52,128]{2,1,0:T(8,128)S(1)} custom-call(f32[16,9216]{1,0:T(8,128)S(1)} %get-tuple-element.40.ev_own, f32[16,768]{1,0:T(8,128)S(1)} %collective-permute-done.before, f32[16,768]{1,0:T(8,128)S(1)} %collective-permute-done.1.after, s32[72,128]{1,0:T(8,128)S(1)} %get-tuple-element.41.epos, s32[32,128]{1,0:T(8,128)S(1)} %get-tuple-element.42.pos, ...), custom_call_target="tpu_custom_call" | custom-call | tf_op jit(solution)/shard_map/restrict/pallas_call | solution.py:473
  31.4 32.5 %all_to_all.20.arrived = f32[32,52,128]{2,1,0:T(8,128)S(1)} all-to-all(f32[32,52,128]{2,1,0:T(8,128)S(1)} %restrict.1), channel_id=1, replica_groups=mesh['grp'=8,'dev'=32] {'dev'}, dimensions={0} | all-to-all | bytes 1703936 | tf_op jit(solution)/shard_map/all_to_all | solution.py:485
  64.0 5.0 %first_iter.1 = (f32[32,48,128]{2,1,0:T(8,128)S(1)}, f32[7,48,256]{2,1,0:T(8,128)S(1)}, f32[7,3,256]{2,1,0:T(4,128)S(1)}, s32[32,128]{1,0:T(8,128)S(1)}) custom-call(f32[32,52,128]{2,1,0:T(8,128)S(1)} %all_to_all.20.arrived), custom_call_target="tpu_custom_call" | custom-call | tf_op jit(solution)/shard_map/first_iter/pallas_call | solution.py:473
  69.0 27.3 %all_to_all.21.arrived = f32[32,48,128]{2,1,0:T(8,128)S(1)} all-to-all(f32[32,48,128]{2,1,0:T(8,128)S(1)} %get-tuple-element.44), channel_id=1, replica_groups=mesh['grp'=8,'dev'=32] {'dev'}, dimensions={0} | all-to-all | bytes 1572864 | tf_op jit(solution)/shard_map/all_to_all | solution.py:485
  96.4 15.2 %operator.1 = f32[32,48,128]{2,1,0:T(8,128)S(1)} custom-call(f32[32,48,128]{2,1,0:T(8,128)S(1)} %all_to_all.21.arrived, s32[32,128]{1,0:T(8,128)S(1)} %get-tuple-element.42.pos, f32[64,64]{1,0:T(8,128)S(1)} %copy-done.2, f32[64,64]{1,0:T(8,128)S(1)} %copy-done.3, f32[6,64]{1,0:T(8,128)S(1)} %copy-done.4, f32[1,64]{1,0:T(1,128)S(1)} %bitcast.8), custom_call_target="tpu_custom_call" | custom-call | tf_op jit(solution)/shard_map/operator/pallas_call | solution.py:473
  111.6 27.0 %all_to_all.22.arrived = f32[32,48,128]{2,1,0:T(8,128)S(1)} all-to-all(f32[32,48,128]{2,1,0:T(8,128)S(1)} %operator.1), channel_id=1, replica_groups=mesh['grp'=8,'dev'=32] {'dev'}, dimensions={0} | all-to-all | bytes 1572864 | tf_op jit(solution)/shard_map/all_to_all | solution.py:485
  138.6 4.8 %second_iter.1 = f32[32,48,128]{2,1,0:T(8,128)S(1)} custom-call(f32[32,48,128]{2,1,0:T(8,128)S(1)} %all_to_all.22.arrived, f32[7,48,256]{2,1,0:T(8,128)S(1)} %get-tuple-element.45.rhs, f32[7,3,256]{2,1,0:T(4,128)S(1)} %get-tuple-element.46.floor, s32[32,128]{1,0:T(8,128)S(1)} %get-tuple-element.47.slots), custom_call_target="tpu_custom_call" | custom-call | tf_op jit(solution)/shard_map/second_iter/pallas_call | solution.py:473
  143.4 26.9 %all_to_all.23.arrived = f32[32,48,128]{2,1,0:T(8,128)S(1)} all-to-all(f32[32,48,128]{2,1,0:T(8,128)S(1)} %second_iter.1), channel_id=1, replica_groups=mesh['grp'=8,'dev'=32] {'dev'}, dimensions={0} | all-to-all | bytes 1572864 | tf_op jit(solution)/shard_map/all_to_all | solution.py:485
  170.3 12.8 %prolong.1 = (f32[16,5376]{1,0:T(8,128)}, f32[16,768]{1,0:T(8,128)S(1)}, f32[16,768]{1,0:T(8,128)S(1)}) custom-call(f32[32,48,128]{2,1,0:T(8,128)S(1)} %all_to_all.23.arrived, s32[32,128]{1,0:T(8,128)S(1)} %get-tuple-element.42.pos, s32[72,128]{1,0:T(8,128)S(1)} %get-tuple-element.41.epos, f32[144,192]{1,0:T(8,128)S(1)} %copy-done), custom_call_target="tpu_custom_call" | custom-call | tf_op jit(solution)/shard_map/prolong/pallas_call | solution.py:473
  183.1 3.6 %collective-permute-start.2 = (f32[16,768]{1,0:T(8,128)S(1)}, f32[16,768]{1,0:T(8,128)S(1)}, u32[]{:S(2)}, u32[]{:S(2)}) collective-permute-start(f32[16,768]{1,0:T(8,128)S(1)} %get-tuple-element.49), channel_id=1, source_target_pairs={{0,1},{1,2},{2,3},{3,4},{4,5},{5,6},{6,7},{7,8},{8,9},{9,10},{10,1... | collective-permute-start | bytes 147464 | tf_op jit(solution)/shard_map/ppermute | solution.py:598
  186.8 0.7 compare_reduce_fusion
  187.4 6.1 %collective-permute-start.3 = (f32[16,768]{1,0:T(8,128)S(1)}, f32[16,768]{1,0:T(8,128)S(1)}, u32[]{:S(2)}, u32[]{:S(2)}) collective-permute-start(f32[16,768]{1,0:T(8,128)S(1)} %get-tuple-element.50), channel_id=1, source_target_pairs={{1,0},{2,1},{3,2},{4,3},{5,4},{6,5},{7,6},{8,7},{9,8},{10,9},{11,1... | collective-permute-start | bytes 147464 | tf_op jit(solution)/shard_map/ppermute | solution.py:599
  193.6 0.0 collective-permute-done.2
  193.6 2.1 %fusion = f32[16,5376]{1,0:T(8,128)} fusion(f32[16,5376]{1,0:T(8,128)} %get-tuple-element.48, f32[16,768]{1,0:T(8,128)S(1)} %collective-permute-done.2, pred[]{:T(512)} %compare_reduce_fusion), kind=kLoop, calls=%fused_computation.1 | loop fusion | flops 24576 | bytes 147968 | tf_op jit(solution)/shard_map/scatter-add | solution.py:600
  195.7 0.0 collective-permute-done.3
  195.7 1.4 fusion.1
  (1 shorter events, 0.0 us)
Async XLA Ops:
  0.0 14.6 %copy-start.1 = (f32[16,5376]{1,0:T(8,128)S(1)}, f32[16,5376]{1,0:T(8,128)}, u32[]{:S(2)}) copy-start(f32[16,5376]{1,0:T(8,128)} %res.1) | copy-start | bytes 1032196
  0.9 20.2 %collective-permute-start = (f32[16,768]{1,0:T(8,128)S(1)}, f32[16,768]{1,0:T(8,128)S(1)}, u32[]{:S(2)}, u32[]{:S(2)}) collective-permute-start(f32[16,768]{1,0:T(8,128)S(1)} %get-tuple-element.52), channel_id=1, source_target_pairs={{0,1},{1,2},{2,3},{3,4},{4,5},{5,6},{6,7},{7,8},{8,9},{9,10},{10,1... | collective-permute-start | bytes 147464 | tf_op jit(solution)/shard_map/ppermute | solution.py:504
  4.7 16.4 %collective-permute-start.1 = (f32[16,768]{1,0:T(8,128)S(1)}, f32[16,768]{1,0:T(8,128)S(1)}, u32[]{:S(2)}, u32[]{:S(2)}) collective-permute-start(f32[16,768]{1,0:T(8,128)S(1)} %get-tuple-element.51), channel_id=1, source_target_pairs={{1,0},{2,1},{3,2},{4,3},{5,4},{6,5},{7,6},{8,7},{9,8},{10,9},{11,1... | collective-permute-start | bytes 147464 | tf_op jit(solution)/shard_map/ppermute | solution.py:505
  13.7 0.8 copy-start.8
  14.5 0.7 copy-start.5
  14.5 0.7 copy-start.6
  15.3 5.9 %copy-start = (f32[144,192]{1,0:T(8,128)S(1)}, f32[144,192]{1,0:T(8,128)}, u32[]{:S(2)}) copy-start(f32[144,192]{1,0:T(8,128)} %pi.3) | copy-start | bytes 331780
  15.3 5.9 %copy-start.2 = (f32[64,64]{1,0:T(8,128)S(1)}, f32[64,64]{1,0:T(8,128)}, u32[]{:S(2)}) copy-start(f32[64,64]{1,0:T(8,128)} %stiff.3) | copy-start | bytes 49156
  15.3 5.9 %copy-start.3 = (f32[64,64]{1,0:T(8,128)S(1)}, f32[64,64]{1,0:T(8,128)}, u32[]{:S(2)}) copy-start(f32[64,64]{1,0:T(8,128)} %mass.3) | copy-start | bytes 49156
  21.1 0.7 copy-start.4
  21.1 0.7 copy-start.7
  183.1 10.4 %collective-permute-start.2 = (f32[16,768]{1,0:T(8,128)S(1)}, f32[16,768]{1,0:T(8,128)S(1)}, u32[]{:S(2)}, u32[]{:S(2)}) collective-permute-start(f32[16,768]{1,0:T(8,128)S(1)} %get-tuple-element.49), channel_id=1, source_target_pairs={{0,1},{1,2},{2,3},{3,4},{4,5},{5,6},{6,7},{7,8},{8,9},{9,10},{10,1... | collective-permute-start | bytes 147464 | tf_op jit(solution)/shard_map/ppermute | solution.py:598
  187.4 8.2 %collective-permute-start.3 = (f32[16,768]{1,0:T(8,128)S(1)}, f32[16,768]{1,0:T(8,128)S(1)}, u32[]{:S(2)}, u32[]{:S(2)}) collective-permute-start(f32[16,768]{1,0:T(8,128)S(1)} %get-tuple-element.50), channel_id=1, source_target_pairs={{1,0},{2,1},{3,2},{4,3},{5,4},{6,5},{7,6},{8,7},{9,8},{10,9},{11,1... | collective-permute-start | bytes 147464 | tf_op jit(solution)/shard_map/ppermute | solution.py:599

commit v2 on v1

v2 whole, which is shorter than its diff:
```python
import jax
import jax.numpy as jnp
from jax import lax
from jax.experimental import pallas as pl
from jax.experimental.pallas import tpu as pltpu
from jax.sharding import PartitionSpec as P

RHS = 16
ED = 144
NN = 64
EL = 64
E_LOC = 5376
RIM = 672
U_LOC = 2048
PEERS = 32
CAP = 128
ROWS = 3 * RHS
PAIR = 2 * ROWS
SENT = ROWS + 4
SLOTS = PEERS * CAP
ELN = NN * EL
LANE = 128
WIDE = 256
RIM_W = 768
H_OWN = E_LOC // WIDE
H_RIM = RIM_W // WIDE
H_EDGE = H_OWN + 2 * H_RIM
H_POS = U_LOC // WIDE
H_NODE = 7
E_TILES = 72
N_TILES = ELN // LANE
BF = jnp.bfloat16
F32 = jnp.float32
I32 = jnp.int32

CHEB_LOW = 0.3
CHEB_HIGH = 2.0


def cheb_factors():
    center = 0.5 * (CHEB_HIGH + CHEB_LOW)
    half_width = 0.5 * (CHEB_HIGH - CHEB_LOW)
    sigma_ratio = center / half_width
    rho_first = 1.0 / sigma_ratio
    rho_second = 1.0 / (2.0 * sigma_ratio - rho_first)
    return (1.0 / center, 1.0 + rho_second * rho_first, 2.0 * rho_second / half_width)


def split(x):
    high = x.astype(BF)
    return high, (x - high.astype(F32)).astype(BF)


def stack(x):
    return jnp.concatenate([x, x - x.astype(BF).astype(F32)], axis=0).astype(BF)


def iota(shape, dim):
    return lax.broadcasted_iota(I32, shape, dim)


def spread(index_rows, height):
    return jnp.concatenate(
        [jnp.broadcast_to(index_rows[i : i + 1], (height, LANE)) for i in range(index_rows.shape[0])],
        axis=1,
    )


def one_hot_low(index_rows):
    low = spread(index_rows & (WIDE - 1), WIDE)
    return jnp.where(low == iota(low.shape, 0), 1.0, 0.0).astype(BF)


def gather_tile(table, index_rows, rows, count):
    hot = one_hot_low(index_rows)
    found = jnp.dot(table, jnp.concatenate([hot, hot], axis=0), preferred_element_type=F32)
    high = spread(index_rows >> 8, rows)
    out = found[:rows]
    for h in range(1, count):
        out = jnp.where(high == h, found[h * rows : (h + 1) * rows], out)
    return out


def fill_table(table, source, rows, count):
    each = 1 if rows % 16 == 0 else 2
    for h in range(0, count, each):
        high, low = split(jnp.concatenate([source(h + i) for i in range(each)], axis=0))
        table[h * rows : (h + each) * rows, :WIDE] = high
        table[h * rows : (h + each) * rows, WIDE:] = low


def mask_rows(left, x, index_rows, first, count):
    rows, width = x.shape
    high = spread(index_rows >> 8, 1).astype(F32).astype(BF)
    high = jnp.broadcast_to(high, (rows, width))
    for h in range(count):
        left[h * rows : (h + 1) * rows, :] = jnp.where(high == float(first + h), x, jnp.zeros_like(x))


def mask_diag(left, base, diag, index_rows):
    width = diag[0].shape[1]
    here = spread(index_rows >> 8, 16) == iota((16, width), 0)
    for c in range(3):
        left[base + c * 32 : base + (c + 1) * 32, :] = stack(
            jnp.where(here, jnp.broadcast_to(diag[c], (16, width)), 0.0)
        )


def accumulate(acc, step, left, index_rows):
    part = lax.dot_general(
        left[...], one_hot_low(index_rows), (((1,), (1,)), ((), ())), preferred_element_type=F32
    )

    @pl.when(step == 0)
    def _():
        acc[...] = part

    @pl.when(step > 0)
    def _():
        acc[...] += part


def summed(acc, h, rows, at=slice(None)):
    base = h * 2 * rows
    return acc[base : base + rows, at] + acc[base + rows : base + 2 * rows, at]


def diag_summed(acc, base, c, h, at=slice(None)):
    row = base + c * 32 + h
    return acc[row : row + 1, at] + acc[row + 16 : row + 17, at]


def rows_of(step, count):
    return pl.ds(pl.multiple_of(step * count, count), count)


def lanes(step, width):
    return pl.ds(pl.multiple_of(step * width, width), width)


def prep_kernel(
    res, em, lm, owner, slot, epos_out, pos_out, slot_out, start_out, low_out, high_out, hots, rank_s, pos_s, tr
):
    low_out[...] = res[:, :RIM_W]
    high_out[...] = res[:, E_LOC - RIM_W :]
    tr[:, : ED - LANE] = em[:, LANE:]
    rest = [tr[pl.ds(i, 8, stride=8), :][:, : ED - LANE] for i in range(8)]
    m = jnp.concatenate([em[:, :LANE], jnp.concatenate(rest, axis=1)], axis=0)
    epos_out[...] = jnp.where(
        m < RIM,
        m + (E_LOC + RIM_W - RIM),
        jnp.where(m < RIM + E_LOC, m - RIM, m - (RIM + E_LOC) + E_LOC + RIM_W),
    )
    chunks = U_LOC // LANE
    for t in range(chunks):
        o = jnp.broadcast_to(owner[t : t + 1, :], (PEERS, LANE))
        hots[t * PEERS : (t + 1) * PEERS, :] = jnp.where(o == iota((PEERS, LANE), 0), 1.0, 0.0).astype(BF)
    before = jnp.where(iota((LANE, LANE), 0) < iota((LANE, LANE), 1), 1.0, 0.0)
    tri = jnp.concatenate([before, jnp.ones((LANE, LANE), F32)], axis=1).astype(BF)
    ranks = jnp.dot(hots[...], tri, preferred_element_type=F32)
    counts = ranks[:PEERS, LANE:]
    for t in range(1, chunks):
        counts = counts + ranks[t * PEERS : (t + 1) * PEERS, LANE:]
    below = jnp.where(iota((PEERS, PEERS), 1) < iota((PEERS, PEERS), 0), 1.0, 0.0).astype(BF)
    starts = jnp.dot(below, counts.astype(BF), preferred_element_type=F32)
    start_out[...] = starts.astype(I32)
    base = jnp.zeros((PEERS, LANE), F32)
    for t in range(chunks):
        hot = hots[t * PEERS : (t + 1) * PEERS, :].astype(F32)
        here = ranks[t * PEERS : (t + 1) * PEERS]
        rank = here[:, :LANE] + base
        base = base + here[:, LANE:]
        rank_s[t : t + 1, :] = jnp.sum(hot * rank, axis=0, keepdims=True).astype(I32)
        pos_s[t : t + 1, :] = jnp.sum(hot * (rank + starts), axis=0, keepdims=True).astype(I32)
    left = []
    right = []
    for t in range(chunks):
        hot = hots[t * PEERS : (t + 1) * PEERS, :].astype(F32)
        s = slot[t : t + 1, :] + 1
        left.append(
            jnp.concatenate([hot * (s >> 6).astype(F32), hot * (s & 63).astype(F32)], axis=0).astype(BF)
        )
        r = jnp.broadcast_to(rank_s[t : t + 1, :], (LANE, LANE))
        right.append(jnp.where(r == iota((LANE, LANE), 0), 1.0, 0.0).astype(BF))
    packed = lax.dot_general(
        jnp.concatenate(left, axis=1),
        jnp.concatenate(right, axis=1),
        (((1,), (1,)), ((), ())),
        preferred_element_type=F32,
    )
    slot_out[...] = packed[:PEERS] * 64.0 + packed[PEERS:] - 1.0
    tr[:, :NN] = lm[...].T
    idx = jnp.concatenate([tr[pl.ds(i, N_TILES, stride=2), :][:, :NN] for i in (0, 1)], axis=1)
    high, low = idx >> 7, idx & (LANE - 1)
    pos = jnp.zeros((N_TILES, LANE), I32)
    for t in range(chunks):
        row = jnp.broadcast_to(pos_s[t : t + 1, :], (N_TILES, LANE))
        pos = jnp.where(high == t, jnp.take_along_axis(row, low, axis=1), pos)
    pos_out[...] = pos


def own_edges_kernel(res, epos, ev_out, table):
    fill_table(table, lambda h: res[:, h * WIDE : (h + 1) * WIDE], RHS, H_OWN)

    def body(step, carry):
        ev_out[:, lanes(step, 1024)] = gather_tile(table[...], epos[rows_of(step, 8), :], RHS, H_OWN)
        return carry

    lax.fori_loop(0, E_TILES // 8, body, 0)


def fill_pi(w, pi):
    zero = jnp.zeros((384, 384), BF)
    for v in range(4):
        for k in (0, 1):
            w[v, k] = zero
    for c in range(3):
        part = split(pi[:, c * NN : (c + 1) * NN])
        for k in (0, 1):
            for e2 in (0, 1):
                cols = slice(c * LANE + e2 * NN, c * LANE + (e2 + 1) * NN)
                for v in range(4):
                    w[v, k, e2 * LANE : (e2 + 1) * LANE, cols] = part[k][:LANE]
                    at = 2 * LANE + (2 * v + e2) * 16
                    w[v, k, at : at + 16, cols] = part[k][LANE:]


def fill_coefs(coef, wide, perm, curl):
    coef[...] = jnp.zeros((8, LANE), F32)
    coef[0:6, 0:EL] = perm[...]
    coef[6:7, 0:EL] = curl[...]
    c = coef[...]
    second = jnp.where(iota((8, LANE), 1) >= NN, 1, 0)
    for t in range(N_TILES):
        wide[:, t * LANE : (t + 1) * LANE] = jnp.take_along_axis(c, second + 2 * t, axis=1)


NODE_STEP = 2048
NODE_ROWS = NODE_STEP // LANE
EDGE_STEP = 3072
EDGE_ROWS = EDGE_STEP // LANE


def from_acc(compact, acc):
    compact[:, U_LOC:] = jnp.zeros((compact.shape[0], 2 * LANE), F32)
    for h in range(H_POS):
        compact[0:ROWS, h * WIDE : (h + 1) * WIDE] = summed(acc, h, ROWS)


def expand(out, compact, starts, rows):
    lane = iota((rows, LANE), 1)
    for p in range(PEERS):
        start = starts[p, 0]
        shift = start & (LANE - 1)
        base = start - shift
        back = lax.rem(LANE - shift, LANE)
        one = pltpu.roll(compact[0:rows, lanes(base // LANE, LANE)], back, 1)
        two = pltpu.roll(compact[0:rows, lanes(base // LANE + 1, LANE)], back, 1)
        out[p] = jnp.where(lane < LANE - shift, one, two)[: out.shape[1]]


def shrink(compact, arrived, starts):
    lane = iota((ROWS, LANE), 1)
    for p in range(PEERS):
        start = starts[p, 0]
        shift = start & (LANE - 1)
        base = (start - shift) // LANE
        block = pltpu.roll(arrived[p], shift, 1)
        at = lanes(base, LANE)
        compact[:, at] = jnp.where(lane >= shift, block, compact[:, at])
        compact[:, lanes(base + 1, LANE)] = block


def restrict_kernel(
    ev_own, before, after, epos, pos, slots, pi, stiff, mass, perm, curl, starts,
    out, table, ev, w, coef, wide, xs, diag, left, acc, compact,
):
    def rim(h):
        ref = before if h < H_RIM else after
        at = h % H_RIM * WIDE
        return ref[:, at : at + WIDE]

    fill_table(table, rim, RHS, 2 * H_RIM)

    def rim_body(step, carry):
        idx = epos[rows_of(step, 8), :] - E_LOC
        found = gather_tile(table[...], idx, RHS, 2 * H_RIM)
        at = lanes(step, 1024)
        ev[:, at] = jnp.where(spread(idx, RHS) >= 0, found, ev_own[:, at])
        return carry

    lax.fori_loop(0, E_TILES // 8, rim_body, 0)
    fill_pi(w, pi)
    for v in range(4):
        blocks = []
        for g in range(8):
            t = 4 * g + v
            blocks.append(
                jnp.concatenate(
                    [ev[:, 2 * t * LANE : (2 * t + 2) * LANE], ev[:, (EL + g) * LANE : (EL + g + 1) * LANE]],
                    axis=1,
                )
            )
        high, low = split(jnp.concatenate(blocks, axis=0))
        y = (
            jnp.dot(high, w[v, 0], preferred_element_type=F32)
            + jnp.dot(high, w[v, 1], preferred_element_type=F32)
            + jnp.dot(low, w[v, 0], preferred_element_type=F32)
        )
        for g in range(8):
            t = 4 * g + v
            xs[:, t * LANE : (t + 1) * LANE] = stack(
                jnp.concatenate(
                    [y[g * RHS : (g + 1) * RHS, c * LANE : (c + 1) * LANE] for c in range(3)], axis=0
                )
            )
    fill_coefs(coef, wide, perm, curl)
    eye = iota((NN, NN), 0) == iota((NN, NN), 1)

    def diagonal(ref):
        d = jnp.sum(jnp.where(eye, ref[...], 0.0), axis=0, keepdims=True)
        return jnp.concatenate([d, d], axis=1)

    sd, md = diagonal(stiff), diagonal(mass)
    for t in range(N_TILES):
        at = slice(t * LANE, (t + 1) * LANE)
        diag[:, at] = wide[6:7, at] * sd + md * wide[0:3, at]

    def body(step, carry):
        at = lanes(step, NODE_STEP)
        idx = pos[rows_of(step, NODE_ROWS), :]
        mask_rows(left, xs[:, at], idx, 0, H_POS)
        mask_diag(left, H_POS * PAIR, [diag[c : c + 1, at] for c in range(3)], idx)
        accumulate(acc, step, left, idx)
        return carry

    lax.fori_loop(0, ELN // NODE_STEP, body, 0)
    from_acc(compact, acc)
    for h in range(H_POS):
        for c in range(3):
            compact[ROWS + c : ROWS + c + 1, h * WIDE : (h + 1) * WIDE] = diag_summed(
                acc, H_POS * PAIR, c, h
            )
    expand(out, compact, starts, SENT + 4)
    for p in range(PEERS):
        out[p, SENT - 1 : SENT, :] = slots[p : p + 1, :]


def collect(arrived, slots, left, acc, with_diag):
    def body(step, carry):
        idx = slots[rows_of(step, NODE_ROWS), :]
        block = arrived[rows_of(step, NODE_ROWS)]
        x = jnp.concatenate([block[i, 0:ROWS] for i in range(NODE_ROWS)], axis=1)
        mask_rows(left, stack(x), idx, 0, H_NODE)
        if with_diag:
            diag = [
                jnp.concatenate([block[i, ROWS + c : ROWS + c + 1] for i in range(NODE_ROWS)], axis=1)
                for c in range(3)
            ]
            mask_diag(left, H_NODE * PAIR, diag, idx)
        accumulate(acc, step, left, idx)
        return carry

    lax.fori_loop(0, PEERS // NODE_ROWS, body, 0)


def serve(out, table, slots):
    def body(step, carry):
        found = gather_tile(table[...], slots[rows_of(step, 8), :], ROWS, H_NODE)
        for i in range(8):
            out[step * 8 + i] = found[:, i * LANE : (i + 1) * LANE]
        return carry

    lax.fori_loop(0, PEERS // 8, body, 0)


def first_values(rhs, floor):
    first = cheb_factors()[0]

    def value(h):
        if h >= H_NODE:
            return jnp.zeros((ROWS, WIDE), F32)
        return jnp.concatenate(
            [
                first * rhs[h, c * RHS : (c + 1) * RHS, :] / floor[h, c : c + 1, :]
                for c in range(3)
            ],
            axis=0,
        )

    return value


def first_kernel(arrived, out, rhs_out, floor_out, slot_out, table, left, acc):
    for p in range(PEERS):
        slot_out[p : p + 1, :] = arrived[p, SENT - 1 : SENT, :].astype(I32)
    collect(arrived, slot_out, left, acc, True)
    for h in range(H_NODE):
        rhs_out[h] = summed(acc, h, ROWS)
        for c in range(3):
            floor_out[h, c : c + 1, :] = jnp.maximum(diag_summed(acc, H_NODE * PAIR, c, h), 1.0)
    fill_table(table, first_values(rhs_out, floor_out), ROWS, H_NODE + 1)
    serve(out, table, slot_out)


def second_kernel(arrived, rhs, floor, slots, out, table, left, acc):
    first, keep, step = cheb_factors()
    collect(arrived, slots, left, acc, False)

    def value(h):
        if h >= H_NODE:
            return jnp.zeros((ROWS, WIDE), F32)
        applied = summed(acc, h, ROWS)
        parts = []
        for c in range(3):
            at = slice(c * RHS, (c + 1) * RHS)
            part = rhs[h, at, :]
            low = floor[h, c : c + 1, :]
            parts.append(keep * (first * part / low) + step * (part - applied[at]) / low)
        return jnp.concatenate(parts, axis=0)

    fill_table(table, value, ROWS, H_NODE + 1)
    serve(out, table, slots)


def touched_table(table, compact, arrived, starts):
    shrink(compact, arrived, starts)
    fill_table(table, lambda h: compact[:, h * WIDE : (h + 1) * WIDE], ROWS, H_POS)


def apply_kernel(
    arrived, pos, stiff, mass, perm, curl, starts, out, table, op, coef, wide, xs, left, acc, compact
):
    touched_table(table, compact, arrived, starts)
    fill_coefs(coef, wide, perm, curl)
    op[...] = jnp.zeros((2, LANE, 2 * LANE), BF)
    for m, ref in enumerate((stiff, mass)):
        part = split(ref[...].T)
        for k in (0, 1):
            for e2 in (0, 1):
                at = slice(m * LANE + e2 * NN, m * LANE + (e2 + 1) * NN)
                op[k, e2 * NN : (e2 + 1) * NN, at] = part[k]

    def element_body(step, carry):
        values = gather_tile(table[...], pos[rows_of(step, 8), :], ROWS, H_POS)
        high, low = split(
            jnp.concatenate([values[:, i * LANE : (i + 1) * LANE] for i in range(8)], axis=0)
        )
        y = (
            jnp.dot(high, op[0], preferred_element_type=F32)
            + jnp.dot(high, op[1], preferred_element_type=F32)
            + jnp.dot(low, op[0], preferred_element_type=F32)
        )
        cols = wide[:, lanes(step, 1024)]
        tensor = ((0, 3, 4), (3, 1, 5), (4, 5, 2))
        tiles = []
        for i in range(8):
            k = cols[:, i * LANE : (i + 1) * LANE]
            rows = [slice(i * ROWS + c * RHS, i * ROWS + (c + 1) * RHS) for c in range(3)]
            s = [y[r, :LANE] for r in rows]
            m = [y[r, LANE:] for r in rows]
            tiles.append(
                jnp.concatenate(
                    [
                        k[6:7] * s[c]
                        + k[tensor[c][0]][None] * m[0]
                        + k[tensor[c][1]][None] * m[1]
                        + k[tensor[c][2]][None] * m[2]
                        for c in range(3)
                    ],
                    axis=0,
                )
            )
        xs[:, lanes(step, 1024)] = stack(jnp.concatenate(tiles, axis=1))
        return carry

    lax.fori_loop(0, ELN // 1024, element_body, 0)

    def body(step, carry):
        idx = pos[rows_of(step, NODE_ROWS), :]
        mask_rows(left, xs[:, lanes(step, NODE_STEP)], idx, 0, H_POS)
        accumulate(acc, step, left, idx)
        return carry

    lax.fori_loop(0, ELN // NODE_STEP, body, 0)
    from_acc(compact, acc)
    expand(out, compact, starts, ROWS)


def edge_terms(arrived, pos, pi, starts, terms, table, w, values, compact):
    touched_table(table, compact, arrived, starts)
    fill_pi(w, pi)

    def gather_body(step, carry):
        values[:, lanes(step, 1024)] = gather_tile(table[...], pos[rows_of(step, 8), :], ROWS, H_POS)
        return carry

    lax.fori_loop(0, ELN // 1024, gather_body, 0)
    dims = (((1,), (1,)), ((), ()))
    rest = None
    for v in range(4):
        blocks = []
        for g in range(8):
            at = slice((4 * g + v) * LANE, (4 * g + v + 1) * LANE)
            blocks.append(
                jnp.concatenate([values[c * RHS : (c + 1) * RHS, at] for c in range(3)], axis=1)
            )
        high, low = split(jnp.concatenate(blocks, axis=0))
        y = (
            lax.dot_general(high, w[v, 0], dims, preferred_element_type=F32)
            + lax.dot_general(high, w[v, 1], dims, preferred_element_type=F32)
            + lax.dot_general(low, w[v, 0], dims, preferred_element_type=F32)
        )
        for g in range(8):
            t = 4 * g + v
            terms[:, 2 * t * LANE : (2 * t + 2) * LANE] = stack(y[g * RHS : (g + 1) * RHS, : 2 * LANE])
        rest = y[:, 2 * LANE :] if rest is None else rest + y[:, 2 * LANE :]
    for g in range(8):
        terms[:, (EL + g) * LANE : (EL + g + 1) * LANE] = stack(rest[g * RHS : (g + 1) * RHS])


def edge_scatter(terms, epos, left, acc, first, count):
    def body(step, carry):
        idx = epos[rows_of(step, EDGE_ROWS), :]
        mask_rows(left, terms[:, lanes(step, EDGE_STEP)], idx, first, count)
        accumulate(acc, step, left, idx)
        return carry

    lax.fori_loop(0, E_TILES // EDGE_ROWS, body, 0)


def prolong_rim_kernel(
    arrived, pos, epos, pi, starts, terms, low_out, high_out, table, w, values, compact, left, acc
):
    edge_terms(arrived, pos, pi, starts, terms, table, w, values, compact)
    edge_scatter(terms, epos, left, acc, H_OWN, 2 * H_RIM)
    for h in range(H_RIM):
        at = slice(h * WIDE, (h + 1) * WIDE)
        low_out[:, at] = summed(acc, h, RHS)
        high_out[:, at] = summed(acc, H_RIM + h, RHS)


def prolong_own_kernel(terms, epos, own, left, acc):
    edge_scatter(terms, epos, left, acc, 0, H_OWN)
    for h in range(H_OWN):
        own[:, h * WIDE : (h + 1) * WIDE] = summed(acc, h, RHS)


def finish_kernel(own, before, after, out):
    out[...] = own[...]
    out[:, :RIM_W] += before[...]
    out[:, E_LOC - RIM_W :] += after[...]


VM = pl.BlockSpec(memory_space=pltpu.VMEM)


SM = pl.BlockSpec(memory_space=pltpu.SMEM)


def call(kernel, name, micros, outs, scratch, *args, scalars=0):
    return pl.pallas_call(
        kernel,
        out_shape=[jax.ShapeDtypeStruct(s, t) for s, t in outs],
        in_specs=[VM] * (len(args) - scalars) + [SM] * scalars,
        out_specs=[VM] * len(outs),
        scratch_shapes=[pltpu.VMEM(s, t) for s, t in scratch],
        compiler_params=pltpu.CompilerParams(vmem_limit_bytes=40 << 20),
        cost_estimate=pl.CostEstimate(flops=0, bytes_accessed=micros * 3600000, transcendentals=0),
        name=name,
    )(*args)


def exchange(x):
    return lax.all_to_all(x, "dev", split_axis=0, concat_axis=0, tiled=True)


def per_device(
    residual_edges,
    pi_block,
    stiff_block,
    mass_block,
    permittivity,
    curl_coef,
    edge_map,
    local_map,
    node_owner,
    node_slot,
):
    axes = ("grp", "dev")
    size = lax.axis_size(axes)
    up = [(i, i + 1) for i in range(size - 1)]
    down = [(i + 1, i) for i in range(size - 1)]
    curl = curl_coef.reshape(1, EL)
    chunks = U_LOC // LANE
    rim = ((RHS, RIM_W), F32)
    epos, pos, slot_rows, starts, low, high = call(
        prep_kernel,
        "index_prep",
        2,
        [
            ((E_TILES, LANE), I32),
            ((N_TILES, LANE), I32),
            ((PEERS, CAP), F32),
            ((PEERS, LANE), I32),
            rim,
            rim,
        ],
        [((chunks * PEERS, LANE), BF), ((chunks, LANE), I32), ((chunks, LANE), I32), ((EL, LANE), I32)],
        residual_edges,
        edge_map.T,
        local_map,
        node_owner.reshape(chunks, LANE),
        node_slot.reshape(chunks, LANE),
    )
    before = lax.ppermute(high, axes, up)
    after = lax.ppermute(low, axes, down)
    edge_rows = ((RHS, E_TILES * LANE), F32)
    (ev_own,) = call(
        own_edges_kernel, "own_edges", 4, [edge_rows], [((H_OWN * RHS, 2 * WIDE), BF)], residual_edges, epos
    )
    pi_scratch = ((4, 2, 384, 384), BF)
    coefs = [((8, LANE), F32), ((8, ELN), F32)]
    served = ((PEERS, ROWS, CAP), F32)
    compact = ((ROWS, U_LOC + 2 * LANE), F32)
    (packed,) = call(
        restrict_kernel,
        "restrict",
        6,
        [((PEERS, SENT, CAP), F32)],
        [
            ((2 * H_RIM * RHS, 2 * WIDE), BF),
            edge_rows,
            pi_scratch,
            *coefs,
            ((PAIR, ELN), BF),
            ((3, ELN), F32),
            ((H_POS * PAIR + 96, NODE_STEP), BF),
            ((H_POS * PAIR + 96, WIDE), F32),
            ((SENT + 4, U_LOC + 2 * LANE), F32),
        ],
        ev_own, before, after, epos, pos, slot_rows, pi_block, stiff_block, mass_block, permittivity, curl, starts,
        scalars=1,
    )
    table = (((H_NODE + 1) * ROWS, 2 * WIDE), BF)
    wanted, rhs, floor, slots = call(
        first_kernel,
        "first_iter",
        5,
        [served, ((H_NODE, ROWS, WIDE), F32), ((H_NODE, 3, WIDE), F32), ((PEERS, CAP), I32)],
        [table, ((H_NODE * PAIR + 96, NODE_STEP), BF), ((H_NODE * PAIR + 96, WIDE), F32)],
        exchange(packed),
    )
    position_table = ((H_POS * ROWS, 2 * WIDE), BF)
    (applied,) = call(
        apply_kernel,
        "operator",
        8,
        [served],
        [
            position_table,
            ((2, LANE, 2 * LANE), BF),
            *coefs,
            ((PAIR, ELN), BF),
            ((H_POS * PAIR, NODE_STEP), BF),
            ((H_POS * PAIR, WIDE), F32),
            compact,
        ],
        exchange(wanted), pos, stiff_block, mass_block, permittivity, curl, starts,
        scalars=1,
    )
    (wanted,) = call(
        second_kernel,
        "second_iter",
        5,
        [served],
        [table, ((H_NODE * PAIR, NODE_STEP), BF), ((H_NODE * PAIR, WIDE), F32)],
        exchange(applied), rhs, floor, slots,
    )
    terms, low, high = call(
        prolong_rim_kernel,
        "prolong_rim",
        6,
        [((2 * RHS, E_TILES * LANE), BF), rim, rim],
        [
            position_table,
            pi_scratch,
            ((ROWS, ELN), F32),
            compact,
            ((2 * H_RIM * 2 * RHS, EDGE_STEP), BF),
            ((2 * H_RIM * 2 * RHS, WIDE), F32),
        ],
        exchange(wanted), pos, epos, pi_block, starts,
        scalars=1,
    )
    from_before = lax.ppermute(high, axes, up)
    from_after = lax.ppermute(low, axes, down)
    (own,) = call(
        prolong_own_kernel,
        "prolong_own",
        5,
        [((RHS, E_LOC), F32)],
        [((H_OWN * 2 * RHS, EDGE_STEP), BF), ((H_OWN * 2 * RHS, WIDE), F32)],
        terms, epos,
    )
    (out,) = call(finish_kernel, "finish", 1, [((RHS, E_LOC), F32)], [], own, from_before, from_after)
    return out


def solution(mesh):
    in_specs = (
        P(None, ("grp", "dev")),
        P(),
        P(),
        P(),
        P(None, ("grp", "dev")),
        P(("grp", "dev")),
        P(None, ("grp", "dev")),
        P(None, ("grp", "dev")),
        P(("grp", "dev")),
        P(("grp", "dev")),
    )
    out_specs = P(None, ("grp", "dev"))
    return jax.shard_map(
        per_device, mesh=mesh, in_specs=in_specs, out_specs=out_specs, check_vma=False
    )
```

time: 198 us -> 185 us (0.934)
  Pallas kernels: 53.3 us -> 44.4 us
  other arithmetic: 4.16 us -> 0 us
    pallas_call x6 -> x9, Pallas kernels: 53.3 us -> 44.4 us  [call(): pl.pallas_call(kernel, out_shape=[jax.ShapeDtypeStruct(s, t) for s, t in...]
    scatter-add x2 -> x0, other arithmetic: 3.48 us -> none  [the longest x1 2.06 us: per_device(): own = own.at[:, :RIM_W].add(from_before)]
    unnamed x18 -> x20, local copies, waits for them, and re-layouts: 2.05 us -> 4.61 us
    slice x3 -> x0, local copies, waits for them, and re-layouts: 2.4 us -> none  [the longest x2 1.52 us: per_device(): em = jnp.concatenate([em[:, :LANE], em[:, LANE:].reshape(8, LANE)], axis=0)]
  transfers between devices with their start and end apart: 4 -> 4, of which waited for: 0 -> 0; matrix products, arithmetic and copies ran while one was open for 2% -> 0% of each run, Pallas kernels for 3% -> 5%
where the time goes in v2:
time: 185 us; the launch traced here: 184 us
  blocking collectives  114 us (62%)
  Pallas kernels  44.4 us (24%)
  starting transfers between devices  21 us (11%)
  local copies, waits for them, and re-layouts  4.61 us (2%)
    all_to_all x4, blocking collectives, exchange(): return lax.all_to_all(x, 'dev', split_axis=0, concat_axis=0, tiled=True)  114 us
    pallas_call x9, Pallas kernels, call(): pl.pallas_call(kernel, out_shape=[jax.ShapeDtypeStruct(s, t) for s, t in...  44.4 us
    ppermute x1, starting transfers between devices, per_device(): after = lax.ppermute(low, axes, down)  7.38 us
    ppermute x1, starting transfers between devices, per_device(): from_after = lax.ppermute(low, axes, down)  6.15 us
    unnamed x20, local copies, waits for them, and re-layouts  4.61 us
    ppermute x1, starting transfers between devices, per_device(): before = lax.ppermute(high, axes, up)  3.83 us
  transfers between devices with their start and end apart: 4, of which 0 were waited for; matrix products, arithmetic and copies ran while one was open for 0% of the time, Pallas kernels for 5%

profile of v2, /device:TPU:16, one launch (start us, length us, event | category | flops | bytes accessed | tf_op | source)
XLA Modules:
  0.0 184.1 jit_solution(17683874407312494460)
XLA Ops:
  0.0 0.0 copy-start
  0.0 1.0 copy-done
  1.0 0.0 copy-start.4
  1.0 0.8 copy-done.4
  1.8 0.0 copy-start.5
  1.8 0.8 copy-done.5
  2.6 0.0 copy-start.7
  2.6 0.7 copy-done.7
  3.3 0.0 copy-start.8
  3.3 0.7 copy-done.8
  4.0 0.7 index_prep.1
  4.6 3.8 %collective-permute-start = (f32[16,768]{1,0:T(8,128)S(1)}, f32[16,768]{1,0:T(8,128)S(1)}, u32[]{:S(2)}, u32[]{:S(2)}) collective-permute-start(f32[16,768]{1,0:T(8,128)S(1)} %get-tuple-element.19), channel_id=1, source_target_pairs={{0,1},{1,2},{2,3},{3,4},{4,5},{5,6},{6,7},{7,8},{8,9},{9,10},{10,1... | collective-permute-start | bytes 147464 | tf_op jit(solution)/shard_map/ppermute | solution.py:616
  8.5 7.4 %collective-permute-start.1 = (f32[16,768]{1,0:T(8,128)S(1)}, f32[16,768]{1,0:T(8,128)S(1)}, u32[]{:S(2)}, u32[]{:S(2)}) collective-permute-start(f32[16,768]{1,0:T(8,128)S(1)} %get-tuple-element.20), channel_id=1, source_target_pairs={{1,0},{2,1},{3,2},{4,3},{5,4},{6,5},{7,6},{8,7},{9,8},{10,9},{11,1... | collective-permute-start | bytes 147464 | tf_op jit(solution)/shard_map/ppermute | solution.py:617
  15.8 0.0 copy-start.1
  15.9 0.0 copy-start.2
  15.9 0.0 copy-start.3
  15.9 5.1 %own_edges.1.ev_own = f32[16,9216]{1,0:T(8,128)S(1)} custom-call(f32[16,5376]{1,0:T(8,128)S(1)} %copy-done, s32[72,128]{1,0:T(8,128)S(1)} %get-tuple-element.18.epos), custom_call_target="tpu_custom_call" | custom-call | bytes 14400000 | tf_op jit(solution)/shard_map/own_edges/pallas_call | solution.py:562
  21.0 0.0 copy-start.6
  21.1 0.0 collective-permute-done.before
  21.1 0.0 collective-permute-done.1.after
  21.1 0.0 copy-start.9
  21.1 0.0 copy-done.1
  21.1 0.0 copy-done.2
  21.1 0.0 copy-done.3
  21.1 0.6 copy-done.6
  21.7 0.0 copy-done.9
  21.7 8.8 %restrict.1 = f32[32,52,128]{2,1,0:T(8,128)S(1)} custom-call(f32[16,9216]{1,0:T(8,128)S(1)} %own_edges.1.ev_own, f32[16,768]{1,0:T(8,128)S(1)} %collective-permute-done.before, f32[16,768]{1,0:T(8,128)S(1)} %collective-permute-done.1.after, s32[72,128]{1,0:T(8,128)S(1)} %get-tuple-element.18.epos, s32[32,128]{1,0:T(8,128)S(1)} %get-tuple-element.21.pos, ...), custom_call_target="tpu_custom_call" | custom-call | bytes 21600000 | tf_op jit(solution)/shard_map/restrict/pallas_call | solution.py:562
  30.5 32.5 %all_to_all.20.arrived = f32[32,52,128]{2,1,0:T(8,128)S(1)} all-to-all(f32[32,52,128]{2,1,0:T(8,128)S(1)} %restrict.1), channel_id=1, replica_groups=mesh['grp'=8,'dev'=32] {'dev'}, dimensions={0} | all-to-all | bytes 1703936 | tf_op jit(solution)/shard_map/all_to_all | solution.py:575
  63.0 4.8 %first_iter.1 = (f32[32,48,128]{2,1,0:T(8,128)S(1)}, f32[7,48,256]{2,1,0:T(8,128)S(1)}, f32[7,3,256]{2,1,0:T(4,128)S(1)}, s32[32,128]{1,0:T(8,128)S(1)}) custom-call(f32[32,52,128]{2,1,0:T(8,128)S(1)} %all_to_all.20.arrived), custom_call_target="tpu_custom_call" | custom-call | bytes 18000000 | tf_op jit(solution)/shard_map/first_iter/pallas_call | solution.py:562
  67.8 27.4 %all_to_all.21.arrived = f32[32,48,128]{2,1,0:T(8,128)S(1)} all-to-all(f32[32,48,128]{2,1,0:T(8,128)S(1)} %get-tuple-element.24), channel_id=1, replica_groups=mesh['grp'=8,'dev'=32] {'dev'}, dimensions={0} | all-to-all | bytes 1572864 | tf_op jit(solution)/shard_map/all_to_all | solution.py:575
  95.2 8.3 %operator.1 = f32[32,48,128]{2,1,0:T(8,128)S(1)} custom-call(f32[32,48,128]{2,1,0:T(8,128)S(1)} %all_to_all.21.arrived, s32[32,128]{1,0:T(8,128)S(1)} %get-tuple-element.21.pos, f32[64,64]{1,0:T(8,128)S(1)} %copy-done.2, f32[64,64]{1,0:T(8,128)S(1)} %copy-done.3, f32[6,64]{1,0:T(8,128)S(1)} %copy-done.6, f32[1,64]{1,0:T(1,128)S(1)} %bitcast.8, ...), custom_call_target="tpu_custom_call" | custom-call | bytes 28800000 | tf_op jit(solution)/shard_map/operator/pallas_call | solution.py:562
  103.5 27.0 %all_to_all.22.arrived = f32[32,48,128]{2,1,0:T(8,128)S(1)} all-to-all(f32[32,48,128]{2,1,0:T(8,128)S(1)} %operator.1), channel_id=1, replica_groups=mesh['grp'=8,'dev'=32] {'dev'}, dimensions={0} | all-to-all | bytes 1572864 | tf_op jit(solution)/shard_map/all_to_all | solution.py:575
  130.5 4.6 %second_iter.1 = f32[32,48,128]{2,1,0:T(8,128)S(1)} custom-call(f32[32,48,128]{2,1,0:T(8,128)S(1)} %all_to_all.22.arrived, f32[7,48,256]{2,1,0:T(8,128)S(1)} %get-tuple-element.25.rhs, f32[7,3,256]{2,1,0:T(4,128)S(1)} %get-tuple-element.26.floor, s32[32,128]{1,0:T(8,128)S(1)} %get-tuple-element.27.slots), custom_call_target="tpu_custom_call" | custom-call | bytes 18000000 | tf_op jit(solution)/shard_map/second_iter/pallas_call | solution.py:562
  135.1 26.9 %all_to_all.23.arrived = f32[32,48,128]{2,1,0:T(8,128)S(1)} all-to-all(f32[32,48,128]{2,1,0:T(8,128)S(1)} %second_iter.1), channel_id=1, replica_groups=mesh['grp'=8,'dev'=32] {'dev'}, dimensions={0} | all-to-all | bytes 1572864 | tf_op jit(solution)/shard_map/all_to_all | solution.py:575
  162.1 7.4 %prolong_rim.1 = (bf16[32,9216]{1,0:T(8,128)(2,1)S(1)}, f32[16,768]{1,0:T(8,128)S(1)}, f32[16,768]{1,0:T(8,128)S(1)}) custom-call(f32[32,48,128]{2,1,0:T(8,128)S(1)} %all_to_all.23.arrived, s32[32,128]{1,0:T(8,128)S(1)} %get-tuple-element.21.pos, s32[72,128]{1,0:T(8,128)S(1)} %get-tuple-element.18.epos, f32[144,192]{1,0:T(8,128)S(1)} %copy-done.1, ...), custom_call_target="tpu_custom_call" | custom-call | bytes 21600000 | tf_op jit(solution)/shard_map/prolong_rim/pallas_call | solution.py:562
  169.5 3.6 %collective-permute-start.2 = (f32[16,768]{1,0:T(8,128)S(1)}, f32[16,768]{1,0:T(8,128)S(1)}, u32[]{:S(2)}, u32[]{:S(2)}) collective-permute-start(f32[16,768]{1,0:T(8,128)S(1)} %get-tuple-element.29), channel_id=1, source_target_pairs={{0,1},{1,2},{2,3},{3,4},{4,5},{5,6},{6,7},{7,8},{8,9},{9,10},{10,1... | collective-permute-start | bytes 147464 | tf_op jit(solution)/shard_map/ppermute | solution.py:696
  173.1 6.2 %collective-permute-start.3 = (f32[16,768]{1,0:T(8,128)S(1)}, f32[16,768]{1,0:T(8,128)S(1)}, u32[]{:S(2)}, u32[]{:S(2)}) collective-permute-start(f32[16,768]{1,0:T(8,128)S(1)} %get-tuple-element.30), channel_id=1, source_target_pairs={{1,0},{2,1},{3,2},{4,3},{5,4},{6,5},{7,6},{8,7},{9,8},{10,9},{11,1... | collective-permute-start | bytes 147464 | tf_op jit(solution)/shard_map/ppermute | solution.py:697
  179.3 4.0 %prolong_own.1.own = f32[16,5376]{1,0:T(8,128)S(1)} custom-call(bf16[32,9216]{1,0:T(8,128)(2,1)S(1)} %get-tuple-element.28.terms, s32[72,128]{1,0:T(8,128)S(1)} %get-tuple-element.18.epos), custom_call_target="tpu_custom_call" | custom-call | bytes 18000000 | tf_op jit(solution)/shard_map/prolong_own/pallas_call | solution.py:562
  183.3 0.0 collective-permute-done.2.before
  183.3 0.0 collective-permute-done.3.after
  183.3 0.8 finish.1
Async XLA Ops:
  0.0 1.0 copy-start
  1.0 0.8 copy-start.4
  1.8 0.8 copy-start.5
  2.6 0.7 copy-start.7
  3.3 0.7 copy-start.8
  4.6 16.4 %collective-permute-start = (f32[16,768]{1,0:T(8,128)S(1)}, f32[16,768]{1,0:T(8,128)S(1)}, u32[]{:S(2)}, u32[]{:S(2)}) collective-permute-start(f32[16,768]{1,0:T(8,128)S(1)} %get-tuple-element.19), channel_id=1, source_target_pairs={{0,1},{1,2},{2,3},{3,4},{4,5},{5,6},{6,7},{7,8},{8,9},{9,10},{10,1... | collective-permute-start | bytes 147464 | tf_op jit(solution)/shard_map/ppermute | solution.py:616
  8.5 12.6 %collective-permute-start.1 = (f32[16,768]{1,0:T(8,128)S(1)}, f32[16,768]{1,0:T(8,128)S(1)}, u32[]{:S(2)}, u32[]{:S(2)}) collective-permute-start(f32[16,768]{1,0:T(8,128)S(1)} %get-tuple-element.20), channel_id=1, source_target_pairs={{1,0},{2,1},{3,2},{4,3},{5,4},{6,5},{7,6},{8,7},{9,8},{10,9},{11,1... | collective-permute-start | bytes 147464 | tf_op jit(solution)/shard_map/ppermute | solution.py:617
  15.8 5.2 %copy-start.1 = (f32[144,192]{1,0:T(8,128)S(1)}, f32[144,192]{1,0:T(8,128)}, u32[]{:S(2)}) copy-start(f32[144,192]{1,0:T(8,128)} %pi.3) | copy-start | bytes 331780
  15.9 5.2 %copy-start.2 = (f32[64,64]{1,0:T(8,128)S(1)}, f32[64,64]{1,0:T(8,128)}, u32[]{:S(2)}) copy-start(f32[64,64]{1,0:T(8,128)} %stiff.3) | copy-start | bytes 49156
  15.9 5.2 %copy-start.3 = (f32[64,64]{1,0:T(8,128)S(1)}, f32[64,64]{1,0:T(8,128)}, u32[]{:S(2)}) copy-start(f32[64,64]{1,0:T(8,128)} %mass.3) | copy-start | bytes 49156
  21.0 0.7 copy-start.6
  21.1 0.7 copy-start.9
  169.5 13.8 %collective-permute-start.2 = (f32[16,768]{1,0:T(8,128)S(1)}, f32[16,768]{1,0:T(8,128)S(1)}, u32[]{:S(2)}, u32[]{:S(2)}) collective-permute-start(f32[16,768]{1,0:T(8,128)S(1)} %get-tuple-element.29), channel_id=1, source_target_pairs={{0,1},{1,2},{2,3},{3,4},{4,5},{5,6},{6,7},{7,8},{8,9},{9,10},{10,1... | collective-permute-start | bytes 147464 | tf_op jit(solution)/shard_map/ppermute | solution.py:696
  173.1 10.2 %collective-permute-start.3 = (f32[16,768]{1,0:T(8,128)S(1)}, f32[16,768]{1,0:T(8,128)S(1)}, u32[]{:S(2)}, u32[]{:S(2)}) collective-permute-start(f32[16,768]{1,0:T(8,128)S(1)} %get-tuple-element.30), channel_id=1, source_target_pairs={{1,0},{2,1},{3,2},{4,3},{5,4},{6,5},{7,6},{8,7},{9,8},{10,9},{11,1... | collective-permute-start | bytes 147464 | tf_op jit(solution)/shard_map/ppermute | solution.py:697

commit v3 on v2

--- a/solution.py
+++ b/solution.py
@@ -27,6 +27,10 @@
 H_EDGE = H_OWN + 2 * H_RIM
 H_POS = U_LOC // WIDE
 H_NODE = 7
+TAIL = 4
+TAIL_H = TAIL // 2
+GATHER_STEP = 512
+GATHER_ROWS = GATHER_STEP // LANE
 E_TILES = 72
 N_TILES = ELN // LANE
 BF = jnp.bfloat16
@@ -66,27 +70,38 @@
     )
 
 
+def low_part(index_rows):
+    return spread(index_rows & (WIDE - 1), 1).astype(F32).astype(BF)
+
+
 def one_hot_low(index_rows):
-    low = spread(index_rows & (WIDE - 1), WIDE)
-    return jnp.where(low == iota(low.shape, 0), 1.0, 0.0).astype(BF)
-
-
-def gather_tile(table, index_rows, rows, count):
-    hot = one_hot_low(index_rows)
-    found = jnp.dot(table, jnp.concatenate([hot, hot], axis=0), preferred_element_type=F32)
-    high = spread(index_rows >> 8, rows)
-    out = found[:rows]
+    low = low_part(index_rows)
+    shape = (WIDE, low.shape[1])
+    here = jnp.broadcast_to(low, shape) == iota(shape, 0).astype(F32).astype(BF)
+    return jnp.where(here, jnp.ones(shape, BF), jnp.zeros(shape, BF))
+
+
+def gather_tile(table, index_rows, rows, count, tail):
+    found = jnp.dot(table, one_hot_low(index_rows), preferred_element_type=F32)
+    high = spread(index_rows >> 8, 2 * rows)
+    out = found[: 2 * rows]
     for h in range(1, count):
-        out = jnp.where(high == h, found[h * rows : (h + 1) * rows], out)
-    return out
+        out = jnp.where(high == h, found[h * 2 * rows : (h + 1) * 2 * rows], out)
+    out = out[:rows] + out[rows:]
+    tiles = []
+    for i in range(index_rows.shape[0]):
+        index = jnp.broadcast_to(index_rows[i : i + 1], (rows, LANE))
+        part = out[:, i * LANE : (i + 1) * LANE]
+        for k in range(TAIL):
+            picked = jnp.take_along_axis(tail(k), index & (LANE - 1), axis=1)
+            part = jnp.where((index >> 7) == 2 * count + k, picked, part)
+        tiles.append(part)
+    return jnp.concatenate(tiles, axis=1)
 
 
 def fill_table(table, source, rows, count):
-    each = 1 if rows % 16 == 0 else 2
-    for h in range(0, count, each):
-        high, low = split(jnp.concatenate([source(h + i) for i in range(each)], axis=0))
-        table[h * rows : (h + each) * rows, :WIDE] = high
-        table[h * rows : (h + each) * rows, WIDE:] = low
+    for h in range(count):
+        table[h * 2 * rows : (h + 1) * 2 * rows, :] = stack(source(h))
 
 
 def mask_rows(left, x, index_rows, first, count):
@@ -110,14 +125,7 @@
     part = lax.dot_general(
         left[...], one_hot_low(index_rows), (((1,), (1,)), ((), ())), preferred_element_type=F32
     )
-
-    @pl.when(step == 0)
-    def _():
-        acc[...] = part
-
-    @pl.when(step > 0)
-    def _():
-        acc[...] += part
+    acc[...] = part if step == 0 else acc[...] + part
 
 
 def summed(acc, h, rows, at=slice(None)):
@@ -131,7 +139,11 @@
 
 
 def rows_of(step, count):
-    return pl.ds(pl.multiple_of(step * count, count), count)
+    return slice(step * count, (step + 1) * count)
+
+
+def cols_of(step, width):
+    return slice(step * width, (step + 1) * width)
 
 
 def lanes(step, width):
@@ -139,10 +151,23 @@
 
 
 def prep_kernel(
-    res, em, lm, owner, slot, epos_out, pos_out, slot_out, start_out, low_out, high_out, hots, rank_s, pos_s, tr
+    res, em_in, lm_in, owner_in, slot_in,
+    epos_out, pos_out, slot_out, start_out, low_out, high_out,
+    em, lm, owner, slot, hots, rank_s, pos_s, tr, sems,
 ):
-    low_out[...] = res[:, :RIM_W]
-    high_out[...] = res[:, E_LOC - RIM_W :]
+    moves = [
+        (owner_in, owner),
+        (em_in, em),
+        (lm_in, lm),
+        (slot_in, slot),
+        (res.at[:, :RIM_W], low_out),
+        (res.at[:, E_LOC - RIM_W :], high_out),
+    ]
+    moves = [pltpu.make_async_copy(a, b, sems.at[i]) for i, (a, b) in enumerate(moves)]
+    for move in moves:
+        move.start()
+    for move in moves:
+        move.wait()
     tr[:, : ED - LANE] = em[:, LANE:]
     rest = [tr[pl.ds(i, 8, stride=8), :][:, : ED - LANE] for i in range(8)]
     m = jnp.concatenate([em[:, :LANE], jnp.concatenate(rest, axis=1)], axis=0)
@@ -200,13 +225,16 @@
 
 
 def own_edges_kernel(res, epos, ev_out, table):
-    fill_table(table, lambda h: res[:, h * WIDE : (h + 1) * WIDE], RHS, H_OWN)
-
-    def body(step, carry):
-        ev_out[:, lanes(step, 1024)] = gather_tile(table[...], epos[rows_of(step, 8), :], RHS, H_OWN)
-        return carry
-
-    lax.fori_loop(0, E_TILES // 8, body, 0)
+    count = H_OWN - TAIL_H
+    fill_table(table, lambda h: res[:, cols_of(h, WIDE)], RHS, count)
+    for step in range(E_TILES * LANE // GATHER_STEP):
+        ev_out[:, cols_of(step, GATHER_STEP)] = gather_tile(
+            table[...],
+            epos[rows_of(step, GATHER_ROWS), :],
+            RHS,
+            count,
+            lambda k: res[:, cols_of(2 * count + k, LANE)],
+        )
 
 
 def fill_pi(w, pi):
@@ -235,10 +263,13 @@
         wide[:, t * LANE : (t + 1) * LANE] = jnp.take_along_axis(c, second + 2 * t, axis=1)
 
 
-NODE_STEP = 2048
+NODE_STEP = 1024
 NODE_ROWS = NODE_STEP // LANE
-EDGE_STEP = 3072
+NODE_STEPS = ELN // NODE_STEP
+EDGE_STEP = 1024
 EDGE_ROWS = EDGE_STEP // LANE
+EDGE_STEPS = E_TILES * LANE // EDGE_STEP
+BUFFERS = 3
 
 
 def from_acc(compact, acc):
@@ -252,11 +283,9 @@
     for p in range(PEERS):
         start = starts[p, 0]
         shift = start & (LANE - 1)
-        base = start - shift
-        back = lax.rem(LANE - shift, LANE)
-        one = pltpu.roll(compact[0:rows, lanes(base // LANE, LANE)], back, 1)
-        two = pltpu.roll(compact[0:rows, lanes(base // LANE + 1, LANE)], back, 1)
-        out[p] = jnp.where(lane < LANE - shift, one, two)[: out.shape[1]]
+        base = (start - shift) // LANE
+        both = jnp.where(lane >= shift, compact[0:rows, lanes(base, LANE)], compact[0:rows, lanes(base + 1, LANE)])
+        out[p] = pltpu.roll(both, lax.rem(LANE - shift, LANE), 1)[: out.shape[1]]
 
 
 def shrink(compact, arrived, starts):
@@ -266,30 +295,30 @@
         shift = start & (LANE - 1)
         base = (start - shift) // LANE
         block = pltpu.roll(arrived[p], shift, 1)
-        at = lanes(base, LANE)
-        compact[:, at] = jnp.where(lane >= shift, block, compact[:, at])
+        pltpu.store(compact.at[:, lanes(base, LANE)], block, mask=lane >= shift)
         compact[:, lanes(base + 1, LANE)] = block
 
 
 def restrict_kernel(
-    ev_own, before, after, epos, pos, slots, pi, stiff, mass, perm, curl, starts,
-    out, table, ev, w, coef, wide, xs, diag, left, acc, compact,
+    ev_own, before, after, epos, pos, slots, pi, stiff, mass, perm, curl, starts_in,
+    out, starts, sem, table, ev, w, coef, wide, xs, diag, left, acc, compact,
 ):
+    move = pltpu.make_async_copy(starts_in, starts, sem)
+    move.start()
+    count = 2 * H_RIM - TAIL_H
+
     def rim(h):
         ref = before if h < H_RIM else after
-        at = h % H_RIM * WIDE
-        return ref[:, at : at + WIDE]
-
-    fill_table(table, rim, RHS, 2 * H_RIM)
-
-    def rim_body(step, carry):
-        idx = epos[rows_of(step, 8), :] - E_LOC
-        found = gather_tile(table[...], idx, RHS, 2 * H_RIM)
-        at = lanes(step, 1024)
+        return ref[:, cols_of(h % H_RIM, WIDE)]
+
+    fill_table(table, rim, RHS, count)
+    for step in range(EDGE_STEPS):
+        idx = epos[rows_of(step, EDGE_ROWS), :] - E_LOC
+        found = gather_tile(
+            table[...], idx, RHS, count, lambda k: after[:, cols_of(2 * (count - H_RIM) + k, LANE)]
+        )
+        at = cols_of(step, EDGE_STEP)
         ev[:, at] = jnp.where(spread(idx, RHS) >= 0, found, ev_own[:, at])
-        return carry
-
-    lax.fori_loop(0, E_TILES // 8, rim_body, 0)
     fill_pi(w, pi)
     for v in range(4):
         blocks = []
@@ -326,15 +355,14 @@
         at = slice(t * LANE, (t + 1) * LANE)
         diag[:, at] = wide[6:7, at] * sd + md * wide[0:3, at]
 
-    def body(step, carry):
-        at = lanes(step, NODE_STEP)
+    for step in range(NODE_STEPS):
+        at = cols_of(step, NODE_STEP)
         idx = pos[rows_of(step, NODE_ROWS), :]
-        mask_rows(left, xs[:, at], idx, 0, H_POS)
-        mask_diag(left, H_POS * PAIR, [diag[c : c + 1, at] for c in range(3)], idx)
-        accumulate(acc, step, left, idx)
-        return carry
-
-    lax.fori_loop(0, ELN // NODE_STEP, body, 0)
+        now = left.at[step % BUFFERS]
+        mask_rows(now, xs[:, at], idx, 0, H_POS)
+        mask_diag(now, H_POS * PAIR, [diag[c : c + 1, at] for c in range(3)], idx)
+        accumulate(acc, step, now, idx)
+    move.wait()
     from_acc(compact, acc)
     for h in range(H_POS):
         for c in range(3):
@@ -347,39 +375,42 @@
 
 
 def collect(arrived, slots, left, acc, with_diag):
-    def body(step, carry):
+    for step in range(SLOTS // NODE_STEP):
         idx = slots[rows_of(step, NODE_ROWS), :]
         block = arrived[rows_of(step, NODE_ROWS)]
         x = jnp.concatenate([block[i, 0:ROWS] for i in range(NODE_ROWS)], axis=1)
-        mask_rows(left, stack(x), idx, 0, H_NODE)
+        now = left.at[step % BUFFERS]
+        mask_rows(now, stack(x), idx, 0, H_NODE)
         if with_diag:
             diag = [
                 jnp.concatenate([block[i, ROWS + c : ROWS + c + 1] for i in range(NODE_ROWS)], axis=1)
                 for c in range(3)
             ]
-            mask_diag(left, H_NODE * PAIR, diag, idx)
-        accumulate(acc, step, left, idx)
-        return carry
-
-    lax.fori_loop(0, PEERS // NODE_ROWS, body, 0)
-
-
-def serve(out, table, slots):
-    def body(step, carry):
-        found = gather_tile(table[...], slots[rows_of(step, 8), :], ROWS, H_NODE)
-        for i in range(8):
-            out[step * 8 + i] = found[:, i * LANE : (i + 1) * LANE]
-        return carry
-
-    lax.fori_loop(0, PEERS // 8, body, 0)
+            mask_diag(now, H_NODE * PAIR, diag, idx)
+        accumulate(acc, step, now, idx)
+
+
+def serve(out, table, last, value, slots):
+    count = H_NODE - TAIL_H
+    fill_table(table, value, ROWS, count)
+    for k in range(TAIL_H):
+        last[:, cols_of(k, WIDE)] = value(count + k)
+    for step in range(SLOTS // GATHER_STEP):
+        found = gather_tile(
+            table[...],
+            slots[rows_of(step, GATHER_ROWS), :],
+            ROWS,
+            count,
+            lambda k: last[:, cols_of(k, LANE)],
+        )
+        for i in range(GATHER_ROWS):
+            out[step * GATHER_ROWS + i] = found[:, cols_of(i, LANE)]
 
 
 def first_values(rhs, floor):
     first = cheb_factors()[0]
 
     def value(h):
-        if h >= H_NODE:
-            return jnp.zeros((ROWS, WIDE), F32)
         return jnp.concatenate(
             [
                 first * rhs[h, c * RHS : (c + 1) * RHS, :] / floor[h, c : c + 1, :]
@@ -391,7 +422,7 @@
     return value
 
 
-def first_kernel(arrived, out, rhs_out, floor_out, slot_out, table, left, acc):
+def first_kernel(arrived, out, rhs_out, floor_out, slot_out, table, last, left, acc):
     for p in range(PEERS):
         slot_out[p : p + 1, :] = arrived[p, SENT - 1 : SENT, :].astype(I32)
     collect(arrived, slot_out, left, acc, True)
@@ -399,17 +430,14 @@
         rhs_out[h] = summed(acc, h, ROWS)
         for c in range(3):
             floor_out[h, c : c + 1, :] = jnp.maximum(diag_summed(acc, H_NODE * PAIR, c, h), 1.0)
-    fill_table(table, first_values(rhs_out, floor_out), ROWS, H_NODE + 1)
-    serve(out, table, slot_out)
-
-
-def second_kernel(arrived, rhs, floor, slots, out, table, left, acc):
+    serve(out, table, last, first_values(rhs_out, floor_out), slot_out)
+
+
+def second_kernel(arrived, rhs, floor, slots, out, table, last, left, acc):
     first, keep, step = cheb_factors()
     collect(arrived, slots, left, acc, False)
 
     def value(h):
-        if h >= H_NODE:
-            return jnp.zeros((ROWS, WIDE), F32)
         applied = summed(acc, h, ROWS)
         parts = []
         for c in range(3):
@@ -419,13 +447,23 @@
             parts.append(keep * (first * part / low) + step * (part - applied[at]) / low)
         return jnp.concatenate(parts, axis=0)
 
-    fill_table(table, value, ROWS, H_NODE + 1)
-    serve(out, table, slots)
+    serve(out, table, last, value, slots)
 
 
 def touched_table(table, compact, arrived, starts):
     shrink(compact, arrived, starts)
-    fill_table(table, lambda h: compact[:, h * WIDE : (h + 1) * WIDE], ROWS, H_POS)
+    fill_table(table, lambda h: compact[:, cols_of(h, WIDE)], ROWS, H_POS - TAIL_H)
+
+
+def touched_tile(table, compact, pos, step):
+    count = H_POS - TAIL_H
+    return gather_tile(
+        table[...],
+        pos[rows_of(step, GATHER_ROWS), :],
+        ROWS,
+        count,
+        lambda k: compact[:, cols_of(2 * count + k, LANE)],
+    )
 
 
 def apply_kernel(
@@ -441,21 +479,21 @@
                 at = slice(m * LANE + e2 * NN, m * LANE + (e2 + 1) * NN)
                 op[k, e2 * NN : (e2 + 1) * NN, at] = part[k]
 
-    def element_body(step, carry):
-        values = gather_tile(table[...], pos[rows_of(step, 8), :], ROWS, H_POS)
+    tensor = ((0, 3, 4), (3, 1, 5), (4, 5, 2))
+    for step in range(ELN // GATHER_STEP):
+        values = touched_tile(table, compact, pos, step)
         high, low = split(
-            jnp.concatenate([values[:, i * LANE : (i + 1) * LANE] for i in range(8)], axis=0)
+            jnp.concatenate([values[:, cols_of(i, LANE)] for i in range(GATHER_ROWS)], axis=0)
         )
         y = (
             jnp.dot(high, op[0], preferred_element_type=F32)
             + jnp.dot(high, op[1], preferred_element_type=F32)
             + jnp.dot(low, op[0], preferred_element_type=F32)
         )
-        cols = wide[:, lanes(step, 1024)]
-        tensor = ((0, 3, 4), (3, 1, 5), (4, 5, 2))
+        cols = wide[:, cols_of(step, GATHER_STEP)]
         tiles = []
-        for i in range(8):
-            k = cols[:, i * LANE : (i + 1) * LANE]
+        for i in range(GATHER_ROWS):
+            k = cols[:, cols_of(i, LANE)]
             rows = [slice(i * ROWS + c * RHS, i * ROWS + (c + 1) * RHS) for c in range(3)]
             s = [y[r, :LANE] for r in rows]
             m = [y[r, LANE:] for r in rows]
@@ -471,18 +509,12 @@
                     axis=0,
                 )
             )
-        xs[:, lanes(step, 1024)] = stack(jnp.concatenate(tiles, axis=1))
-        return carry
-
-    lax.fori_loop(0, ELN // 1024, element_body, 0)
-
-    def body(step, carry):
+        xs[:, cols_of(step, GATHER_STEP)] = stack(jnp.concatenate(tiles, axis=1))
+    for step in range(NODE_STEPS):
         idx = pos[rows_of(step, NODE_ROWS), :]
-        mask_rows(left, xs[:, lanes(step, NODE_STEP)], idx, 0, H_POS)
-        accumulate(acc, step, left, idx)
-        return carry
-
-    lax.fori_loop(0, ELN // NODE_STEP, body, 0)
+        now = left.at[step % BUFFERS]
+        mask_rows(now, xs[:, cols_of(step, NODE_STEP)], idx, 0, H_POS)
+        accumulate(acc, step, now, idx)
     from_acc(compact, acc)
     expand(out, compact, starts, ROWS)
 
@@ -491,11 +523,8 @@
     touched_table(table, compact, arrived, starts)
     fill_pi(w, pi)
 
-    def gather_body(step, carry):
-        values[:, lanes(step, 1024)] = gather_tile(table[...], pos[rows_of(step, 8), :], ROWS, H_POS)
-        return carry
-
-    lax.fori_loop(0, ELN // 1024, gather_body, 0)
+    for step in range(ELN // GATHER_STEP):
+        values[:, cols_of(step, GATHER_STEP)] = touched_tile(table, compact, pos, step)
     dims = (((1,), (1,)), ((), ()))
     rest = None
     for v in range(4):
@@ -520,13 +549,11 @@
 
 
 def edge_scatter(terms, epos, left, acc, first, count):
-    def body(step, carry):
+    for step in range(EDGE_STEPS):
         idx = epos[rows_of(step, EDGE_ROWS), :]
-        mask_rows(left, terms[:, lanes(step, EDGE_STEP)], idx, first, count)
-        accumulate(acc, step, left, idx)
-        return carry
-
-    lax.fori_loop(0, E_TILES // EDGE_ROWS, body, 0)
+        now = left.at[step % BUFFERS]
+        mask_rows(now, terms[:, cols_of(step, EDGE_STEP)], idx, first, count)
+        accumulate(acc, step, now, idx)
 
 
 def prolong_rim_kernel(
@@ -556,15 +583,17 @@
 
 
 SM = pl.BlockSpec(memory_space=pltpu.SMEM)
-
-
-def call(kernel, name, micros, outs, scratch, *args, scalars=0):
+ANY = pl.BlockSpec(memory_space=pl.ANY)
+
+
+def call(kernel, name, micros, outs, scratch, *args, scalars=0, outside=0):
+    inside = len(args) - scalars - outside
     return pl.pallas_call(
         kernel,
         out_shape=[jax.ShapeDtypeStruct(s, t) for s, t in outs],
-        in_specs=[VM] * (len(args) - scalars) + [SM] * scalars,
+        in_specs=[ANY] * outside + [VM] * inside + [SM] * scalars,
         out_specs=[VM] * len(outs),
-        scratch_shapes=[pltpu.VMEM(s, t) for s, t in scratch],
+        scratch_shapes=[x if not isinstance(x, tuple) else pltpu.VMEM(*x) for x in scratch],
         compiler_params=pltpu.CompilerParams(vmem_limit_bytes=40 << 20),
         cost_estimate=pl.CostEstimate(flops=0, bytes_accessed=micros * 3600000, transcendentals=0),
         name=name,
@@ -606,18 +635,29 @@
             rim,
             rim,
         ],
-        [((chunks * PEERS, LANE), BF), ((chunks, LANE), I32), ((chunks, LANE), I32), ((EL, LANE), I32)],
+        [
+            ((EL, ED), I32),
+            ((NN, EL), I32),
+            ((chunks, LANE), I32),
+            ((chunks, LANE), I32),
+            ((chunks * PEERS, LANE), BF),
+            ((chunks, LANE), I32),
+            ((chunks, LANE), I32),
+            ((EL, LANE), I32),
+            pltpu.SemaphoreType.DMA((6,)),
+        ],
         residual_edges,
         edge_map.T,
         local_map,
         node_owner.reshape(chunks, LANE),
         node_slot.reshape(chunks, LANE),
+        outside=5,
     )
     before = lax.ppermute(high, axes, up)
     after = lax.ppermute(low, axes, down)
     edge_rows = ((RHS, E_TILES * LANE), F32)
     (ev_own,) = call(
-        own_edges_kernel, "own_edges", 4, [edge_rows], [((H_OWN * RHS, 2 * WIDE), BF)], residual_edges, epos
+        own_edges_kernel, "own_edges", 4, [edge_rows], [(((H_OWN - TAIL_H) * 2 * RHS, WIDE), BF)], residual_edges, epos
     )
     pi_scratch = ((4, 2, 384, 384), BF)
     coefs = [((8, LANE), F32), ((8, ELN), F32)]
@@ -629,29 +669,30 @@
         6,
         [((PEERS, SENT, CAP), F32)],
         [
-            ((2 * H_RIM * RHS, 2 * WIDE), BF),
+            pltpu.SMEM((PEERS, LANE), I32),
+            pltpu.SemaphoreType.DMA,
+            (((2 * H_RIM - TAIL_H) * 2 * RHS, WIDE), BF),
             edge_rows,
             pi_scratch,
             *coefs,
             ((PAIR, ELN), BF),
             ((3, ELN), F32),
-            ((H_POS * PAIR + 96, NODE_STEP), BF),
+            ((BUFFERS, H_POS * PAIR + 96, NODE_STEP), BF),
             ((H_POS * PAIR + 96, WIDE), F32),
             ((SENT + 4, U_LOC + 2 * LANE), F32),
         ],
         ev_own, before, after, epos, pos, slot_rows, pi_block, stiff_block, mass_block, permittivity, curl, starts,
-        scalars=1,
-    )
-    table = (((H_NODE + 1) * ROWS, 2 * WIDE), BF)
+    )
+    served_scratch = [(((H_NODE - TAIL_H) * PAIR, WIDE), BF), ((ROWS, TAIL_H * WIDE), F32)]
     wanted, rhs, floor, slots = call(
         first_kernel,
         "first_iter",
         5,
         [served, ((H_NODE, ROWS, WIDE), F32), ((H_NODE, 3, WIDE), F32), ((PEERS, CAP), I32)],
-        [table, ((H_NODE * PAIR + 96, NODE_STEP), BF), ((H_NODE * PAIR + 96, WIDE), F32)],
+        [*served_scratch, ((BUFFERS, H_NODE * PAIR + 96, NODE_STEP), BF), ((H_NODE * PAIR + 96, WIDE), F32)],
         exchange(packed),
     )
-    position_table = ((H_POS * ROWS, 2 * WIDE), BF)
+    position_table = (((H_POS - TAIL_H) * PAIR, WIDE), BF)
     (applied,) = call(
         apply_kernel,
         "operator",
@@ -662,7 +703,7 @@
             ((2, LANE, 2 * LANE), BF),
             *coefs,
             ((PAIR, ELN), BF),
-            ((H_POS * PAIR, NODE_STEP), BF),
+            ((BUFFERS, H_POS * PAIR, NODE_STEP), BF),
             ((H_POS * PAIR, WIDE), F32),
             compact,
         ],
@@ -674,7 +715,7 @@
         "second_iter",
         5,
         [served],
-        [table, ((H_NODE * PAIR, NODE_STEP), BF), ((H_NODE * PAIR, WIDE), F32)],
+        [*served_scratch, ((BUFFERS, H_NODE * PAIR, NODE_STEP), BF), ((H_NODE * PAIR, WIDE), F32)],
         exchange(applied), rhs, floor, slots,
     )
     terms, low, high = call(
@@ -687,7 +728,7 @@
             pi_scratch,
             ((ROWS, ELN), F32),
             compact,
-            ((2 * H_RIM * 2 * RHS, EDGE_STEP), BF),
+            ((BUFFERS, 2 * H_RIM * 2 * RHS, EDGE_STEP), BF),
             ((2 * H_RIM * 2 * RHS, WIDE), F32),
         ],
         exchange(wanted), pos, epos, pi_block, starts,
@@ -700,7 +741,7 @@
         "prolong_own",
         5,
         [((RHS, E_LOC), F32)],
-        [((H_OWN * 2 * RHS, EDGE_STEP), BF), ((H_OWN * 2 * RHS, WIDE), F32)],
+        [((BUFFERS, H_OWN * 2 * RHS, EDGE_STEP), BF), ((H_OWN * 2 * RHS, WIDE), F32)],
         terms, epos,
     )
     (out,) = call(finish_kernel, "finish", 1, [((RHS, E_LOC), F32)], [], own, from_before, from_after)

time: 185 us -> 179 us (0.968)
  Pallas kernels: 44.4 us -> 37.5 us
    pallas_call x9, Pallas kernels: 44.4 us -> 37.5 us  [call(): pl.pallas_call(kernel, out_shape=[jax.ShapeDtypeStruct(s, t) for s, t in...]
  transfers between devices with their start and end apart: 4 -> 4, of which waited for: 0 -> 0; matrix products, arithmetic and copies ran while one was open for 0% -> 0% of each run, Pallas kernels for 5% -> 4%
where the time goes in v3:
time: 179 us; the launch traced here: 178 us
  blocking collectives  115 us (64%)
  Pallas kernels  37.5 us (21%)
  starting transfers between devices  21 us (12%)
  local copies, waits for them, and re-layouts  4.61 us (3%)
    all_to_all x4, blocking collectives, exchange(): return lax.all_to_all(x, 'dev', split_axis=0, concat_axis=0, tiled=True)  115 us
    pallas_call x9, Pallas kernels, call(): pl.pallas_call(kernel, out_shape=[jax.ShapeDtypeStruct(s, t) for s, t in...  37.5 us
    ppermute x1, starting transfers between devices, per_device(): after = lax.ppermute(low, axes, down)  7.38 us
    ppermute x1, starting transfers between devices, per_device(): from_after = lax.ppermute(low, axes, down)  6.16 us
    unnamed x20, local copies, waits for them, and re-layouts  4.61 us
    ppermute x1, starting transfers between devices, per_device(): before = lax.ppermute(high, axes, up)  3.82 us
    ppermute x1, starting transfers between devices, per_device(): from_before = lax.ppermute(high, axes, up)  3.63 us
  transfers between devices with their start and end apart: 4, of which 0 were waited for; matrix products, arithmetic and copies ran while one was open for 0% of the time, Pallas kernels for 4%

profile of v3, /device:TPU:16, one launch (start us, length us, event | category | flops | bytes accessed | tf_op | source)
XLA Modules:
  0.0 177.9 jit_solution(13322881160877673653)
XLA Ops:
  0.0 0.0 copy-start
  0.0 1.0 copy-done
  1.0 0.0 copy-start.4
  1.0 0.8 copy-done.4
  1.8 0.0 copy-start.5
  1.8 0.8 copy-done.5
  2.6 0.0 copy-start.7
  2.6 0.7 copy-done.7
  3.3 0.0 copy-start.8
  3.3 0.7 copy-done.8
  4.0 0.9 index_prep.1
  4.9 3.8 %collective-permute-start = (f32[16,768]{1,0:T(8,128)S(1)}, f32[16,768]{1,0:T(8,128)S(1)}, u32[]{:S(2)}, u32[]{:S(2)}) collective-permute-start(f32[16,768]{1,0:T(8,128)S(1)} %get-tuple-element.19), channel_id=1, source_target_pairs={{0,1},{1,2},{2,3},{3,4},{4,5},{5,6},{6,7},{7,8},{8,9},{9,10},{10,1... | collective-permute-start | bytes 147464 | tf_op jit(solution)/shard_map/ppermute | solution.py:656
  8.7 7.4 %collective-permute-start.1 = (f32[16,768]{1,0:T(8,128)S(1)}, f32[16,768]{1,0:T(8,128)S(1)}, u32[]{:S(2)}, u32[]{:S(2)}) collective-permute-start(f32[16,768]{1,0:T(8,128)S(1)} %get-tuple-element.20), channel_id=1, source_target_pairs={{1,0},{2,1},{3,2},{4,3},{5,4},{6,5},{7,6},{8,7},{9,8},{10,9},{11,1... | collective-permute-start | bytes 147464 | tf_op jit(solution)/shard_map/ppermute | solution.py:657
  16.1 0.0 copy-start.1
  16.1 0.0 copy-start.2
  16.1 0.0 copy-start.3
  16.1 3.1 %own_edges.1.ev_own = f32[16,9216]{1,0:T(8,128)S(1)} custom-call(f32[16,5376]{1,0:T(8,128)S(1)} %copy-done, s32[72,128]{1,0:T(8,128)S(1)} %get-tuple-element.18.epos), custom_call_target="tpu_custom_call" | custom-call | bytes 14400000 | tf_op jit(solution)/shard_map/own_edges/pallas_call | solution.py:591
  19.3 0.0 copy-start.6
  19.3 0.0 collective-permute-done.before
  19.3 0.0 collective-permute-done.1.after
  19.3 0.0 copy-start.9
  19.3 0.0 copy-done.1
  19.3 0.0 copy-done.2
  19.3 0.0 copy-done.3
  19.3 0.6 copy-done.6
  20.0 0.0 copy-done.9
  20.0 4.8 %restrict.1 = f32[32,52,128]{2,1,0:T(8,128)S(1)} custom-call(f32[16,9216]{1,0:T(8,128)S(1)} %own_edges.1.ev_own, f32[16,768]{1,0:T(8,128)S(1)} %collective-permute-done.before, f32[16,768]{1,0:T(8,128)S(1)} %collective-permute-done.1.after, s32[72,128]{1,0:T(8,128)S(1)} %get-tuple-element.18.epos, s32[32,128]{1,0:T(8,128)S(1)} %get-tuple-element.21.pos, ...), custom_call_target="tpu_custom_call" | custom-call | bytes 21600000 | tf_op jit(solution)/shard_map/restrict/pallas_call | solution.py:591
  24.7 33.0 %all_to_all.20.arrived = f32[32,52,128]{2,1,0:T(8,128)S(1)} all-to-all(f32[32,52,128]{2,1,0:T(8,128)S(1)} %restrict.1), channel_id=1, replica_groups=mesh['grp'=8,'dev'=32] {'dev'}, dimensions={0} | all-to-all | bytes 1703936 | tf_op jit(solution)/shard_map/all_to_all | solution.py:604
  57.7 5.0 %first_iter.1 = (f32[32,48,128]{2,1,0:T(8,128)S(1)}, f32[7,48,256]{2,1,0:T(8,128)S(1)}, f32[7,3,256]{2,1,0:T(4,128)S(1)}, s32[32,128]{1,0:T(8,128)S(1)}) custom-call(f32[32,52,128]{2,1,0:T(8,128)S(1)} %all_to_all.20.arrived), custom_call_target="tpu_custom_call" | custom-call | bytes 18000000 | tf_op jit(solution)/shard_map/first_iter/pallas_call | solution.py:591
  62.8 27.5 %all_to_all.21.arrived = f32[32,48,128]{2,1,0:T(8,128)S(1)} all-to-all(f32[32,48,128]{2,1,0:T(8,128)S(1)} %get-tuple-element.24), channel_id=1, replica_groups=mesh['grp'=8,'dev'=32] {'dev'}, dimensions={0} | all-to-all | bytes 1572864 | tf_op jit(solution)/shard_map/all_to_all | solution.py:604
  90.3 6.4 %operator.1 = f32[32,48,128]{2,1,0:T(8,128)S(1)} custom-call(f32[32,48,128]{2,1,0:T(8,128)S(1)} %all_to_all.21.arrived, s32[32,128]{1,0:T(8,128)S(1)} %get-tuple-element.21.pos, f32[64,64]{1,0:T(8,128)S(1)} %copy-done.2, f32[64,64]{1,0:T(8,128)S(1)} %copy-done.3, f32[6,64]{1,0:T(8,128)S(1)} %copy-done.6, f32[1,64]{1,0:T(1,128)S(1)} %bitcast.8, ...), custom_call_target="tpu_custom_call" | custom-call | bytes 28800000 | tf_op jit(solution)/shard_map/operator/pallas_call | solution.py:591
  96.7 27.0 %all_to_all.22.arrived = f32[32,48,128]{2,1,0:T(8,128)S(1)} all-to-all(f32[32,48,128]{2,1,0:T(8,128)S(1)} %operator.1), channel_id=1, replica_groups=mesh['grp'=8,'dev'=32] {'dev'}, dimensions={0} | all-to-all | bytes 1572864 | tf_op jit(solution)/shard_map/all_to_all | solution.py:604
  123.8 4.6 %second_iter.1 = f32[32,48,128]{2,1,0:T(8,128)S(1)} custom-call(f32[32,48,128]{2,1,0:T(8,128)S(1)} %all_to_all.22.arrived, f32[7,48,256]{2,1,0:T(8,128)S(1)} %get-tuple-element.25.rhs, f32[7,3,256]{2,1,0:T(4,128)S(1)} %get-tuple-element.26.floor, s32[32,128]{1,0:T(8,128)S(1)} %get-tuple-element.27.slots), custom_call_target="tpu_custom_call" | custom-call | bytes 18000000 | tf_op jit(solution)/shard_map/second_iter/pallas_call | solution.py:591
  128.4 26.9 %all_to_all.23.arrived = f32[32,48,128]{2,1,0:T(8,128)S(1)} all-to-all(f32[32,48,128]{2,1,0:T(8,128)S(1)} %second_iter.1), channel_id=1, replica_groups=mesh['grp'=8,'dev'=32] {'dev'}, dimensions={0} | all-to-all | bytes 1572864 | tf_op jit(solution)/shard_map/all_to_all | solution.py:604
  155.3 7.6 %prolong_rim.1 = (bf16[32,9216]{1,0:T(8,128)(2,1)S(1)}, f32[16,768]{1,0:T(8,128)S(1)}, f32[16,768]{1,0:T(8,128)S(1)}) custom-call(f32[32,48,128]{2,1,0:T(8,128)S(1)} %all_to_all.23.arrived, s32[32,128]{1,0:T(8,128)S(1)} %get-tuple-element.21.pos, s32[72,128]{1,0:T(8,128)S(1)} %get-tuple-element.18.epos, f32[144,192]{1,0:T(8,128)S(1)} %copy-done.1, ...), custom_call_target="tpu_custom_call" | custom-call | bytes 21600000 | tf_op jit(solution)/shard_map/prolong_rim/pallas_call | solution.py:591
  162.9 3.6 %collective-permute-start.2 = (f32[16,768]{1,0:T(8,128)S(1)}, f32[16,768]{1,0:T(8,128)S(1)}, u32[]{:S(2)}, u32[]{:S(2)}) collective-permute-start(f32[16,768]{1,0:T(8,128)S(1)} %get-tuple-element.29), channel_id=1, source_target_pairs={{0,1},{1,2},{2,3},{3,4},{4,5},{5,6},{6,7},{7,8},{8,9},{9,10},{10,1... | collective-permute-start | bytes 147464 | tf_op jit(solution)/shard_map/ppermute | solution.py:737
  166.6 6.2 %collective-permute-start.3 = (f32[16,768]{1,0:T(8,128)S(1)}, f32[16,768]{1,0:T(8,128)S(1)}, u32[]{:S(2)}, u32[]{:S(2)}) collective-permute-start(f32[16,768]{1,0:T(8,128)S(1)} %get-tuple-element.30), channel_id=1, source_target_pairs={{1,0},{2,1},{3,2},{4,3},{5,4},{6,5},{7,6},{8,7},{9,8},{10,9},{11,1... | collective-permute-start | bytes 147464 | tf_op jit(solution)/shard_map/ppermute | solution.py:738
  172.7 4.4 %prolong_own.1.own = f32[16,5376]{1,0:T(8,128)S(1)} custom-call(bf16[32,9216]{1,0:T(8,128)(2,1)S(1)} %get-tuple-element.28.terms, s32[72,128]{1,0:T(8,128)S(1)} %get-tuple-element.18.epos), custom_call_target="tpu_custom_call" | custom-call | bytes 18000000 | tf_op jit(solution)/shard_map/prolong_own/pallas_call | solution.py:591
  177.1 0.0 collective-permute-done.2.before
  177.1 0.0 collective-permute-done.3.after
  177.1 0.8 finish.1
Async XLA Ops:
  0.0 1.0 copy-start
  1.0 0.8 copy-start.4
  1.8 0.8 copy-start.5
  2.6 0.7 copy-start.7
  3.3 0.7 copy-start.8
  4.9 14.4 %collective-permute-start = (f32[16,768]{1,0:T(8,128)S(1)}, f32[16,768]{1,0:T(8,128)S(1)}, u32[]{:S(2)}, u32[]{:S(2)}) collective-permute-start(f32[16,768]{1,0:T(8,128)S(1)} %get-tuple-element.19), channel_id=1, source_target_pairs={{0,1},{1,2},{2,3},{3,4},{4,5},{5,6},{6,7},{7,8},{8,9},{9,10},{10,1... | collective-permute-start | bytes 147464 | tf_op jit(solution)/shard_map/ppermute | solution.py:656
  8.7 10.6 %collective-permute-start.1 = (f32[16,768]{1,0:T(8,128)S(1)}, f32[16,768]{1,0:T(8,128)S(1)}, u32[]{:S(2)}, u32[]{:S(2)}) collective-permute-start(f32[16,768]{1,0:T(8,128)S(1)} %get-tuple-element.20), channel_id=1, source_target_pairs={{1,0},{2,1},{3,2},{4,3},{5,4},{6,5},{7,6},{8,7},{9,8},{10,9},{11,1... | collective-permute-start | bytes 147464 | tf_op jit(solution)/shard_map/ppermute | solution.py:657
  16.1 3.2 %copy-start.1 = (f32[144,192]{1,0:T(8,128)S(1)}, f32[144,192]{1,0:T(8,128)}, u32[]{:S(2)}) copy-start(f32[144,192]{1,0:T(8,128)} %pi.3) | copy-start | bytes 331780
  16.1 3.2 %copy-start.2 = (f32[64,64]{1,0:T(8,128)S(1)}, f32[64,64]{1,0:T(8,128)}, u32[]{:S(2)}) copy-start(f32[64,64]{1,0:T(8,128)} %stiff.3) | copy-start | bytes 49156
  16.1 3.2 %copy-start.3 = (f32[64,64]{1,0:T(8,128)S(1)}, f32[64,64]{1,0:T(8,128)}, u32[]{:S(2)}) copy-start(f32[64,64]{1,0:T(8,128)} %mass.3) | copy-start | bytes 49156
  19.3 0.7 copy-start.6
  19.3 0.7 copy-start.9
  162.9 14.2 %collective-permute-start.2 = (f32[16,768]{1,0:T(8,128)S(1)}, f32[16,768]{1,0:T(8,128)S(1)}, u32[]{:S(2)}, u32[]{:S(2)}) collective-permute-start(f32[16,768]{1,0:T(8,128)S(1)} %get-tuple-element.29), channel_id=1, source_target_pairs={{0,1},{1,2},{2,3},{3,4},{4,5},{5,6},{6,7},{7,8},{8,9},{9,10},{10,1... | collective-permute-start | bytes 147464 | tf_op jit(solution)/shard_map/ppermute | solution.py:737
  166.6 10.6 %collective-permute-start.3 = (f32[16,768]{1,0:T(8,128)S(1)}, f32[16,768]{1,0:T(8,128)S(1)}, u32[]{:S(2)}, u32[]{:S(2)}) collective-permute-start(f32[16,768]{1,0:T(8,128)S(1)} %get-tuple-element.30), channel_id=1, source_target_pairs={{1,0},{2,1},{3,2},{4,3},{5,4},{6,5},{7,6},{8,7},{9,8},{10,9},{11,1... | collective-permute-start | bytes 147464 | tf_op jit(solution)/shard_map/ppermute | solution.py:738

commit v4 on v3

--- a/solution.py
+++ b/solution.py
@@ -29,7 +29,7 @@
 H_NODE = 7
 TAIL = 4
 TAIL_H = TAIL // 2
-GATHER_STEP = 512
+GATHER_STEP = 1024
 GATHER_ROWS = GATHER_STEP // LANE
 E_TILES = 72
 N_TILES = ELN // LANE
@@ -125,7 +125,17 @@
     part = lax.dot_general(
         left[...], one_hot_low(index_rows), (((1,), (1,)), ((), ())), preferred_element_type=F32
     )
-    acc[...] = part if step == 0 else acc[...] + part
+    if isinstance(step, int):
+        acc[...] = part if step == 0 else acc[...] + part
+        return
+
+    @pl.when(step == 0)
+    def _():
+        acc[...] = part
+
+    @pl.when(step > 0)
+    def _():
+        acc[...] += part
 
 
 def summed(acc, h, rows, at=slice(None)):
@@ -138,12 +148,22 @@
     return acc[row : row + 1, at] + acc[row + 16 : row + 17, at]
 
 
+def over(count, body, loop):
+    if loop:
+        lax.fori_loop(0, count, lambda step, carry: (body(step), carry)[1], 0)
+    else:
+        for step in range(count):
+            body(step)
+
+
 def rows_of(step, count):
-    return slice(step * count, (step + 1) * count)
+    if isinstance(step, int):
+        return slice(step * count, (step + 1) * count)
+    return pl.ds(pl.multiple_of(step * count, count), count)
 
 
 def cols_of(step, width):
-    return slice(step * width, (step + 1) * width)
+    return rows_of(step, width)
 
 
 def lanes(step, width):
@@ -263,13 +283,14 @@
         wide[:, t * LANE : (t + 1) * LANE] = jnp.take_along_axis(c, second + 2 * t, axis=1)
 
 
-NODE_STEP = 1024
+NODE_STEP = 2048
 NODE_ROWS = NODE_STEP // LANE
 NODE_STEPS = ELN // NODE_STEP
-EDGE_STEP = 1024
+EDGE_STEP = 3072
 EDGE_ROWS = EDGE_STEP // LANE
 EDGE_STEPS = E_TILES * LANE // EDGE_STEP
-BUFFERS = 3
+BUFFERS = 2
+LOOP = {'collect': 1, 'edge': 1, 'node': 0, 'serve': 0, 'tile': 0, 'rim': 0}
 
 
 def from_acc(compact, acc):
@@ -312,13 +333,15 @@
         return ref[:, cols_of(h % H_RIM, WIDE)]
 
     fill_table(table, rim, RHS, count)
-    for step in range(EDGE_STEPS):
-        idx = epos[rows_of(step, EDGE_ROWS), :] - E_LOC
+    def step_body(step):
+        idx = epos[rows_of(step, GATHER_ROWS), :] - E_LOC
         found = gather_tile(
             table[...], idx, RHS, count, lambda k: after[:, cols_of(2 * (count - H_RIM) + k, LANE)]
         )
-        at = cols_of(step, EDGE_STEP)
+        at = cols_of(step, GATHER_STEP)
         ev[:, at] = jnp.where(spread(idx, RHS) >= 0, found, ev_own[:, at])
+
+    over(E_TILES // GATHER_ROWS, step_body, LOOP['rim'])
     fill_pi(w, pi)
     for v in range(4):
         blocks = []
@@ -355,13 +378,15 @@
         at = slice(t * LANE, (t + 1) * LANE)
         diag[:, at] = wide[6:7, at] * sd + md * wide[0:3, at]
 
-    for step in range(NODE_STEPS):
+    def step_body(step):
         at = cols_of(step, NODE_STEP)
         idx = pos[rows_of(step, NODE_ROWS), :]
-        now = left.at[step % BUFFERS]
+        now = left.at[step % BUFFERS] if isinstance(step, int) else left.at[0]
         mask_rows(now, xs[:, at], idx, 0, H_POS)
         mask_diag(now, H_POS * PAIR, [diag[c : c + 1, at] for c in range(3)], idx)
         accumulate(acc, step, now, idx)
+
+    over(NODE_STEPS, step_body, LOOP['node'])
     move.wait()
     from_acc(compact, acc)
     for h in range(H_POS):
@@ -375,11 +400,11 @@
 
 
 def collect(arrived, slots, left, acc, with_diag):
-    for step in range(SLOTS // NODE_STEP):
+    def step_body(step):
         idx = slots[rows_of(step, NODE_ROWS), :]
         block = arrived[rows_of(step, NODE_ROWS)]
         x = jnp.concatenate([block[i, 0:ROWS] for i in range(NODE_ROWS)], axis=1)
-        now = left.at[step % BUFFERS]
+        now = left.at[step % BUFFERS] if isinstance(step, int) else left.at[0]
         mask_rows(now, stack(x), idx, 0, H_NODE)
         if with_diag:
             diag = [
@@ -389,13 +414,15 @@
             mask_diag(now, H_NODE * PAIR, diag, idx)
         accumulate(acc, step, now, idx)
 
+    over(SLOTS // NODE_STEP, step_body, LOOP['collect'])
+
 
 def serve(out, table, last, value, slots):
     count = H_NODE - TAIL_H
     fill_table(table, value, ROWS, count)
     for k in range(TAIL_H):
         last[:, cols_of(k, WIDE)] = value(count + k)
-    for step in range(SLOTS // GATHER_STEP):
+    def step_body(step):
         found = gather_tile(
             table[...],
             slots[rows_of(step, GATHER_ROWS), :],
@@ -405,6 +432,8 @@
         )
         for i in range(GATHER_ROWS):
             out[step * GATHER_ROWS + i] = found[:, cols_of(i, LANE)]
+
+    over(SLOTS // GATHER_STEP, step_body, LOOP['serve'])
 
 
 def first_values(rhs, floor):
@@ -480,7 +509,7 @@
                 op[k, e2 * NN : (e2 + 1) * NN, at] = part[k]
 
     tensor = ((0, 3, 4), (3, 1, 5), (4, 5, 2))
-    for step in range(ELN // GATHER_STEP):
+    def step_body(step):
         values = touched_tile(table, compact, pos, step)
         high, low = split(
             jnp.concatenate([values[:, cols_of(i, LANE)] for i in range(GATHER_ROWS)], axis=0)
@@ -510,11 +539,15 @@
                 )
             )
         xs[:, cols_of(step, GATHER_STEP)] = stack(jnp.concatenate(tiles, axis=1))
-    for step in range(NODE_STEPS):
+
+    over(ELN // GATHER_STEP, step_body, LOOP['tile'])
+    def step_body(step):
         idx = pos[rows_of(step, NODE_ROWS), :]
-        now = left.at[step % BUFFERS]
+        now = left.at[step % BUFFERS] if isinstance(step, int) else left.at[0]
         mask_rows(now, xs[:, cols_of(step, NODE_STEP)], idx, 0, H_POS)
         accumulate(acc, step, now, idx)
+
+    over(NODE_STEPS, step_body, LOOP['node'])
     from_acc(compact, acc)
     expand(out, compact, starts, ROWS)
 
@@ -523,8 +556,10 @@
     touched_table(table, compact, arrived, starts)
     fill_pi(w, pi)
 
-    for step in range(ELN // GATHER_STEP):
+    def step_body(step):
         values[:, cols_of(step, GATHER_STEP)] = touched_tile(table, compact, pos, step)
+
+    over(ELN // GATHER_STEP, step_body, LOOP['tile'])
     dims = (((1,), (1,)), ((), ()))
     rest = None
     for v in range(4):
@@ -549,11 +584,13 @@
 
 
 def edge_scatter(terms, epos, left, acc, first, count):
-    for step in range(EDGE_STEPS):
+    def step_body(step):
         idx = epos[rows_of(step, EDGE_ROWS), :]
-        now = left.at[step % BUFFERS]
+        now = left.at[step % BUFFERS] if isinstance(step, int) else left.at[0]
         mask_rows(now, terms[:, cols_of(step, EDGE_STEP)], idx, first, count)
         accumulate(acc, step, now, idx)
+
+    over(EDGE_STEPS, step_body, LOOP['edge'])
 
 
 def prolong_rim_kernel(
@@ -594,7 +631,7 @@
         in_specs=[ANY] * outside + [VM] * inside + [SM] * scalars,
         out_specs=[VM] * len(outs),
         scratch_shapes=[x if not isinstance(x, tuple) else pltpu.VMEM(*x) for x in scratch],
-        compiler_params=pltpu.CompilerParams(vmem_limit_bytes=40 << 20),
+        compiler_params=pltpu.CompilerParams(vmem_limit_bytes=(56 if outside else 40) << 20),
         cost_estimate=pl.CostEstimate(flops=0, bytes_accessed=micros * 3600000, transcendentals=0),
         name=name,
     )(*args)

time: 179 us -> 170 us (0.950)
  Pallas kernels: 37.5 us -> 32.9 us
  local copies, waits for them, and re-layouts: 4.61 us -> 1.39 us
    pallas_call x9, Pallas kernels: 37.5 us -> 32.9 us  [call(): pl.pallas_call(kernel, out_shape=[jax.ShapeDtypeStruct(s, t) for s, t in...]
    unnamed x20 -> x22, local copies, waits for them, and re-layouts: 4.61 us -> 1.39 us
where the time goes in v4:
time: 170 us; the launch traced here: 169 us
  blocking collectives  114 us (67%)
  Pallas kernels  32.9 us (19%)
  starting transfers between devices  21 us (12%)
    all_to_all x4, blocking collectives, exchange(): return lax.all_to_all(x, 'dev', split_axis=0, concat_axis=0, tiled=True)  114 us
    pallas_call x9, Pallas kernels, call(): pl.pallas_call(kernel, out_shape=[jax.ShapeDtypeStruct(s, t) for s, t in...  32.9 us
    ppermute x1, starting transfers between devices, per_device(): after = lax.ppermute(low, axes, down)  7.38 us
    ppermute x1, starting transfers between devices, per_device(): from_after = lax.ppermute(low, axes, down)  6.15 us
    ppermute x1, starting transfers between devices, per_device(): before = lax.ppermute(high, axes, up)  3.83 us
    ppermute x1, starting transfers between devices, per_device(): from_before = lax.ppermute(high, axes, up)  3.64 us
  transfers between devices with their start and end apart: 4, of which 0 were waited for; matrix products, arithmetic and copies ran while one was open for 0% of the time, Pallas kernels for 4%

profile of v4, /device:TPU:16, one launch (start us, length us, event | category | flops | bytes accessed | tf_op | source)
XLA Modules:
  0.0 169.3 jit_solution(10985322364267042653)
XLA Ops:
  0.0 0.0 copy-start
  0.0 2.3 %index_prep.1 = (s32[72,128]{1,0:T(8,128)}, s32[32,128]{1,0:T(8,128)}, f32[32,128]{1,0:T(8,128)}, s32[32,128]{1,0:T(8,128)}, f32[16,768]{1,0:T(8,128)}, /*index=5*/f32[16,768]{1,0:T(8,128)}) custom-call(f32[16,5376]{1,0:T(8,128)} %res.3, s32[64,144]{1,0:T(8,128)} %bitcast.6, s32[64,64]{1,0:T(8,128)} %lm_in.1, s32[16,128]{1,0:T(8,128)} %bitcast.7, ...), custom_call_target="tpu_custom_call" | custom-call | bytes 7200000 | tf_op jit(solution)/shard_map/index_prep/pallas_call | solution.py:628
  2.3 3.8 %collective-permute-start = (f32[16,768]{1,0:T(8,128)}, f32[16,768]{1,0:T(8,128)S(1)}, u32[]{:S(2)}, u32[]{:S(2)}) collective-permute-start(f32[16,768]{1,0:T(8,128)} %get-tuple-element.19), channel_id=1, source_target_pairs={{0,1},{1,2},{2,3},{3,4},{4,5},{5,6},{6,7},{7,8},{8,9},{9,10},{10,1... | collective-permute-start | bytes 147464 | tf_op jit(solution)/shard_map/ppermute | solution.py:693
  6.1 7.4 %collective-permute-start.1 = (f32[16,768]{1,0:T(8,128)}, f32[16,768]{1,0:T(8,128)S(1)}, u32[]{:S(2)}, u32[]{:S(2)}) collective-permute-start(f32[16,768]{1,0:T(8,128)} %get-tuple-element.20), channel_id=1, source_target_pairs={{1,0},{2,1},{3,2},{4,3},{5,4},{6,5},{7,6},{8,7},{9,8},{10,9},{11,1... | collective-permute-start | bytes 147464 | tf_op jit(solution)/shard_map/ppermute | solution.py:694
  13.5 0.0 copy-done
  13.5 0.0 copy-start.2
  13.5 0.8 copy-done.2
  14.3 0.0 copy-start.1
  14.3 0.0 copy-start.4
  14.3 0.0 copy-start.5
  14.3 0.0 copy-start.6
  14.3 0.0 copy-start.7
  14.3 0.0 copy-start.8
  14.3 3.1 %own_edges.1.ev_own = f32[16,9216]{1,0:T(8,128)S(1)} custom-call(f32[16,5376]{1,0:T(8,128)S(1)} %copy-done, s32[72,128]{1,0:T(8,128)S(1)} %copy-done.2), custom_call_target="tpu_custom_call" | custom-call | bytes 14400000 | tf_op jit(solution)/shard_map/own_edges/pallas_call | solution.py:628
  17.4 0.0 copy-start.9
  17.5 0.0 collective-permute-done.before
  17.5 0.0 collective-permute-done.1.after
  17.5 0.0 copy-start.10
  17.5 0.0 copy-done.1
  17.5 0.0 copy-done.4
  17.5 0.0 copy-done.5
  17.5 0.0 copy-done.6
  17.5 0.0 copy-done.7
  17.5 0.0 copy-done.8
  17.5 0.6 copy-done.9
  18.1 0.0 copy-done.10
  18.1 4.7 %restrict.1 = f32[32,52,128]{2,1,0:T(8,128)S(1)} custom-call(f32[16,9216]{1,0:T(8,128)S(1)} %own_edges.1.ev_own, f32[16,768]{1,0:T(8,128)S(1)} %collective-permute-done.before, f32[16,768]{1,0:T(8,128)S(1)} %collective-permute-done.1.after, s32[72,128]{1,0:T(8,128)S(1)} %copy-done.2, s32[32,128]{1,0:T(8,128)S(1)} %copy-done.4, f32[32,128]{1,0:T(8,128)S(1)} %copy-done.8, ...), custom_call_target="tpu_custom_call" | custom-call | bytes 21600000 | tf_op jit(solution)/shard_map/restrict/pallas_call | solution.py:628
  22.9 32.5 %all_to_all.20.arrived = f32[32,52,128]{2,1,0:T(8,128)S(1)} all-to-all(f32[32,52,128]{2,1,0:T(8,128)S(1)} %restrict.1), channel_id=1, replica_groups=mesh['grp'=8,'dev'=32] {'dev'}, dimensions={0} | all-to-all | bytes 1703936 | tf_op jit(solution)/shard_map/all_to_all | solution.py:641
  55.4 3.4 %first_iter.1 = (f32[32,48,128]{2,1,0:T(8,128)S(1)}, f32[7,48,256]{2,1,0:T(8,128)S(1)}, f32[7,3,256]{2,1,0:T(4,128)S(1)}, s32[32,128]{1,0:T(8,128)S(1)}) custom-call(f32[32,52,128]{2,1,0:T(8,128)S(1)} %all_to_all.20.arrived), custom_call_target="tpu_custom_call" | custom-call | bytes 18000000 | tf_op jit(solution)/shard_map/first_iter/pallas_call | solution.py:628
  58.9 27.3 %all_to_all.21.arrived = f32[32,48,128]{2,1,0:T(8,128)S(1)} all-to-all(f32[32,48,128]{2,1,0:T(8,128)S(1)} %get-tuple-element.24), channel_id=1, replica_groups=mesh['grp'=8,'dev'=32] {'dev'}, dimensions={0} | all-to-all | bytes 1572864 | tf_op jit(solution)/shard_map/all_to_all | solution.py:641
  86.2 5.3 %operator.1 = f32[32,48,128]{2,1,0:T(8,128)S(1)} custom-call(f32[32,48,128]{2,1,0:T(8,128)S(1)} %all_to_all.21.arrived, s32[32,128]{1,0:T(8,128)S(1)} %copy-done.4, f32[64,64]{1,0:T(8,128)S(1)} %copy-done.6, f32[64,64]{1,0:T(8,128)S(1)} %copy-done.7, f32[6,64]{1,0:T(8,128)S(1)} %copy-done.9, f32[1,64]{1,0:T(1,128)S(1)} %bitcast.5, s32[32,128]{1,0:T(8,128)S(1)} %copy-done.5), custom_call_target="tpu_custom_call" | custom-call | bytes 28800000 | tf_op jit(solution)/shard_map/operator/pallas_call | solution.py:628
  91.5 27.0 %all_to_all.22.arrived = f32[32,48,128]{2,1,0:T(8,128)S(1)} all-to-all(f32[32,48,128]{2,1,0:T(8,128)S(1)} %operator.1), channel_id=1, replica_groups=mesh['grp'=8,'dev'=32] {'dev'}, dimensions={0} | all-to-all | bytes 1572864 | tf_op jit(solution)/shard_map/all_to_all | solution.py:641
  118.5 3.2 %second_iter.1 = f32[32,48,128]{2,1,0:T(8,128)S(1)} custom-call(f32[32,48,128]{2,1,0:T(8,128)S(1)} %all_to_all.22.arrived, f32[7,48,256]{2,1,0:T(8,128)S(1)} %get-tuple-element.25.rhs, f32[7,3,256]{2,1,0:T(4,128)S(1)} %get-tuple-element.26.floor, s32[32,128]{1,0:T(8,128)S(1)} %get-tuple-element.27.slots), custom_call_target="tpu_custom_call" | custom-call | bytes 18000000 | tf_op jit(solution)/shard_map/second_iter/pallas_call | solution.py:628
  121.8 0.0 copy-start.3
  121.8 26.9 %all_to_all.23.arrived = f32[32,48,128]{2,1,0:T(8,128)S(1)} all-to-all(f32[32,48,128]{2,1,0:T(8,128)S(1)} %second_iter.1), channel_id=1, replica_groups=mesh['grp'=8,'dev'=32] {'dev'}, dimensions={0} | all-to-all | bytes 1572864 | tf_op jit(solution)/shard_map/all_to_all | solution.py:641
  148.7 0.0 copy-done.3
  148.7 6.0 %prolong_rim.1 = (bf16[32,9216]{1,0:T(8,128)(2,1)S(1)}, f32[16,768]{1,0:T(8,128)S(1)}, f32[16,768]{1,0:T(8,128)S(1)}) custom-call(f32[32,48,128]{2,1,0:T(8,128)S(1)} %all_to_all.23.arrived, s32[32,128]{1,0:T(8,128)S(1)} %copy-done.4, s32[72,128]{1,0:T(8,128)S(1)} %copy-done.3, f32[144,192]{1,0:T(8,128)S(1)} %copy-done.1, s32[32,128]{1,0:T(8,128)S(1)} %copy-done.5), custom_call_target="tpu_custom_call" | custom-call | bytes 21600000 | tf_op jit(solution)/shard_map/prolong_rim/pallas_call | solution.py:628
  154.7 3.6 %collective-permute-start.2 = (f32[16,768]{1,0:T(8,128)S(1)}, f32[16,768]{1,0:T(8,128)S(1)}, u32[]{:S(2)}, u32[]{:S(2)}) collective-permute-start(f32[16,768]{1,0:T(8,128)S(1)} %get-tuple-element.29), channel_id=1, source_target_pairs={{0,1},{1,2},{2,3},{3,4},{4,5},{5,6},{6,7},{7,8},{8,9},{9,10},{10,1... | collective-permute-start | bytes 147464 | tf_op jit(solution)/shard_map/ppermute | solution.py:774
  158.4 6.1 %collective-permute-start.3 = (f32[16,768]{1,0:T(8,128)S(1)}, f32[16,768]{1,0:T(8,128)S(1)}, u32[]{:S(2)}, u32[]{:S(2)}) collective-permute-start(f32[16,768]{1,0:T(8,128)S(1)} %get-tuple-element.30), channel_id=1, source_target_pairs={{1,0},{2,1},{3,2},{4,3},{5,4},{6,5},{7,6},{8,7},{9,8},{10,9},{11,1... | collective-permute-start | bytes 147464 | tf_op jit(solution)/shard_map/ppermute | solution.py:775
  164.5 4.0 %prolong_own.1.own = f32[16,5376]{1,0:T(8,128)S(1)} custom-call(bf16[32,9216]{1,0:T(8,128)(2,1)S(1)} %get-tuple-element.28.terms, s32[72,128]{1,0:T(8,128)S(1)} %copy-done.3), custom_call_target="tpu_custom_call" | custom-call | bytes 18000000 | tf_op jit(solution)/shard_map/prolong_own/pallas_call | solution.py:628
  168.5 0.0 collective-permute-done.2.before
  168.5 0.0 collective-permute-done.3.after
  168.6 0.8 finish.1
Async XLA Ops:
  0.0 13.5 %copy-start = (f32[16,5376]{1,0:T(8,128)S(1)}, f32[16,5376]{1,0:T(8,128)}, u32[]{:S(2)}) copy-start(f32[16,5376]{1,0:T(8,128)} %res.3) | copy-start | bytes 1032196
  2.3 15.2 %collective-permute-start = (f32[16,768]{1,0:T(8,128)}, f32[16,768]{1,0:T(8,128)S(1)}, u32[]{:S(2)}, u32[]{:S(2)}) collective-permute-start(f32[16,768]{1,0:T(8,128)} %get-tuple-element.19), channel_id=1, source_target_pairs={{0,1},{1,2},{2,3},{3,4},{4,5},{5,6},{6,7},{7,8},{8,9},{9,10},{10,1... | collective-permute-start | bytes 147464 | tf_op jit(solution)/shard_map/ppermute | solution.py:693
  6.1 11.4 %collective-permute-start.1 = (f32[16,768]{1,0:T(8,128)}, f32[16,768]{1,0:T(8,128)S(1)}, u32[]{:S(2)}, u32[]{:S(2)}) collective-permute-start(f32[16,768]{1,0:T(8,128)} %get-tuple-element.20), channel_id=1, source_target_pairs={{1,0},{2,1},{3,2},{4,3},{5,4},{6,5},{7,6},{8,7},{9,8},{10,9},{11,1... | collective-permute-start | bytes 147464 | tf_op jit(solution)/shard_map/ppermute | solution.py:694
  13.5 0.8 copy-start.2
  14.3 3.2 %copy-start.1 = (f32[144,192]{1,0:T(8,128)S(1)}, f32[144,192]{1,0:T(8,128)}, u32[]{:S(2)}) copy-start(f32[144,192]{1,0:T(8,128)} %pi.3) | copy-start | bytes 331780
  14.3 3.2 %copy-start.4 = (s32[32,128]{1,0:T(8,128)S(1)}, s32[32,128]{1,0:T(8,128)}, u32[]{:S(2)}) copy-start(s32[32,128]{1,0:T(8,128)} %get-tuple-element.21.pos) | copy-start | bytes 49156
  14.3 3.2 %copy-start.5 = (s32[32,128]{1,0:T(8,128)S(1)}, s32[32,128]{1,0:T(8,128)}, u32[]{:S(2)}) copy-start(s32[32,128]{1,0:T(8,128)} %get-tuple-element.23.starts_in.starts) | copy-start | bytes 49156
  14.3 3.2 %copy-start.6 = (f32[64,64]{1,0:T(8,128)S(1)}, f32[64,64]{1,0:T(8,128)}, u32[]{:S(2)}) copy-start(f32[64,64]{1,0:T(8,128)} %stiff.3) | copy-start | bytes 49156
  14.3 3.2 %copy-start.7 = (f32[64,64]{1,0:T(8,128)S(1)}, f32[64,64]{1,0:T(8,128)}, u32[]{:S(2)}) copy-start(f32[64,64]{1,0:T(8,128)} %mass.3) | copy-start | bytes 49156
  14.3 3.2 %copy-start.8 = (f32[32,128]{1,0:T(8,128)S(1)}, f32[32,128]{1,0:T(8,128)}, u32[]{:S(2)}) copy-start(f32[32,128]{1,0:T(8,128)} %get-tuple-element.22.slots) | copy-start | bytes 49156
  17.4 0.7 copy-start.9
  17.5 0.7 copy-start.10
  121.8 27.0 %copy-start.3 = (s32[72,128]{1,0:T(8,128)S(1)}, s32[72,128]{1,0:T(8,128)}, u32[]{:S(2)}) copy-start(s32[72,128]{1,0:T(8,128)} %get-tuple-element.18.epos) | copy-start | bytes 110596
  154.7 13.8 %collective-permute-start.2 = (f32[16,768]{1,0:T(8,128)S(1)}, f32[16,768]{1,0:T(8,128)S(1)}, u32[]{:S(2)}, u32[]{:S(2)}) collective-permute-start(f32[16,768]{1,0:T(8,128)S(1)} %get-tuple-element.29), channel_id=1, source_target_pairs={{0,1},{1,2},{2,3},{3,4},{4,5},{5,6},{6,7},{7,8},{8,9},{9,10},{10,1... | collective-permute-start | bytes 147464 | tf_op jit(solution)/shard_map/ppermute | solution.py:774
  158.4 10.2 %collective-permute-start.3 = (f32[16,768]{1,0:T(8,128)S(1)}, f32[16,768]{1,0:T(8,128)S(1)}, u32[]{:S(2)}, u32[]{:S(2)}) collective-permute-start(f32[16,768]{1,0:T(8,128)S(1)} %get-tuple-element.30), channel_id=1, source_target_pairs={{1,0},{2,1},{3,2},{4,3},{5,4},{6,5},{7,6},{8,7},{9,8},{10,9},{11,1... | collective-permute-start | bytes 147464 | tf_op jit(solution)/shard_map/ppermute | solution.py:775

commit v5 on v4

--- a/solution.py
+++ b/solution.py
@@ -29,6 +29,7 @@
 H_NODE = 7
 TAIL = 4
 TAIL_H = TAIL // 2
+OWN_TAIL = 14
 GATHER_STEP = 1024
 GATHER_ROWS = GATHER_STEP // LANE
 E_TILES = 72
@@ -81,7 +82,7 @@
     return jnp.where(here, jnp.ones(shape, BF), jnp.zeros(shape, BF))
 
 
-def gather_tile(table, index_rows, rows, count, tail):
+def gather_tile(table, index_rows, rows, count, tail, tail_count=TAIL):
     found = jnp.dot(table, one_hot_low(index_rows), preferred_element_type=F32)
     high = spread(index_rows >> 8, 2 * rows)
     out = found[: 2 * rows]
@@ -92,7 +93,7 @@
     for i in range(index_rows.shape[0]):
         index = jnp.broadcast_to(index_rows[i : i + 1], (rows, LANE))
         part = out[:, i * LANE : (i + 1) * LANE]
-        for k in range(TAIL):
+        for k in range(tail_count):
             picked = jnp.take_along_axis(tail(k), index & (LANE - 1), axis=1)
             part = jnp.where((index >> 7) == 2 * count + k, picked, part)
         tiles.append(part)
@@ -244,8 +245,20 @@
     pos_out[...] = pos
 
 
-def own_edges_kernel(res, epos, ev_out, table):
-    count = H_OWN - TAIL_H
+def own_edges_kernel(res, epos, pi, stiff, mass, perm, curl, ev_out, w, wide, diag, coef, table):
+    fill_pi(w, pi)
+    fill_coefs(coef, wide, perm, curl)
+    eye = iota((NN, NN), 0) == iota((NN, NN), 1)
+
+    def diagonal(ref):
+        d = jnp.sum(jnp.where(eye, ref[...], 0.0), axis=0, keepdims=True)
+        return jnp.concatenate([d, d], axis=1)
+
+    sd, md = diagonal(stiff), diagonal(mass)
+    for t in range(N_TILES):
+        at = cols_of(t, LANE)
+        diag[:, at] = wide[6:7, at] * sd + md * wide[0:3, at]
+    count = H_OWN - OWN_TAIL // 2
     fill_table(table, lambda h: res[:, cols_of(h, WIDE)], RHS, count)
     for step in range(E_TILES * LANE // GATHER_STEP):
         ev_out[:, cols_of(step, GATHER_STEP)] = gather_tile(
@@ -254,23 +267,24 @@
             RHS,
             count,
             lambda k: res[:, cols_of(2 * count + k, LANE)],
+            OWN_TAIL,
         )
 
 
 def fill_pi(w, pi):
-    zero = jnp.zeros((384, 384), BF)
-    for v in range(4):
-        for k in (0, 1):
-            w[v, k] = zero
-    for c in range(3):
-        part = split(pi[:, c * NN : (c + 1) * NN])
-        for k in (0, 1):
-            for e2 in (0, 1):
-                cols = slice(c * LANE + e2 * NN, c * LANE + (e2 + 1) * NN)
-                for v in range(4):
-                    w[v, k, e2 * LANE : (e2 + 1) * LANE, cols] = part[k][:LANE]
-                    at = 2 * LANE + (2 * v + e2) * 16
-                    w[v, k, at : at + 16, cols] = part[k][LANE:]
+    for k, part in enumerate(split(pi[...])):
+        w[k, :LANE, :] = part[:LANE]
+        for i in range(8):
+            w[k, LANE + 16 * i : LANE + 16 * (i + 1), :] = part[LANE:]
+
+
+def three_terms(x, product):
+    high, low = split(x)
+    both = product(jnp.concatenate([high, low], axis=0), 0)
+    return both[: x.shape[0]] + both[x.shape[0] :] + product(high, 1)
+
+
+PI_STEP = 16
 
 
 def fill_coefs(coef, wide, perm, curl):
@@ -321,8 +335,8 @@
 
 
 def restrict_kernel(
-    ev_own, before, after, epos, pos, slots, pi, stiff, mass, perm, curl, starts_in,
-    out, starts, sem, table, ev, w, coef, wide, xs, diag, left, acc, compact,
+    ev_own, before, after, epos, pos, slots, w, diag, starts_in,
+    out, starts, sem, table, ev, xs, left, acc, compact,
 ):
     move = pltpu.make_async_copy(starts_in, starts, sem)
     move.start()
@@ -342,42 +356,32 @@
         ev[:, at] = jnp.where(spread(idx, RHS) >= 0, found, ev_own[:, at])
 
     over(E_TILES // GATHER_ROWS, step_body, LOOP['rim'])
-    fill_pi(w, pi)
-    for v in range(4):
+    group = iota((RHS, LANE), 1) >> 4
+    for step in range(EL // PI_STEP):
         blocks = []
-        for g in range(8):
-            t = 4 * g + v
+        for e in range(step * PI_STEP, (step + 1) * PI_STEP):
+            rest = ev[:, cols_of(EL + e // 8, LANE)]
             blocks.append(
                 jnp.concatenate(
-                    [ev[:, 2 * t * LANE : (2 * t + 2) * LANE], ev[:, (EL + g) * LANE : (EL + g + 1) * LANE]],
-                    axis=1,
+                    [ev[:, cols_of(e, LANE)], jnp.where(group == e % 8, rest, 0.0)], axis=1
                 )
             )
-        high, low = split(jnp.concatenate(blocks, axis=0))
-        y = (
-            jnp.dot(high, w[v, 0], preferred_element_type=F32)
-            + jnp.dot(high, w[v, 1], preferred_element_type=F32)
-            + jnp.dot(low, w[v, 0], preferred_element_type=F32)
-        )
-        for g in range(8):
-            t = 4 * g + v
-            xs[:, t * LANE : (t + 1) * LANE] = stack(
+        y = three_terms(
+            jnp.concatenate(blocks, axis=0),
+            lambda x, k: jnp.dot(x, w[k], preferred_element_type=F32),
+        )
+        for t in range(PI_STEP // 2):
+            even = y[2 * t * RHS : (2 * t + 1) * RHS]
+            odd = y[(2 * t + 1) * RHS : (2 * t + 2) * RHS]
+            xs[:, cols_of(step * PI_STEP // 2 + t, LANE)] = stack(
                 jnp.concatenate(
-                    [y[g * RHS : (g + 1) * RHS, c * LANE : (c + 1) * LANE] for c in range(3)], axis=0
+                    [
+                        jnp.concatenate([even[:, cols_of(c, NN)], odd[:, cols_of(c, NN)]], axis=1)
+                        for c in range(3)
+                    ],
+                    axis=0,
                 )
             )
-    fill_coefs(coef, wide, perm, curl)
-    eye = iota((NN, NN), 0) == iota((NN, NN), 1)
-
-    def diagonal(ref):
-        d = jnp.sum(jnp.where(eye, ref[...], 0.0), axis=0, keepdims=True)
-        return jnp.concatenate([d, d], axis=1)
-
-    sd, md = diagonal(stiff), diagonal(mass)
-    for t in range(N_TILES):
-        at = slice(t * LANE, (t + 1) * LANE)
-        diag[:, at] = wide[6:7, at] * sd + md * wide[0:3, at]
-
     def step_body(step):
         at = cols_of(step, NODE_STEP)
         idx = pos[rows_of(step, NODE_ROWS), :]
@@ -495,18 +499,15 @@
     )
 
 
-def apply_kernel(
-    arrived, pos, stiff, mass, perm, curl, starts, out, table, op, coef, wide, xs, left, acc, compact
-):
+def apply_kernel(arrived, pos, stiff, mass, wide, starts, out, table, op, xs, left, acc, compact):
     touched_table(table, compact, arrived, starts)
-    fill_coefs(coef, wide, perm, curl)
-    op[...] = jnp.zeros((2, LANE, 2 * LANE), BF)
+    op[...] = jnp.zeros((3, LANE, 2 * LANE), BF)
     for m, ref in enumerate((stiff, mass)):
         part = split(ref[...].T)
-        for k in (0, 1):
+        for k in (0, 1, 2):
             for e2 in (0, 1):
                 at = slice(m * LANE + e2 * NN, m * LANE + (e2 + 1) * NN)
-                op[k, e2 * NN : (e2 + 1) * NN, at] = part[k]
+                op[k, e2 * NN : (e2 + 1) * NN, at] = part[k // 2]
 
     tensor = ((0, 3, 4), (3, 1, 5), (4, 5, 2))
     def step_body(step):
@@ -514,11 +515,11 @@
         high, low = split(
             jnp.concatenate([values[:, cols_of(i, LANE)] for i in range(GATHER_ROWS)], axis=0)
         )
-        y = (
-            jnp.dot(high, op[0], preferred_element_type=F32)
-            + jnp.dot(high, op[1], preferred_element_type=F32)
-            + jnp.dot(low, op[0], preferred_element_type=F32)
-        )
+        y = jnp.dot(
+            jnp.concatenate([high, low], axis=1),
+            jnp.concatenate([op[0], op[1]], axis=0),
+            preferred_element_type=F32,
+        ) + jnp.dot(high, op[2], preferred_element_type=F32)
         cols = wide[:, cols_of(step, GATHER_STEP)]
         tiles = []
         for i in range(GATHER_ROWS):
@@ -552,35 +553,31 @@
     expand(out, compact, starts, ROWS)
 
 
-def edge_terms(arrived, pos, pi, starts, terms, table, w, values, compact):
+def edge_terms(arrived, pos, w, starts, terms, table, values, compact):
     touched_table(table, compact, arrived, starts)
-    fill_pi(w, pi)
 
     def step_body(step):
         values[:, cols_of(step, GATHER_STEP)] = touched_tile(table, compact, pos, step)
 
     over(ELN // GATHER_STEP, step_body, LOOP['tile'])
-    dims = (((1,), (1,)), ((), ()))
-    rest = None
-    for v in range(4):
+    group = iota((RHS, LANE), 1) >> 4
+    rest = [jnp.zeros((RHS, LANE), F32)] * 8
+    for step in range(EL // PI_STEP):
         blocks = []
-        for g in range(8):
-            at = slice((4 * g + v) * LANE, (4 * g + v + 1) * LANE)
-            blocks.append(
-                jnp.concatenate([values[c * RHS : (c + 1) * RHS, at] for c in range(3)], axis=1)
-            )
-        high, low = split(jnp.concatenate(blocks, axis=0))
-        y = (
-            lax.dot_general(high, w[v, 0], dims, preferred_element_type=F32)
-            + lax.dot_general(high, w[v, 1], dims, preferred_element_type=F32)
-            + lax.dot_general(low, w[v, 0], dims, preferred_element_type=F32)
-        )
-        for g in range(8):
-            t = 4 * g + v
-            terms[:, 2 * t * LANE : (2 * t + 2) * LANE] = stack(y[g * RHS : (g + 1) * RHS, : 2 * LANE])
-        rest = y[:, 2 * LANE :] if rest is None else rest + y[:, 2 * LANE :]
+        for e in range(step * PI_STEP, (step + 1) * PI_STEP):
+            at = cols_of(e, NN)
+            blocks.append(jnp.concatenate([values[cols_of(c, RHS), at] for c in range(3)], axis=1))
+        y = three_terms(
+            jnp.concatenate(blocks, axis=0),
+            lambda x, k: lax.dot_general(x, w[k], (((1,), (1,)), ((), ())), preferred_element_type=F32),
+        )
+        for i in range(PI_STEP):
+            e = step * PI_STEP + i
+            part = y[cols_of(i, RHS)]
+            terms[:, cols_of(e, LANE)] = stack(part[:, :LANE])
+            rest[e // 8] = jnp.where(group == e % 8, part[:, LANE:], rest[e // 8])
     for g in range(8):
-        terms[:, (EL + g) * LANE : (EL + g + 1) * LANE] = stack(rest[g * RHS : (g + 1) * RHS])
+        terms[:, cols_of(EL + g, LANE)] = stack(rest[g])
 
 
 def edge_scatter(terms, epos, left, acc, first, count):
@@ -594,9 +591,9 @@
 
 
 def prolong_rim_kernel(
-    arrived, pos, epos, pi, starts, terms, low_out, high_out, table, w, values, compact, left, acc
+    arrived, pos, epos, w, starts, terms, low_out, high_out, table, values, compact, left, acc
 ):
-    edge_terms(arrived, pos, pi, starts, terms, table, w, values, compact)
+    edge_terms(arrived, pos, w, starts, terms, table, values, compact)
     edge_scatter(terms, epos, left, acc, H_OWN, 2 * H_RIM)
     for h in range(H_RIM):
         at = slice(h * WIDE, (h + 1) * WIDE)
@@ -693,11 +690,14 @@
     before = lax.ppermute(high, axes, up)
     after = lax.ppermute(low, axes, down)
     edge_rows = ((RHS, E_TILES * LANE), F32)
-    (ev_own,) = call(
-        own_edges_kernel, "own_edges", 4, [edge_rows], [(((H_OWN - TAIL_H) * 2 * RHS, WIDE), BF)], residual_edges, epos
-    )
-    pi_scratch = ((4, 2, 384, 384), BF)
-    coefs = [((8, LANE), F32), ((8, ELN), F32)]
+    ev_own, w, wide, diag = call(
+        own_edges_kernel,
+        "own_edges",
+        4,
+        [edge_rows, ((2, WIDE, 3 * NN), BF), ((8, ELN), F32), ((3, ELN), F32)],
+        [((8, LANE), F32), (((H_OWN - OWN_TAIL // 2) * 2 * RHS, WIDE), BF)],
+        residual_edges, epos, pi_block, stiff_block, mass_block, permittivity, curl,
+    )
     served = ((PEERS, ROWS, CAP), F32)
     compact = ((ROWS, U_LOC + 2 * LANE), F32)
     (packed,) = call(
@@ -710,15 +710,12 @@
             pltpu.SemaphoreType.DMA,
             (((2 * H_RIM - TAIL_H) * 2 * RHS, WIDE), BF),
             edge_rows,
-            pi_scratch,
-            *coefs,
             ((PAIR, ELN), BF),
-            ((3, ELN), F32),
             ((BUFFERS, H_POS * PAIR + 96, NODE_STEP), BF),
             ((H_POS * PAIR + 96, WIDE), F32),
             ((SENT + 4, U_LOC + 2 * LANE), F32),
         ],
-        ev_own, before, after, epos, pos, slot_rows, pi_block, stiff_block, mass_block, permittivity, curl, starts,
+        ev_own, before, after, epos, pos, slot_rows, w, diag, starts,
     )
     served_scratch = [(((H_NODE - TAIL_H) * PAIR, WIDE), BF), ((ROWS, TAIL_H * WIDE), F32)]
     wanted, rhs, floor, slots = call(
@@ -737,14 +734,13 @@
         [served],
         [
             position_table,
-            ((2, LANE, 2 * LANE), BF),
-            *coefs,
+            ((3, LANE, 2 * LANE), BF),
             ((PAIR, ELN), BF),
             ((BUFFERS, H_POS * PAIR, NODE_STEP), BF),
             ((H_POS * PAIR, WIDE), F32),
             compact,
         ],
-        exchange(wanted), pos, stiff_block, mass_block, permittivity, curl, starts,
+        exchange(wanted), pos, stiff_block, mass_block, wide, starts,
         scalars=1,
     )
     (wanted,) = call(
@@ -762,13 +758,12 @@
         [((2 * RHS, E_TILES * LANE), BF), rim, rim],
         [
             position_table,
-            pi_scratch,
             ((ROWS, ELN), F32),
             compact,
             ((BUFFERS, 2 * H_RIM * 2 * RHS, EDGE_STEP), BF),
             ((2 * H_RIM * 2 * RHS, WIDE), F32),
         ],
-        exchange(wanted), pos, epos, pi_block, starts,
+        exchange(wanted), pos, epos, w, starts,
         scalars=1,
     )
     from_before = lax.ppermute(high, axes, up)

time: 170 us -> 169 us (level)
  Pallas kernels: 32.9 us -> 30.7 us
    pallas_call x9, Pallas kernels: 32.9 us -> 30.7 us  [call(): pl.pallas_call(kernel, out_shape=[jax.ShapeDtypeStruct(s, t) for s, t in...]
where the time goes in v5:
time: 169 us; the launch traced here: 168 us
  blocking collectives  114 us (67%)
  Pallas kernels  30.7 us (18%)
  starting transfers between devices  21 us (12%)
  local copies, waits for them, and re-layouts  2.32 us (1%)
    all_to_all x4, blocking collectives, exchange(): return lax.all_to_all(x, 'dev', split_axis=0, concat_axis=0, tiled=True)  114 us
    pallas_call x9, Pallas kernels, call(): pl.pallas_call(kernel, out_shape=[jax.ShapeDtypeStruct(s, t) for s, t in...  30.7 us
    ppermute x1, starting transfers between devices, per_device(): after = lax.ppermute(low, axes, down)  7.38 us
    ppermute x1, starting transfers between devices, per_device(): from_after = lax.ppermute(low, axes, down)  6.16 us
    ppermute x1, starting transfers between devices, per_device(): before = lax.ppermute(high, axes, up)  3.83 us
    ppermute x1, starting transfers between devices, per_device(): from_before = lax.ppermute(high, axes, up)  3.62 us
  transfers between devices with their start and end apart: 4, of which 0 were waited for; matrix products, arithmetic and copies ran while one was open for 0% of the time, Pallas kernels for 4%

profile of v5, /device:TPU:16, one launch (start us, length us, event | category | flops | bytes accessed | tf_op | source)
XLA Modules:
  0.0 168.1 jit_solution(4884685396855696080)
XLA Ops:
  0.0 0.0 copy-start
  0.0 0.0 copy-start.6
  0.0 0.0 copy-start.7
  0.0 2.3 %index_prep.1 = (s32[72,128]{1,0:T(8,128)}, s32[32,128]{1,0:T(8,128)}, f32[32,128]{1,0:T(8,128)}, s32[32,128]{1,0:T(8,128)}, f32[16,768]{1,0:T(8,128)}, /*index=5*/f32[16,768]{1,0:T(8,128)}) custom-call(f32[16,5376]{1,0:T(8,128)} %res.3, s32[64,144]{1,0:T(8,128)} %bitcast.5, s32[64,64]{1,0:T(8,128)} %lm_in.1, s32[16,128]{1,0:T(8,128)} %bitcast.6, ...), custom_call_target="tpu_custom_call" | custom-call | bytes 7200000 | tf_op jit(solution)/shard_map/index_prep/pallas_call | solution.py:625
  2.3 0.0 copy-start.9
  2.3 3.8 %collective-permute-start = (f32[16,768]{1,0:T(8,128)}, f32[16,768]{1,0:T(8,128)S(1)}, u32[]{:S(2)}, u32[]{:S(2)}) collective-permute-start(f32[16,768]{1,0:T(8,128)} %get-tuple-element.24), channel_id=1, source_target_pairs={{0,1},{1,2},{2,3},{3,4},{4,5},{5,6},{6,7},{7,8},{8,9},{9,10},{10,1... | collective-permute-start | bytes 147464 | tf_op jit(solution)/shard_map/ppermute | solution.py:690
  6.1 7.4 %collective-permute-start.1 = (f32[16,768]{1,0:T(8,128)}, f32[16,768]{1,0:T(8,128)S(1)}, u32[]{:S(2)}, u32[]{:S(2)}) collective-permute-start(f32[16,768]{1,0:T(8,128)} %get-tuple-element.25), channel_id=1, source_target_pairs={{1,0},{2,1},{3,2},{4,3},{5,4},{6,5},{7,6},{8,7},{9,8},{10,9},{11,1... | collective-permute-start | bytes 147464 | tf_op jit(solution)/shard_map/ppermute | solution.py:691
  13.5 0.0 copy-start.10
  13.5 0.0 copy-done
  13.5 0.0 copy-done.6
  13.6 0.0 copy-done.7
  13.6 0.0 copy-done.9
  13.6 0.6 copy-done.10
  14.2 0.0 copy-start.1
  14.2 0.8 copy-done.1
  14.9 0.0 copy-start.5
  14.9 0.9 copy-done.5
  15.9 0.0 copy-start.3
  15.9 0.0 copy-start.4
  15.9 0.0 copy-start.8
  15.9 2.7 %own_edges.1 = (f32[16,9216]{1,0:T(8,128)S(1)}, bf16[2,256,192]{2,1,0:T(8,128)(2,1)S(1)}, f32[8,4096]{1,0:T(8,128)S(1)}, f32[3,4096]{1,0:T(4,128)S(1)}) custom-call(f32[16,5376]{1,0:T(8,128)S(1)} %copy-done, s32[72,128]{1,0:T(8,128)S(1)} %copy-done.1, f32[144,192]{1,0:T(8,128)S(1)} %copy-done.5, f32[64,64]{1,0:T(8,128)S(1)} %copy-done.6, ...), custom_call_target="tpu_custom_call" | custom-call | bytes 14400000 | tf_op jit(solution)/shard_map/own_edges/pallas_call | solution.py:625
  18.5 0.0 collective-permute-done.before
  18.5 0.0 collective-permute-done.1.after
  18.6 0.0 copy-done.3
  18.6 0.0 copy-done.4
  18.6 0.0 copy-done.8
  18.6 3.9 %restrict.1 = f32[32,52,128]{2,1,0:T(8,128)S(1)} custom-call(f32[16,9216]{1,0:T(8,128)S(1)} %get-tuple-element.23.ev_own, f32[16,768]{1,0:T(8,128)S(1)} %collective-permute-done.before, f32[16,768]{1,0:T(8,128)S(1)} %collective-permute-done.1.after, s32[72,128]{1,0:T(8,128)S(1)} %copy-done.1, s32[32,128]{1,0:T(8,128)S(1)} %copy-done.3, ...), custom_call_target="tpu_custom_call" | custom-call | bytes 21600000 | tf_op jit(solution)/shard_map/restrict/pallas_call | solution.py:625
  22.5 32.5 %all_to_all.20.arrived = f32[32,52,128]{2,1,0:T(8,128)S(1)} all-to-all(f32[32,52,128]{2,1,0:T(8,128)S(1)} %restrict.1), channel_id=1, replica_groups=mesh['grp'=8,'dev'=32] {'dev'}, dimensions={0} | all-to-all | bytes 1703936 | tf_op jit(solution)/shard_map/all_to_all | solution.py:638
  55.1 3.4 %first_iter.1 = (f32[32,48,128]{2,1,0:T(8,128)S(1)}, f32[7,48,256]{2,1,0:T(8,128)S(1)}, f32[7,3,256]{2,1,0:T(4,128)S(1)}, s32[32,128]{1,0:T(8,128)S(1)}) custom-call(f32[32,52,128]{2,1,0:T(8,128)S(1)} %all_to_all.20.arrived), custom_call_target="tpu_custom_call" | custom-call | bytes 18000000 | tf_op jit(solution)/shard_map/first_iter/pallas_call | solution.py:625
  58.5 27.4 %all_to_all.21.arrived = f32[32,48,128]{2,1,0:T(8,128)S(1)} all-to-all(f32[32,48,128]{2,1,0:T(8,128)S(1)} %get-tuple-element.31), channel_id=1, replica_groups=mesh['grp'=8,'dev'=32] {'dev'}, dimensions={0} | all-to-all | bytes 1572864 | tf_op jit(solution)/shard_map/all_to_all | solution.py:638
  85.9 5.5 %operator.1 = f32[32,48,128]{2,1,0:T(8,128)S(1)} custom-call(f32[32,48,128]{2,1,0:T(8,128)S(1)} %all_to_all.21.arrived, s32[32,128]{1,0:T(8,128)S(1)} %copy-done.3, f32[64,64]{1,0:T(8,128)S(1)} %copy-done.6, f32[64,64]{1,0:T(8,128)S(1)} %copy-done.7, f32[8,4096]{1,0:T(8,128)S(1)} %get-tuple-element.32.wide, s32[32,128]{1,0:T(8,128)S(1)} %copy-done.4), custom_call_target="tpu_custom_call" | custom-call | bytes 28800000 | tf_op jit(solution)/shard_map/operator/pallas_call | solution.py:625
  91.3 27.0 %all_to_all.22.arrived = f32[32,48,128]{2,1,0:T(8,128)S(1)} all-to-all(f32[32,48,128]{2,1,0:T(8,128)S(1)} %operator.1), channel_id=1, replica_groups=mesh['grp'=8,'dev'=32] {'dev'}, dimensions={0} | all-to-all | bytes 1572864 | tf_op jit(solution)/shard_map/all_to_all | solution.py:638
  118.3 3.2 %second_iter.1 = f32[32,48,128]{2,1,0:T(8,128)S(1)} custom-call(f32[32,48,128]{2,1,0:T(8,128)S(1)} %all_to_all.22.arrived, f32[7,48,256]{2,1,0:T(8,128)S(1)} %get-tuple-element.33.rhs, f32[7,3,256]{2,1,0:T(4,128)S(1)} %get-tuple-element.34.floor, s32[32,128]{1,0:T(8,128)S(1)} %get-tuple-element.35.slots), custom_call_target="tpu_custom_call" | custom-call | bytes 18000000 | tf_op jit(solution)/shard_map/second_iter/pallas_call | solution.py:625
  121.6 0.0 copy-start.2
  121.6 26.9 %all_to_all.23.arrived = f32[32,48,128]{2,1,0:T(8,128)S(1)} all-to-all(f32[32,48,128]{2,1,0:T(8,128)S(1)} %second_iter.1), channel_id=1, replica_groups=mesh['grp'=8,'dev'=32] {'dev'}, dimensions={0} | all-to-all | bytes 1572864 | tf_op jit(solution)/shard_map/all_to_all | solution.py:638
  148.5 0.0 copy-done.2
  148.5 5.0 %prolong_rim.1 = (bf16[32,9216]{1,0:T(8,128)(2,1)S(1)}, f32[16,768]{1,0:T(8,128)S(1)}, f32[16,768]{1,0:T(8,128)S(1)}) custom-call(f32[32,48,128]{2,1,0:T(8,128)S(1)} %all_to_all.23.arrived, s32[32,128]{1,0:T(8,128)S(1)} %copy-done.3, s32[72,128]{1,0:T(8,128)S(1)} %copy-done.2, bf16[2,256,192]{2,1,0:T(8,128)(2,1)S(1)} %get-tuple-element.28.w, ...), custom_call_target="tpu_custom_call" | custom-call | bytes 21600000 | tf_op jit(solution)/shard_map/prolong_rim/pallas_call | solution.py:625
  153.5 3.6 %collective-permute-start.2 = (f32[16,768]{1,0:T(8,128)S(1)}, f32[16,768]{1,0:T(8,128)S(1)}, u32[]{:S(2)}, u32[]{:S(2)}) collective-permute-start(f32[16,768]{1,0:T(8,128)S(1)} %get-tuple-element.37), channel_id=1, source_target_pairs={{0,1},{1,2},{2,3},{3,4},{4,5},{5,6},{6,7},{7,8},{8,9},{9,10},{10,1... | collective-permute-start | bytes 147464 | tf_op jit(solution)/shard_map/ppermute | solution.py:769
  157.1 6.2 %collective-permute-start.3 = (f32[16,768]{1,0:T(8,128)S(1)}, f32[16,768]{1,0:T(8,128)S(1)}, u32[]{:S(2)}, u32[]{:S(2)}) collective-permute-start(f32[16,768]{1,0:T(8,128)S(1)} %get-tuple-element.38), channel_id=1, source_target_pairs={{1,0},{2,1},{3,2},{4,3},{5,4},{6,5},{7,6},{8,7},{9,8},{10,9},{11,1... | collective-permute-start | bytes 147464 | tf_op jit(solution)/shard_map/ppermute | solution.py:770
  163.3 4.0 %prolong_own.1.own = f32[16,5376]{1,0:T(8,128)S(1)} custom-call(bf16[32,9216]{1,0:T(8,128)(2,1)S(1)} %get-tuple-element.36.terms, s32[72,128]{1,0:T(8,128)S(1)} %copy-done.2), custom_call_target="tpu_custom_call" | custom-call | bytes 18000000 | tf_op jit(solution)/shard_map/prolong_own/pallas_call | solution.py:625
  167.3 0.0 collective-permute-done.2.before
  167.3 0.0 collective-permute-done.3.after
  167.3 0.8 finish.1
Async XLA Ops:
  0.0 13.5 %copy-start = (f32[16,5376]{1,0:T(8,128)S(1)}, f32[16,5376]{1,0:T(8,128)}, u32[]{:S(2)}) copy-start(f32[16,5376]{1,0:T(8,128)} %res.3) | copy-start | bytes 1032196
  0.0 13.5 %copy-start.6 = (f32[64,64]{1,0:T(8,128)S(1)}, f32[64,64]{1,0:T(8,128)}, u32[]{:S(2)}) copy-start(f32[64,64]{1,0:T(8,128)} %stiff.3) | copy-start | bytes 49156
  0.0 13.5 %copy-start.7 = (f32[64,64]{1,0:T(8,128)S(1)}, f32[64,64]{1,0:T(8,128)}, u32[]{:S(2)}) copy-start(f32[64,64]{1,0:T(8,128)} %mass.3) | copy-start | bytes 49156
  2.3 11.3 %copy-start.9 = (f32[6,64]{1,0:T(8,128)S(1)}, f32[6,64]{1,0:T(8,128)}, u32[]{:S(2)}) copy-start(f32[6,64]{1,0:T(8,128)} %perm.1) | copy-start | bytes 4612
  2.3 16.2 %collective-permute-start = (f32[16,768]{1,0:T(8,128)}, f32[16,768]{1,0:T(8,128)S(1)}, u32[]{:S(2)}, u32[]{:S(2)}) collective-permute-start(f32[16,768]{1,0:T(8,128)} %get-tuple-element.24), channel_id=1, source_target_pairs={{0,1},{1,2},{2,3},{3,4},{4,5},{5,6},{6,7},{7,8},{8,9},{9,10},{10,1... | collective-permute-start | bytes 147464 | tf_op jit(solution)/shard_map/ppermute | solution.py:690
  6.1 12.4 %collective-permute-start.1 = (f32[16,768]{1,0:T(8,128)}, f32[16,768]{1,0:T(8,128)S(1)}, u32[]{:S(2)}, u32[]{:S(2)}) collective-permute-start(f32[16,768]{1,0:T(8,128)} %get-tuple-element.25), channel_id=1, source_target_pairs={{1,0},{2,1},{3,2},{4,3},{5,4},{6,5},{7,6},{8,7},{9,8},{10,9},{11,1... | collective-permute-start | bytes 147464 | tf_op jit(solution)/shard_map/ppermute | solution.py:691
  13.5 0.7 copy-start.10
  14.2 0.8 copy-start.1
  14.9 0.9 copy-start.5
  15.9 2.7 %copy-start.3 = (s32[32,128]{1,0:T(8,128)S(1)}, s32[32,128]{1,0:T(8,128)}, u32[]{:S(2)}) copy-start(s32[32,128]{1,0:T(8,128)} %get-tuple-element.26.pos) | copy-start | bytes 49156
  15.9 2.7 %copy-start.4 = (s32[32,128]{1,0:T(8,128)S(1)}, s32[32,128]{1,0:T(8,128)}, u32[]{:S(2)}) copy-start(s32[32,128]{1,0:T(8,128)} %get-tuple-element.30.starts_in.starts) | copy-start | bytes 49156
  15.9 2.7 %copy-start.8 = (f32[32,128]{1,0:T(8,128)S(1)}, f32[32,128]{1,0:T(8,128)}, u32[]{:S(2)}) copy-start(f32[32,128]{1,0:T(8,128)} %get-tuple-element.27.slots) | copy-start | bytes 49156
  121.6 27.0 %copy-start.2 = (s32[72,128]{1,0:T(8,128)S(1)}, s32[72,128]{1,0:T(8,128)}, u32[]{:S(2)}) copy-start(s32[72,128]{1,0:T(8,128)} %get-tuple-element.22.epos) | copy-start | bytes 110596
  153.5 13.8 %collective-permute-start.2 = (f32[16,768]{1,0:T(8,128)S(1)}, f32[16,768]{1,0:T(8,128)S(1)}, u32[]{:S(2)}, u32[]{:S(2)}) collective-permute-start(f32[16,768]{1,0:T(8,128)S(1)} %get-tuple-element.37), channel_id=1, source_target_pairs={{0,1},{1,2},{2,3},{3,4},{4,5},{5,6},{6,7},{7,8},{8,9},{9,10},{10,1... | collective-permute-start | bytes 147464 | tf_op jit(solution)/shard_map/ppermute | solution.py:769
  157.1 10.2 %collective-permute-start.3 = (f32[16,768]{1,0:T(8,128)S(1)}, f32[16,768]{1,0:T(8,128)S(1)}, u32[]{:S(2)}, u32[]{:S(2)}) collective-permute-start(f32[16,768]{1,0:T(8,128)S(1)} %get-tuple-element.38), channel_id=1, source_target_pairs={{1,0},{2,1},{3,2},{4,3},{5,4},{6,5},{7,6},{8,7},{9,8},{10,9},{11,1... | collective-permute-start | bytes 147464 | tf_op jit(solution)/shard_map/ppermute | solution.py:770

commit v6 on v5

--- a/solution.py
+++ b/solution.py
@@ -335,7 +335,7 @@
 
 
 def restrict_kernel(
-    ev_own, before, after, epos, pos, slots, w, diag, starts_in,
+    ev_own, before, after, epos, pos, slots, w, diag, starts_in, token,
     out, starts, sem, table, ev, xs, left, acc, compact,
 ):
     move = pltpu.make_async_copy(starts_in, starts, sem)
@@ -700,6 +700,9 @@
     )
     served = ((PEERS, ROWS, CAP), F32)
     compact = ((ROWS, U_LOC + 2 * LANE), F32)
+    peers = lax.axis_size("dev")
+    token = diag
+    token = lax.ppermute(token, axes, [(i, i ^ 1) for i in range(size) if i // peers % 2 == 0])
     (packed,) = call(
         restrict_kernel,
         "restrict",
@@ -715,7 +718,7 @@
             ((H_POS * PAIR + 96, WIDE), F32),
             ((SENT + 4, U_LOC + 2 * LANE), F32),
         ],
-        ev_own, before, after, epos, pos, slot_rows, w, diag, starts,
+        ev_own, before, after, epos, pos, slot_rows, w, diag, starts, token,
     )
     served_scratch = [(((H_NODE - TAIL_H) * PAIR, WIDE), BF), ((ROWS, TAIL_H * WIDE), F32)]
     wanted, rhs, floor, slots = call(

time: 169 us -> 151 us (0.89)
  blocking collectives: 114 us -> 90.4 us
  waiting for transfers between devices: 0.01 us -> 4.22 us
  starting transfers between devices: 21 us -> 22.9 us
    all_to_all x4, blocking collectives: 114 us -> 90.4 us  [exchange(): return lax.all_to_all(x, 'dev', split_axis=0, concat_axis=0, tiled=True)]
    ppermute x0 -> x1, waiting for transfers between devices: none -> 4.21 us  [per_device(): lax.ppermute(token, axes, [(i, i ^ 1) for i in range(size) if i // peers...]
    ppermute x0 -> x1, starting transfers between devices: none -> 1.92 us  [per_device(): lax.ppermute(token, axes, [(i, i ^ 1) for i in range(size) if i // peers...]
  transfers between devices with their start and end apart: 4 -> 5, of which waited for: 0 -> 1; matrix products, arithmetic and copies ran while one was open for 0% -> 0% of each run, Pallas kernels for 4% -> 4%
where the time goes in v6:
time: 151 us
  blocking collectives  90.4 us (60%)
  Pallas kernels  30.7 us (20%)
  starting transfers between devices  22.9 us (15%)
  waiting for transfers between devices  4.22 us (3%)
  local copies, waits for them, and re-layouts  2.32 us (2%)
    all_to_all x4, blocking collectives, exchange(): return lax.all_to_all(x, 'dev', split_axis=0, concat_axis=0, tiled=True)  90.4 us
    pallas_call x9, Pallas kernels, call(): pl.pallas_call(kernel, out_shape=[jax.ShapeDtypeStruct(s, t) for s, t in...  30.7 us
    ppermute x1, starting transfers between devices, per_device(): after = lax.ppermute(low, axes, down)  7.38 us
    ppermute x1, starting transfers between devices, per_device(): from_after = lax.ppermute(low, axes, down)  5.43 us
    ppermute x1, starting transfers between devices, per_device(): from_before = lax.ppermute(high, axes, up)  4.35 us
    ppermute x1, waiting for transfers between devices, per_device(): lax.ppermute(token, axes, [(i, i ^ 1) for i in range(size) if i // peers...  4.21 us
    ppermute x1, starting transfers between devices, per_device(): before = lax.ppermute(high, axes, up)  3.83 us
  transfers between devices with their start and end apart: 5, of which 1 were waited for; matrix products, arithmetic and copies ran while one was open for 0% of the time, Pallas kernels for 4%

profile of v6, /device:TPU:16, one launch (start us, length us, event | category | flops | bytes accessed | tf_op | source)
XLA Modules:
  0.0 150.8 jit_solution(3945800704990574507)
XLA Ops:
  0.0 0.0 copy-start
  0.0 0.0 copy-start.6
  0.0 0.0 copy-start.7
  0.0 2.3 %index_prep.1 = (s32[72,128]{1,0:T(8,128)}, s32[32,128]{1,0:T(8,128)}, f32[32,128]{1,0:T(8,128)}, s32[32,128]{1,0:T(8,128)}, f32[16,768]{1,0:T(8,128)}, /*index=5*/f32[16,768]{1,0:T(8,128)}) custom-call(f32[16,5376]{1,0:T(8,128)} %res.3, s32[64,144]{1,0:T(8,128)} %bitcast.5, s32[64,64]{1,0:T(8,128)} %lm_in.1, s32[16,128]{1,0:T(8,128)} %bitcast.6, ...), custom_call_target="tpu_custom_call" | custom-call | bytes 7200000 | tf_op jit(solution)/shard_map/index_prep/pallas_call | solution.py:625
  2.3 0.0 copy-start.9
  2.3 3.8 %collective-permute-start = (f32[16,768]{1,0:T(8,128)}, f32[16,768]{1,0:T(8,128)S(1)}, u32[]{:S(2)}, u32[]{:S(2)}) collective-permute-start(f32[16,768]{1,0:T(8,128)} %get-tuple-element.24), channel_id=1, source_target_pairs={{0,1},{1,2},{2,3},{3,4},{4,5},{5,6},{6,7},{7,8},{8,9},{9,10},{10,1... | collective-permute-start | bytes 147464 | tf_op jit(solution)/shard_map/ppermute | solution.py:690
  6.1 7.4 %collective-permute-start.1 = (f32[16,768]{1,0:T(8,128)}, f32[16,768]{1,0:T(8,128)S(1)}, u32[]{:S(2)}, u32[]{:S(2)}) collective-permute-start(f32[16,768]{1,0:T(8,128)} %get-tuple-element.25), channel_id=1, source_target_pairs={{1,0},{2,1},{3,2},{4,3},{5,4},{6,5},{7,6},{8,7},{9,8},{10,9},{11,1... | collective-permute-start | bytes 147464 | tf_op jit(solution)/shard_map/ppermute | solution.py:691
  13.5 0.0 copy-start.10
  13.5 0.0 copy-done
  13.5 0.0 copy-done.6
  13.5 0.0 copy-done.7
  13.6 0.0 copy-done.9
  13.6 0.6 copy-done.10
  14.2 0.0 copy-start.1
  14.2 0.8 copy-done.1
  14.9 0.0 copy-start.5
  14.9 0.9 copy-done.5
  15.9 0.0 copy-start.3
  15.9 0.0 copy-start.4
  15.9 0.0 copy-start.8
  15.9 2.7 %own_edges.1 = (f32[16,9216]{1,0:T(8,128)S(1)}, bf16[2,256,192]{2,1,0:T(8,128)(2,1)S(1)}, f32[8,4096]{1,0:T(8,128)S(1)}, f32[3,4096]{1,0:T(4,128)S(1)}) custom-call(f32[16,5376]{1,0:T(8,128)S(1)} %copy-done, s32[72,128]{1,0:T(8,128)S(1)} %copy-done.1, f32[144,192]{1,0:T(8,128)S(1)} %copy-done.5, f32[64,64]{1,0:T(8,128)S(1)} %copy-done.6, ...), custom_call_target="tpu_custom_call" | custom-call | bytes 14400000 | tf_op jit(solution)/shard_map/own_edges/pallas_call | solution.py:625
  18.5 1.9 %collective-permute-start.2 = (f32[3,4096]{1,0:T(4,128)S(1)}, f32[3,4096]{1,0:T(4,128)S(1)}, u32[]{:S(2)}, u32[]{:S(2)}) collective-permute-start(f32[3,4096]{1,0:T(4,128)S(1)} %get-tuple-element.29.diag), channel_id=1, source_target_pairs={{0,1},{1,0},{2,3},{3,2},{4,5},{5,4},{6,7},{7,6},{8,9},{9,8},{10,11... | collective-permute-start | bytes 147464 | tf_op jit(solution)/shard_map/ppermute | solution.py:705
  20.5 0.0 collective-permute-done.before
  20.5 0.0 collective-permute-done.1.after
  20.5 4.2 %collective-permute-done.2.token = f32[3,4096]{1,0:T(4,128)S(1)} collective-permute-done((f32[3,4096]{1,0:T(4,128)S(1)}, f32[3,4096]{1,0:T(4,128)S(1)}, u32[]{:S(2)}, u32[]{:S(2)}) %collective-permute-start.2) | collective-permute-done | bytes 49184 | tf_op jit(solution)/shard_map/ppermute | solution.py:705
  24.7 0.0 copy-done.3
  24.7 0.0 copy-done.4
  24.7 0.0 copy-done.8
  24.7 4.0 %restrict.1 = f32[32,52,128]{2,1,0:T(8,128)S(1)} custom-call(f32[16,9216]{1,0:T(8,128)S(1)} %get-tuple-element.23.ev_own, f32[16,768]{1,0:T(8,128)S(1)} %collective-permute-done.before, f32[16,768]{1,0:T(8,128)S(1)} %collective-permute-done.1.after, s32[72,128]{1,0:T(8,128)S(1)} %copy-done.1, s32[32,128]{1,0:T(8,128)S(1)} %copy-done.3, ...), custom_call_target="tpu_custom_call" | custom-call | bytes 21600000 | tf_op jit(solution)/shard_map/restrict/pallas_call | solution.py:625
  28.7 26.4 %all_to_all.20.arrived = f32[32,52,128]{2,1,0:T(8,128)S(1)} all-to-all(f32[32,52,128]{2,1,0:T(8,128)S(1)} %restrict.1), channel_id=1, replica_groups=mesh['grp'=8,'dev'=32] {'dev'}, dimensions={0} | all-to-all | bytes 1703936 | tf_op jit(solution)/shard_map/all_to_all | solution.py:638
  55.0 3.4 %first_iter.1 = (f32[32,48,128]{2,1,0:T(8,128)S(1)}, f32[7,48,256]{2,1,0:T(8,128)S(1)}, f32[7,3,256]{2,1,0:T(4,128)S(1)}, s32[32,128]{1,0:T(8,128)S(1)}) custom-call(f32[32,52,128]{2,1,0:T(8,128)S(1)} %all_to_all.20.arrived), custom_call_target="tpu_custom_call" | custom-call | bytes 18000000 | tf_op jit(solution)/shard_map/first_iter/pallas_call | solution.py:625
  58.5 22.4 %all_to_all.21.arrived = f32[32,48,128]{2,1,0:T(8,128)S(1)} all-to-all(f32[32,48,128]{2,1,0:T(8,128)S(1)} %get-tuple-element.31), channel_id=1, replica_groups=mesh['grp'=8,'dev'=32] {'dev'}, dimensions={0} | all-to-all | bytes 1572864 | tf_op jit(solution)/shard_map/all_to_all | solution.py:638
  80.8 5.5 %operator.1 = f32[32,48,128]{2,1,0:T(8,128)S(1)} custom-call(f32[32,48,128]{2,1,0:T(8,128)S(1)} %all_to_all.21.arrived, s32[32,128]{1,0:T(8,128)S(1)} %copy-done.3, f32[64,64]{1,0:T(8,128)S(1)} %copy-done.6, f32[64,64]{1,0:T(8,128)S(1)} %copy-done.7, f32[8,4096]{1,0:T(8,128)S(1)} %get-tuple-element.32.wide, s32[32,128]{1,0:T(8,128)S(1)} %copy-done.4), custom_call_target="tpu_custom_call" | custom-call | bytes 28800000 | tf_op jit(solution)/shard_map/operator/pallas_call | solution.py:625
  86.3 21.2 %all_to_all.22.arrived = f32[32,48,128]{2,1,0:T(8,128)S(1)} all-to-all(f32[32,48,128]{2,1,0:T(8,128)S(1)} %operator.1), channel_id=1, replica_groups=mesh['grp'=8,'dev'=32] {'dev'}, dimensions={0} | all-to-all | bytes 1572864 | tf_op jit(solution)/shard_map/all_to_all | solution.py:638
  107.5 3.2 %second_iter.1 = f32[32,48,128]{2,1,0:T(8,128)S(1)} custom-call(f32[32,48,128]{2,1,0:T(8,128)S(1)} %all_to_all.22.arrived, f32[7,48,256]{2,1,0:T(8,128)S(1)} %get-tuple-element.33.rhs, f32[7,3,256]{2,1,0:T(4,128)S(1)} %get-tuple-element.34.floor, s32[32,128]{1,0:T(8,128)S(1)} %get-tuple-element.35.slots), custom_call_target="tpu_custom_call" | custom-call | bytes 18000000 | tf_op jit(solution)/shard_map/second_iter/pallas_call | solution.py:625
  110.7 0.0 copy-start.2
  110.7 20.5 %all_to_all.23.arrived = f32[32,48,128]{2,1,0:T(8,128)S(1)} all-to-all(f32[32,48,128]{2,1,0:T(8,128)S(1)} %second_iter.1), channel_id=1, replica_groups=mesh['grp'=8,'dev'=32] {'dev'}, dimensions={0} | all-to-all | bytes 1572864 | tf_op jit(solution)/shard_map/all_to_all | solution.py:638
  131.2 0.0 copy-done.2
  131.2 5.0 %prolong_rim.1 = (bf16[32,9216]{1,0:T(8,128)(2,1)S(1)}, f32[16,768]{1,0:T(8,128)S(1)}, f32[16,768]{1,0:T(8,128)S(1)}) custom-call(f32[32,48,128]{2,1,0:T(8,128)S(1)} %all_to_all.23.arrived, s32[32,128]{1,0:T(8,128)S(1)} %copy-done.3, s32[72,128]{1,0:T(8,128)S(1)} %copy-done.2, bf16[2,256,192]{2,1,0:T(8,128)(2,1)S(1)} %get-tuple-element.28.w, ...), custom_call_target="tpu_custom_call" | custom-call | bytes 21600000 | tf_op jit(solution)/shard_map/prolong_rim/pallas_call | solution.py:625
  136.2 4.4 %collective-permute-start.3 = (f32[16,768]{1,0:T(8,128)S(1)}, f32[16,768]{1,0:T(8,128)S(1)}, u32[]{:S(2)}, u32[]{:S(2)}) collective-permute-start(f32[16,768]{1,0:T(8,128)S(1)} %get-tuple-element.37), channel_id=1, source_target_pairs={{0,1},{1,2},{2,3},{3,4},{4,5},{5,6},{6,7},{7,8},{8,9},{9,10},{10,1... | collective-permute-start | bytes 147464 | tf_op jit(solution)/shard_map/ppermute | solution.py:772
  140.6 5.4 %collective-permute-start.4 = (f32[16,768]{1,0:T(8,128)S(1)}, f32[16,768]{1,0:T(8,128)S(1)}, u32[]{:S(2)}, u32[]{:S(2)}) collective-permute-start(f32[16,768]{1,0:T(8,128)S(1)} %get-tuple-element.38), channel_id=1, source_target_pairs={{1,0},{2,1},{3,2},{4,3},{5,4},{6,5},{7,6},{8,7},{9,8},{10,9},{11,1... | collective-permute-start | bytes 147464 | tf_op jit(solution)/shard_map/ppermute | solution.py:773
  146.0 4.0 %prolong_own.1.own = f32[16,5376]{1,0:T(8,128)S(1)} custom-call(bf16[32,9216]{1,0:T(8,128)(2,1)S(1)} %get-tuple-element.36.terms, s32[72,128]{1,0:T(8,128)S(1)} %copy-done.2), custom_call_target="tpu_custom_call" | custom-call | bytes 18000000 | tf_op jit(solution)/shard_map/prolong_own/pallas_call | solution.py:625
  150.0 0.0 collective-permute-done.3.before
  150.0 0.0 collective-permute-done.4.after
  150.1 0.8 finish.1
Async XLA Ops:
  0.0 13.5 %copy-start = (f32[16,5376]{1,0:T(8,128)S(1)}, f32[16,5376]{1,0:T(8,128)}, u32[]{:S(2)}) copy-start(f32[16,5376]{1,0:T(8,128)} %res.3) | copy-start | bytes 1032196
  0.0 13.5 %copy-start.6 = (f32[64,64]{1,0:T(8,128)S(1)}, f32[64,64]{1,0:T(8,128)}, u32[]{:S(2)}) copy-start(f32[64,64]{1,0:T(8,128)} %stiff.3) | copy-start | bytes 49156
  0.0 13.5 %copy-start.7 = (f32[64,64]{1,0:T(8,128)S(1)}, f32[64,64]{1,0:T(8,128)}, u32[]{:S(2)}) copy-start(f32[64,64]{1,0:T(8,128)} %mass.3) | copy-start | bytes 49156
  2.3 11.3 %copy-start.9 = (f32[6,64]{1,0:T(8,128)S(1)}, f32[6,64]{1,0:T(8,128)}, u32[]{:S(2)}) copy-start(f32[6,64]{1,0:T(8,128)} %perm.1) | copy-start | bytes 4612
  2.3 18.2 %collective-permute-start = (f32[16,768]{1,0:T(8,128)}, f32[16,768]{1,0:T(8,128)S(1)}, u32[]{:S(2)}, u32[]{:S(2)}) collective-permute-start(f32[16,768]{1,0:T(8,128)} %get-tuple-element.24), channel_id=1, source_target_pairs={{0,1},{1,2},{2,3},{3,4},{4,5},{5,6},{6,7},{7,8},{8,9},{9,10},{10,1... | collective-permute-start | bytes 147464 | tf_op jit(solution)/shard_map/ppermute | solution.py:690
  6.1 14.3 %collective-permute-start.1 = (f32[16,768]{1,0:T(8,128)}, f32[16,768]{1,0:T(8,128)S(1)}, u32[]{:S(2)}, u32[]{:S(2)}) collective-permute-start(f32[16,768]{1,0:T(8,128)} %get-tuple-element.25), channel_id=1, source_target_pairs={{1,0},{2,1},{3,2},{4,3},{5,4},{6,5},{7,6},{8,7},{9,8},{10,9},{11,1... | collective-permute-start | bytes 147464 | tf_op jit(solution)/shard_map/ppermute | solution.py:691
  13.5 0.7 copy-start.10
  14.2 0.8 copy-start.1
  14.9 0.9 copy-start.5
  15.9 8.8 %copy-start.3 = (s32[32,128]{1,0:T(8,128)S(1)}, s32[32,128]{1,0:T(8,128)}, u32[]{:S(2)}) copy-start(s32[32,128]{1,0:T(8,128)} %get-tuple-element.26.pos) | copy-start | bytes 49156
  15.9 8.8 %copy-start.4 = (s32[32,128]{1,0:T(8,128)S(1)}, s32[32,128]{1,0:T(8,128)}, u32[]{:S(2)}) copy-start(s32[32,128]{1,0:T(8,128)} %get-tuple-element.30.starts_in.starts) | copy-start | bytes 49156
  15.9 8.8 %copy-start.8 = (f32[32,128]{1,0:T(8,128)S(1)}, f32[32,128]{1,0:T(8,128)}, u32[]{:S(2)}) copy-start(f32[32,128]{1,0:T(8,128)} %get-tuple-element.27.slots) | copy-start | bytes 49156
  18.5 6.2 %collective-permute-start.2 = (f32[3,4096]{1,0:T(4,128)S(1)}, f32[3,4096]{1,0:T(4,128)S(1)}, u32[]{:S(2)}, u32[]{:S(2)}) collective-permute-start(f32[3,4096]{1,0:T(4,128)S(1)} %get-tuple-element.29.diag), channel_id=1, source_target_pairs={{0,1},{1,0},{2,3},{3,2},{4,5},{5,4},{6,7},{7,6},{8,9},{9,8},{10,11... | collective-permute-start | bytes 147464 | tf_op jit(solution)/shard_map/ppermute | solution.py:705
  110.7 20.5 %copy-start.2 = (s32[72,128]{1,0:T(8,128)S(1)}, s32[72,128]{1,0:T(8,128)}, u32[]{:S(2)}) copy-start(s32[72,128]{1,0:T(8,128)} %get-tuple-element.22.epos) | copy-start | bytes 110596
  136.2 13.8 %collective-permute-start.3 = (f32[16,768]{1,0:T(8,128)S(1)}, f32[16,768]{1,0:T(8,128)S(1)}, u32[]{:S(2)}, u32[]{:S(2)}) collective-permute-start(f32[16,768]{1,0:T(8,128)S(1)} %get-tuple-element.37), channel_id=1, source_target_pairs={{0,1},{1,2},{2,3},{3,4},{4,5},{5,6},{6,7},{7,8},{8,9},{9,10},{10,1... | collective-permute-start | bytes 147464 | tf_op jit(solution)/shard_map/ppermute | solution.py:772
  140.6 9.5 %collective-permute-start.4 = (f32[16,768]{1,0:T(8,128)S(1)}, f32[16,768]{1,0:T(8,128)S(1)}, u32[]{:S(2)}, u32[]{:S(2)}) collective-permute-start(f32[16,768]{1,0:T(8,128)S(1)} %get-tuple-element.38), channel_id=1, source_target_pairs={{1,0},{2,1},{3,2},{4,3},{5,4},{6,5},{7,6},{8,7},{9,8},{10,9},{11,1... | collective-permute-start | bytes 147464 | tf_op jit(solution)/shard_map/ppermute | solution.py:773

commit v7 on v5

--- a/solution.py
+++ b/solution.py
@@ -245,19 +245,8 @@
     pos_out[...] = pos
 
 
-def own_edges_kernel(res, epos, pi, stiff, mass, perm, curl, ev_out, w, wide, diag, coef, table):
-    fill_pi(w, pi)
-    fill_coefs(coef, wide, perm, curl)
-    eye = iota((NN, NN), 0) == iota((NN, NN), 1)
-
-    def diagonal(ref):
-        d = jnp.sum(jnp.where(eye, ref[...], 0.0), axis=0, keepdims=True)
-        return jnp.concatenate([d, d], axis=1)
-
-    sd, md = diagonal(stiff), diagonal(mass)
-    for t in range(N_TILES):
-        at = cols_of(t, LANE)
-        diag[:, at] = wide[6:7, at] * sd + md * wide[0:3, at]
+def own_edges_kernel(res, epos, ev_out, token, table):
+    token[...] = jnp.zeros(token.shape, F32)
     count = H_OWN - OWN_TAIL // 2
     fill_table(table, lambda h: res[:, cols_of(h, WIDE)], RHS, count)
     for step in range(E_TILES * LANE // GATHER_STEP):
@@ -335,8 +324,8 @@
 
 
 def restrict_kernel(
-    ev_own, before, after, epos, pos, slots, w, diag, starts_in,
-    out, starts, sem, table, ev, xs, left, acc, compact,
+    ev_own, before, after, epos, pos, slots, pi, stiff, mass, perm, curl, starts_in, token,
+    out, starts, sem, table, ev, w, coef, wide, xs, diag, left, acc, compact,
 ):
     move = pltpu.make_async_copy(starts_in, starts, sem)
     move.start()
@@ -356,6 +345,7 @@
         ev[:, at] = jnp.where(spread(idx, RHS) >= 0, found, ev_own[:, at])
 
     over(E_TILES // GATHER_ROWS, step_body, LOOP['rim'])
+    fill_pi(w, pi)
     group = iota((RHS, LANE), 1) >> 4
     for step in range(EL // PI_STEP):
         blocks = []
@@ -382,6 +372,18 @@
                     axis=0,
                 )
             )
+    fill_coefs(coef, wide, perm, curl)
+    eye = iota((NN, NN), 0) == iota((NN, NN), 1)
+
+    def diagonal(ref):
+        d = jnp.sum(jnp.where(eye, ref[...], 0.0), axis=0, keepdims=True)
+        return jnp.concatenate([d, d], axis=1)
+
+    sd, md = diagonal(stiff), diagonal(mass)
+    for t in range(N_TILES):
+        at = slice(t * LANE, (t + 1) * LANE)
+        diag[:, at] = wide[6:7, at] * sd + md * wide[0:3, at]
+
     def step_body(step):
         at = cols_of(step, NODE_STEP)
         idx = pos[rows_of(step, NODE_ROWS), :]
@@ -499,8 +501,11 @@
     )
 
 
-def apply_kernel(arrived, pos, stiff, mass, wide, starts, out, table, op, xs, left, acc, compact):
+def apply_kernel(
+    arrived, pos, stiff, mass, perm, curl, starts, out, table, op, coef, wide, xs, left, acc, compact
+):
     touched_table(table, compact, arrived, starts)
+    fill_coefs(coef, wide, perm, curl)
     op[...] = jnp.zeros((3, LANE, 2 * LANE), BF)
     for m, ref in enumerate((stiff, mass)):
         part = split(ref[...].T)
@@ -553,8 +558,9 @@
     expand(out, compact, starts, ROWS)
 
 
-def edge_terms(arrived, pos, w, starts, terms, table, values, compact):
+def edge_terms(arrived, pos, pi, starts, terms, table, w, values, compact):
     touched_table(table, compact, arrived, starts)
+    fill_pi(w, pi)
 
     def step_body(step):
         values[:, cols_of(step, GATHER_STEP)] = touched_tile(table, compact, pos, step)
@@ -591,9 +597,9 @@
 
 
 def prolong_rim_kernel(
-    arrived, pos, epos, w, starts, terms, low_out, high_out, table, values, compact, left, acc
+    arrived, pos, epos, pi, starts, terms, low_out, high_out, table, w, values, compact, left, acc
 ):
-    edge_terms(arrived, pos, w, starts, terms, table, values, compact)
+    edge_terms(arrived, pos, pi, starts, terms, table, w, values, compact)
     edge_scatter(terms, epos, left, acc, H_OWN, 2 * H_RIM)
     for h in range(H_RIM):
         at = slice(h * WIDE, (h + 1) * WIDE)
@@ -690,16 +696,15 @@
     before = lax.ppermute(high, axes, up)
     after = lax.ppermute(low, axes, down)
     edge_rows = ((RHS, E_TILES * LANE), F32)
-    ev_own, w, wide, diag = call(
-        own_edges_kernel,
-        "own_edges",
-        4,
-        [edge_rows, ((2, WIDE, 3 * NN), BF), ((8, ELN), F32), ((3, ELN), F32)],
-        [((8, LANE), F32), (((H_OWN - OWN_TAIL // 2) * 2 * RHS, WIDE), BF)],
-        residual_edges, epos, pi_block, stiff_block, mass_block, permittivity, curl,
-    )
+    ev_own, token = call(
+        own_edges_kernel, "own_edges", 4, [edge_rows, ((8, 1024), F32)], [(((H_OWN - OWN_TAIL // 2) * 2 * RHS, WIDE), BF)], residual_edges, epos
+    )
+    pi_scratch = ((2, WIDE, 3 * NN), BF)
+    coefs = [((8, LANE), F32), ((8, ELN), F32)]
     served = ((PEERS, ROWS, CAP), F32)
     compact = ((ROWS, U_LOC + 2 * LANE), F32)
+    peers = lax.axis_size("dev")
+    token = lax.ppermute(token, axes, [(i, i ^ 2) for i in range(size) if i // peers % 2 == 0])
     (packed,) = call(
         restrict_kernel,
         "restrict",
@@ -710,12 +715,15 @@
             pltpu.SemaphoreType.DMA,
             (((2 * H_RIM - TAIL_H) * 2 * RHS, WIDE), BF),
             edge_rows,
+            pi_scratch,
+            *coefs,
             ((PAIR, ELN), BF),
+            ((3, ELN), F32),
             ((BUFFERS, H_POS * PAIR + 96, NODE_STEP), BF),
             ((H_POS * PAIR + 96, WIDE), F32),
             ((SENT + 4, U_LOC + 2 * LANE), F32),
         ],
-        ev_own, before, after, epos, pos, slot_rows, w, diag, starts,
+        ev_own, before, after, epos, pos, slot_rows, pi_block, stiff_block, mass_block, permittivity, curl, starts, token,
     )
     served_scratch = [(((H_NODE - TAIL_H) * PAIR, WIDE), BF), ((ROWS, TAIL_H * WIDE), F32)]
     wanted, rhs, floor, slots = call(
@@ -735,12 +743,13 @@
         [
             position_table,
             ((3, LANE, 2 * LANE), BF),
+            *coefs,
             ((PAIR, ELN), BF),
             ((BUFFERS, H_POS * PAIR, NODE_STEP), BF),
             ((H_POS * PAIR, WIDE), F32),
             compact,
         ],
-        exchange(wanted), pos, stiff_block, mass_block, wide, starts,
+        exchange(wanted), pos, stiff_block, mass_block, permittivity, curl, starts,
         scalars=1,
     )
     (wanted,) = call(
@@ -758,12 +767,13 @@
         [((2 * RHS, E_TILES * LANE), BF), rim, rim],
         [
             position_table,
+            pi_scratch,
             ((ROWS, ELN), F32),
             compact,
             ((BUFFERS, 2 * H_RIM * 2 * RHS, EDGE_STEP), BF),
             ((2 * H_RIM * 2 * RHS, WIDE), F32),
         ],
-        exchange(wanted), pos, epos, w, starts,
+        exchange(wanted), pos, epos, pi_block, starts,
         scalars=1,
     )
     from_before = lax.ppermute(high, axes, up)

time: 169 us -> 150 us (0.89)
  blocking collectives: 114 us -> 89.1 us
  waiting for transfers between devices: 0.01 us -> 4.79 us
  starting transfers between devices: 21 us -> 22.9 us
    all_to_all x4, blocking collectives: 114 us -> 89.1 us  [exchange(): return lax.all_to_all(x, 'dev', split_axis=0, concat_axis=0, tiled=True)]
    ppermute x0 -> x1, waiting for transfers between devices: none -> 4.78 us  [per_device(): lax.ppermute(token, axes, [(i, i ^ 2) for i in range(size) if i // peers...]
    ppermute x0 -> x1, starting transfers between devices: none -> 1.92 us  [per_device(): lax.ppermute(token, axes, [(i, i ^ 2) for i in range(size) if i // peers...]
  transfers between devices with their start and end apart: 4 -> 5, of which waited for: 0 -> 1; matrix products, arithmetic and copies ran while one was open for 0% -> 0% of each run, Pallas kernels for 4% -> 4%
where the time goes in v7:
time: 150 us; the launch traced here: 149 us
  blocking collectives  89.1 us (59%)
  Pallas kernels  30.7 us (20%)
  starting transfers between devices  22.9 us (15%)
  waiting for transfers between devices  4.79 us (3%)
    all_to_all x4, blocking collectives, exchange(): return lax.all_to_all(x, 'dev', split_axis=0, concat_axis=0, tiled=True)  89.1 us
    pallas_call x9, Pallas kernels, call(): pl.pallas_call(kernel, out_shape=[jax.ShapeDtypeStruct(s, t) for s, t in...  30.7 us
    ppermute x1, starting transfers between devices, per_device(): after = lax.ppermute(low, axes, down)  7.38 us
    ppermute x1, starting transfers between devices, per_device(): from_after = lax.ppermute(low, axes, down)  5.78 us
    ppermute x1, waiting for transfers between devices, per_device(): lax.ppermute(token, axes, [(i, i ^ 2) for i in range(size) if i // peers...  4.78 us
    ppermute x1, starting transfers between devices, per_device(): from_before = lax.ppermute(high, axes, up)  4 us
    ppermute x1, starting transfers between devices, per_device(): before = lax.ppermute(high, axes, up)  3.83 us
  transfers between devices with their start and end apart: 5, of which 1 were waited for; matrix products, arithmetic and copies ran while one was open for 0% of the time, Pallas kernels for 4%

profile of v7, /device:TPU:16, one launch (start us, length us, event | category | flops | bytes accessed | tf_op | source)
XLA Modules:
  0.0 149.1 jit_solution(350526324411279644)
XLA Ops:
  0.0 0.0 copy-start
  0.0 2.3 %index_prep.1 = (s32[72,128]{1,0:T(8,128)}, s32[32,128]{1,0:T(8,128)}, f32[32,128]{1,0:T(8,128)}, s32[32,128]{1,0:T(8,128)}, f32[16,768]{1,0:T(8,128)}, /*index=5*/f32[16,768]{1,0:T(8,128)}) custom-call(f32[16,5376]{1,0:T(8,128)} %res.3, s32[64,144]{1,0:T(8,128)} %bitcast.6, s32[64,64]{1,0:T(8,128)} %lm_in.1, s32[16,128]{1,0:T(8,128)} %bitcast.7, ...), custom_call_target="tpu_custom_call" | custom-call | bytes 7200000 | tf_op jit(solution)/shard_map/index_prep/pallas_call | solution.py:631
  2.3 3.8 %collective-permute-start = (f32[16,768]{1,0:T(8,128)}, f32[16,768]{1,0:T(8,128)S(1)}, u32[]{:S(2)}, u32[]{:S(2)}) collective-permute-start(f32[16,768]{1,0:T(8,128)} %get-tuple-element.22), channel_id=1, source_target_pairs={{0,1},{1,2},{2,3},{3,4},{4,5},{5,6},{6,7},{7,8},{8,9},{9,10},{10,1... | collective-permute-start | bytes 147464 | tf_op jit(solution)/shard_map/ppermute | solution.py:696
  6.1 7.4 %collective-permute-start.1 = (f32[16,768]{1,0:T(8,128)}, f32[16,768]{1,0:T(8,128)S(1)}, u32[]{:S(2)}, u32[]{:S(2)}) collective-permute-start(f32[16,768]{1,0:T(8,128)} %get-tuple-element.23), channel_id=1, source_target_pairs={{1,0},{2,1},{3,2},{4,3},{5,4},{6,5},{7,6},{8,7},{9,8},{10,9},{11,1... | collective-permute-start | bytes 147464 | tf_op jit(solution)/shard_map/ppermute | solution.py:697
  13.5 0.0 copy-done
  13.5 0.0 copy-start.2
  13.5 0.8 copy-done.2
  14.3 0.0 copy-start.1
  14.3 0.0 copy-start.4
  14.3 0.0 copy-start.5
  14.3 0.0 copy-start.6
  14.3 0.0 copy-start.7
  14.3 0.0 copy-start.8
  14.3 2.7 %own_edges.1 = (f32[16,9216]{1,0:T(8,128)S(1)}, f32[8,1024]{1,0:T(8,128)S(1)}) custom-call(f32[16,5376]{1,0:T(8,128)S(1)} %copy-done, s32[72,128]{1,0:T(8,128)S(1)} %copy-done.2), custom_call_target="tpu_custom_call" | custom-call | bytes 14400000 | tf_op jit(solution)/shard_map/own_edges/pallas_call | solution.py:631
  17.0 1.9 %collective-permute-start.2 = (f32[8,1024]{1,0:T(8,128)S(1)}, f32[8,1024]{1,0:T(8,128)S(1)}, u32[]{:S(2)}, u32[]{:S(2)}) collective-permute-start(f32[8,1024]{1,0:T(8,128)S(1)} %get-tuple-element.27), channel_id=1, source_target_pairs={{0,2},{1,3},{2,0},{3,1},{4,6},{5,7},{6,4},{7,5},{8,10},{9,11},{10,... | collective-permute-start | bytes 98312 | tf_op jit(solution)/shard_map/ppermute | solution.py:707
  18.9 4.8 %collective-permute-done.2.token = f32[8,1024]{1,0:T(8,128)S(1)} collective-permute-done((f32[8,1024]{1,0:T(8,128)S(1)}, f32[8,1024]{1,0:T(8,128)S(1)}, u32[]{:S(2)}, u32[]{:S(2)}) %collective-permute-start.2) | collective-permute-done | bytes 32800 | tf_op jit(solution)/shard_map/ppermute | solution.py:707
  23.7 0.0 collective-permute-done.before
  23.7 0.0 collective-permute-done.1.after
  23.7 0.0 copy-start.9
  23.7 0.0 copy-start.10
  23.7 0.0 copy-done.1
  23.7 0.0 copy-done.4
  23.7 0.0 copy-done.5
  23.7 0.0 copy-done.6
  23.7 0.0 copy-done.7
  23.7 0.0 copy-done.8
  23.8 0.6 copy-done.9
  24.4 0.0 copy-done.10
  24.4 3.9 %restrict.1 = f32[32,52,128]{2,1,0:T(8,128)S(1)} custom-call(f32[16,9216]{1,0:T(8,128)S(1)} %get-tuple-element.21.ev_own, f32[16,768]{1,0:T(8,128)S(1)} %collective-permute-done.before, f32[16,768]{1,0:T(8,128)S(1)} %collective-permute-done.1.after, s32[72,128]{1,0:T(8,128)S(1)} %copy-done.2, s32[32,128]{1,0:T(8,128)S(1)} %copy-done.4, ...), custom_call_target="tpu_custom_call" | custom-call | bytes 21600000 | tf_op jit(solution)/shard_map/restrict/pallas_call | solution.py:631
  28.3 26.1 %all_to_all.20.arrived = f32[32,52,128]{2,1,0:T(8,128)S(1)} all-to-all(f32[32,52,128]{2,1,0:T(8,128)S(1)} %restrict.1), channel_id=1, replica_groups=mesh['grp'=8,'dev'=32] {'dev'}, dimensions={0} | all-to-all | bytes 1703936 | tf_op jit(solution)/shard_map/all_to_all | solution.py:644
  54.4 3.4 %first_iter.1 = (f32[32,48,128]{2,1,0:T(8,128)S(1)}, f32[7,48,256]{2,1,0:T(8,128)S(1)}, f32[7,3,256]{2,1,0:T(4,128)S(1)}, s32[32,128]{1,0:T(8,128)S(1)}) custom-call(f32[32,52,128]{2,1,0:T(8,128)S(1)} %all_to_all.20.arrived), custom_call_target="tpu_custom_call" | custom-call | bytes 18000000 | tf_op jit(solution)/shard_map/first_iter/pallas_call | solution.py:631
  57.8 22.0 %all_to_all.21.arrived = f32[32,48,128]{2,1,0:T(8,128)S(1)} all-to-all(f32[32,48,128]{2,1,0:T(8,128)S(1)} %get-tuple-element.28), channel_id=1, replica_groups=mesh['grp'=8,'dev'=32] {'dev'}, dimensions={0} | all-to-all | bytes 1572864 | tf_op jit(solution)/shard_map/all_to_all | solution.py:644
  79.8 5.4 %operator.1 = f32[32,48,128]{2,1,0:T(8,128)S(1)} custom-call(f32[32,48,128]{2,1,0:T(8,128)S(1)} %all_to_all.21.arrived, s32[32,128]{1,0:T(8,128)S(1)} %copy-done.4, f32[64,64]{1,0:T(8,128)S(1)} %copy-done.6, f32[64,64]{1,0:T(8,128)S(1)} %copy-done.7, f32[6,64]{1,0:T(8,128)S(1)} %copy-done.9, f32[1,64]{1,0:T(1,128)S(1)} %bitcast.5, s32[32,128]{1,0:T(8,128)S(1)} %copy-done.5), custom_call_target="tpu_custom_call" | custom-call | bytes 28800000 | tf_op jit(solution)/shard_map/operator/pallas_call | solution.py:631
  85.3 19.9 %all_to_all.22.arrived = f32[32,48,128]{2,1,0:T(8,128)S(1)} all-to-all(f32[32,48,128]{2,1,0:T(8,128)S(1)} %operator.1), channel_id=1, replica_groups=mesh['grp'=8,'dev'=32] {'dev'}, dimensions={0} | all-to-all | bytes 1572864 | tf_op jit(solution)/shard_map/all_to_all | solution.py:644
  105.2 3.2 %second_iter.1 = f32[32,48,128]{2,1,0:T(8,128)S(1)} custom-call(f32[32,48,128]{2,1,0:T(8,128)S(1)} %all_to_all.22.arrived, f32[7,48,256]{2,1,0:T(8,128)S(1)} %get-tuple-element.29.rhs, f32[7,3,256]{2,1,0:T(4,128)S(1)} %get-tuple-element.30.floor, s32[32,128]{1,0:T(8,128)S(1)} %get-tuple-element.31.slots), custom_call_target="tpu_custom_call" | custom-call | bytes 18000000 | tf_op jit(solution)/shard_map/second_iter/pallas_call | solution.py:631
  108.4 0.0 copy-start.3
  108.4 21.1 %all_to_all.23.arrived = f32[32,48,128]{2,1,0:T(8,128)S(1)} all-to-all(f32[32,48,128]{2,1,0:T(8,128)S(1)} %second_iter.1), channel_id=1, replica_groups=mesh['grp'=8,'dev'=32] {'dev'}, dimensions={0} | all-to-all | bytes 1572864 | tf_op jit(solution)/shard_map/all_to_all | solution.py:644
  129.5 0.0 copy-done.3
  129.5 5.0 %prolong_rim.1 = (bf16[32,9216]{1,0:T(8,128)(2,1)S(1)}, f32[16,768]{1,0:T(8,128)S(1)}, f32[16,768]{1,0:T(8,128)S(1)}) custom-call(f32[32,48,128]{2,1,0:T(8,128)S(1)} %all_to_all.23.arrived, s32[32,128]{1,0:T(8,128)S(1)} %copy-done.4, s32[72,128]{1,0:T(8,128)S(1)} %copy-done.3, f32[144,192]{1,0:T(8,128)S(1)} %copy-done.1, s32[32,128]{1,0:T(8,128)S(1)} %copy-done.5), custom_call_target="tpu_custom_call" | custom-call | bytes 21600000 | tf_op jit(solution)/shard_map/prolong_rim/pallas_call | solution.py:631
  134.5 4.0 %collective-permute-start.3 = (f32[16,768]{1,0:T(8,128)S(1)}, f32[16,768]{1,0:T(8,128)S(1)}, u32[]{:S(2)}, u32[]{:S(2)}) collective-permute-start(f32[16,768]{1,0:T(8,128)S(1)} %get-tuple-element.33), channel_id=1, source_target_pairs={{0,1},{1,2},{2,3},{3,4},{4,5},{5,6},{6,7},{7,8},{8,9},{9,10},{10,1... | collective-permute-start | bytes 147464 | tf_op jit(solution)/shard_map/ppermute | solution.py:779
  138.5 5.8 %collective-permute-start.4 = (f32[16,768]{1,0:T(8,128)S(1)}, f32[16,768]{1,0:T(8,128)S(1)}, u32[]{:S(2)}, u32[]{:S(2)}) collective-permute-start(f32[16,768]{1,0:T(8,128)S(1)} %get-tuple-element.34), channel_id=1, source_target_pairs={{1,0},{2,1},{3,2},{4,3},{5,4},{6,5},{7,6},{8,7},{9,8},{10,9},{11,1... | collective-permute-start | bytes 147464 | tf_op jit(solution)/shard_map/ppermute | solution.py:780
  144.3 4.0 %prolong_own.1.own = f32[16,5376]{1,0:T(8,128)S(1)} custom-call(bf16[32,9216]{1,0:T(8,128)(2,1)S(1)} %get-tuple-element.32.terms, s32[72,128]{1,0:T(8,128)S(1)} %copy-done.3), custom_call_target="tpu_custom_call" | custom-call | bytes 18000000 | tf_op jit(solution)/shard_map/prolong_own/pallas_call | solution.py:631
  148.3 0.0 collective-permute-done.3.before
  148.3 0.0 collective-permute-done.4.after
  148.3 0.8 finish.1
Async XLA Ops:
  0.0 13.5 %copy-start = (f32[16,5376]{1,0:T(8,128)S(1)}, f32[16,5376]{1,0:T(8,128)}, u32[]{:S(2)}) copy-start(f32[16,5376]{1,0:T(8,128)} %res.3) | copy-start | bytes 1032196
  2.3 21.4 %collective-permute-start = (f32[16,768]{1,0:T(8,128)}, f32[16,768]{1,0:T(8,128)S(1)}, u32[]{:S(2)}, u32[]{:S(2)}) collective-permute-start(f32[16,768]{1,0:T(8,128)} %get-tuple-element.22), channel_id=1, source_target_pairs={{0,1},{1,2},{2,3},{3,4},{4,5},{5,6},{6,7},{7,8},{8,9},{9,10},{10,1... | collective-permute-start | bytes 147464 | tf_op jit(solution)/shard_map/ppermute | solution.py:696
  6.1 17.6 %collective-permute-start.1 = (f32[16,768]{1,0:T(8,128)}, f32[16,768]{1,0:T(8,128)S(1)}, u32[]{:S(2)}, u32[]{:S(2)}) collective-permute-start(f32[16,768]{1,0:T(8,128)} %get-tuple-element.23), channel_id=1, source_target_pairs={{1,0},{2,1},{3,2},{4,3},{5,4},{6,5},{7,6},{8,7},{9,8},{10,9},{11,1... | collective-permute-start | bytes 147464 | tf_op jit(solution)/shard_map/ppermute | solution.py:697
  13.5 0.8 copy-start.2
  14.3 9.4 %copy-start.1 = (f32[144,192]{1,0:T(8,128)S(1)}, f32[144,192]{1,0:T(8,128)}, u32[]{:S(2)}) copy-start(f32[144,192]{1,0:T(8,128)} %pi.3) | copy-start | bytes 331780
  14.3 9.4 %copy-start.4 = (s32[32,128]{1,0:T(8,128)S(1)}, s32[32,128]{1,0:T(8,128)}, u32[]{:S(2)}) copy-start(s32[32,128]{1,0:T(8,128)} %get-tuple-element.24.pos) | copy-start | bytes 49156
  14.3 9.4 %copy-start.5 = (s32[32,128]{1,0:T(8,128)S(1)}, s32[32,128]{1,0:T(8,128)}, u32[]{:S(2)}) copy-start(s32[32,128]{1,0:T(8,128)} %get-tuple-element.26.starts_in.starts) | copy-start | bytes 49156
  14.3 9.4 %copy-start.6 = (f32[64,64]{1,0:T(8,128)S(1)}, f32[64,64]{1,0:T(8,128)}, u32[]{:S(2)}) copy-start(f32[64,64]{1,0:T(8,128)} %stiff.3) | copy-start | bytes 49156
  14.3 9.5 %copy-start.7 = (f32[64,64]{1,0:T(8,128)S(1)}, f32[64,64]{1,0:T(8,128)}, u32[]{:S(2)}) copy-start(f32[64,64]{1,0:T(8,128)} %mass.3) | copy-start | bytes 49156
  14.3 9.5 %copy-start.8 = (f32[32,128]{1,0:T(8,128)S(1)}, f32[32,128]{1,0:T(8,128)}, u32[]{:S(2)}) copy-start(f32[32,128]{1,0:T(8,128)} %get-tuple-element.25.slots) | copy-start | bytes 49156
  17.0 6.7 %collective-permute-start.2 = (f32[8,1024]{1,0:T(8,128)S(1)}, f32[8,1024]{1,0:T(8,128)S(1)}, u32[]{:S(2)}, u32[]{:S(2)}) collective-permute-start(f32[8,1024]{1,0:T(8,128)S(1)} %get-tuple-element.27), channel_id=1, source_target_pairs={{0,2},{1,3},{2,0},{3,1},{4,6},{5,7},{6,4},{7,5},{8,10},{9,11},{10,... | collective-permute-start | bytes 98312 | tf_op jit(solution)/shard_map/ppermute | solution.py:707
  23.7 0.7 copy-start.9
  23.7 0.7 copy-start.10
  108.4 21.1 %copy-start.3 = (s32[72,128]{1,0:T(8,128)S(1)}, s32[72,128]{1,0:T(8,128)}, u32[]{:S(2)}) copy-start(s32[72,128]{1,0:T(8,128)} %get-tuple-element.20.epos) | copy-start | bytes 110596
  134.5 13.8 %collective-permute-start.3 = (f32[16,768]{1,0:T(8,128)S(1)}, f32[16,768]{1,0:T(8,128)S(1)}, u32[]{:S(2)}, u32[]{:S(2)}) collective-permute-start(f32[16,768]{1,0:T(8,128)S(1)} %get-tuple-element.33), channel_id=1, source_target_pairs={{0,1},{1,2},{2,3},{3,4},{4,5},{5,6},{6,7},{7,8},{8,9},{9,10},{10,1... | collective-permute-start | bytes 147464 | tf_op jit(solution)/shard_map/ppermute | solution.py:779
  138.5 9.8 %collective-permute-start.4 = (f32[16,768]{1,0:T(8,128)S(1)}, f32[16,768]{1,0:T(8,128)S(1)}, u32[]{:S(2)}, u32[]{:S(2)}) collective-permute-start(f32[16,768]{1,0:T(8,128)S(1)} %get-tuple-element.34), channel_id=1, source_target_pairs={{1,0},{2,1},{3,2},{4,3},{5,4},{6,5},{7,6},{8,7},{9,8},{10,9},{11,1... | collective-permute-start | bytes 147464 | tf_op jit(solution)/shard_map/ppermute | solution.py:780
